TPU v7x, 256 devices: a whole 4x4x8 slice. The times are simulated.
256 devices in a mesh: gx: 32 (over x, y, core), gy: 8 (over z).
Axes of the slice: x: 4, y: 4, z: 8, core: 2. Of those that a mesh axis runs over, the one named last changes fastest.
Arguments:
- stencil: float32 [14, 3, 3, 64, 64, 128], P(None, None, None, 'gx', 'gy'), as said below
- candidates: float32 [8, 3, 64, 64, 128], P(None, None, 'gx', 'gy'), may hold values from -6 to 6
- segment_id: int32 [32, 32, 128], P('gx', 'gy'), may hold values from 0 to 62, as said below
Outputs:
- prolongator: float32 [8, 3, 64, 64, 128], P(None, None, 'gx', 'gy')
- coarse: float32 [8, 8, 32, 32, 63], P(None, None, 'gx', 'gy')
Inputs may be any that keep to these rules, and one draw needn't show every extreme that they name: `segment_id`: in every footprint column the numbers along the third dimension start at 0 and rise by one at each new aggregate; each aggregate is a run of 2 or 4 nodes beginning at an even position, the first one of 4. `stencil`: each diagonal block is symmetric with diagonal entries at least 6 and off-diagonal entries at most 1 in magnitude.
All inputs are finite; a program needn't handle non-finite values.
Results may differ from a plain program's by a relative error of at most 0.0003.
Values sent between devices are 32-bit elements; how exact they have to be, the bound alone decides.
No kernel may reach another device: no remote copies, remote signals or barrier semaphores. Data moves between devices by JAX's collectives and lax.ppermute only.
A program may use at most 128 MiB of HBM per device.

v0:
```python
import functools

import jax
import jax.numpy as jnp
import numpy as np
from jax import lax
from jax.experimental import pallas as pl
from jax.experimental.pallas import tpu as pltpu
from jax.sharding import PartitionSpec as P

ITERS = 4
NSEG = 63
K = 8
DAMPING = 0.8
F32 = jnp.float32
neighbour_steps = [
    (sx, sy, sz)
    for sx in (-1, 0, 1)
    for sy in (-1, 0, 1)
    for sz in (-1, 0, 1)
    if (sx, sy, sz) > (0, 0, 0)
]
ROLLED = [j for j, o in enumerate(neighbour_steps) if o[2] != 0]
SYM = [(0, 0), (0, 1), (0, 2), (1, 1), (1, 2), (2, 2)]
SYM_OF = {(e, d): SYM.index((min(e, d), max(e, d))) for e in range(3) for d in range(3)}
ROWS = 24
VMEM = pl.BlockSpec(memory_space=pltpu.VMEM)
ANY = pl.BlockSpec(memory_space=pl.ANY)
LIMIT = 12 * 2**20

N_V4 = 48
N_S4 = 2 * (6 + 117)
V4, S4 = 0, 4 * N_V4
V1 = 4 * (N_V4 + N_S4)
S1 = V1 + 48
ONE_DN = [j for j, o in enumerate(neighbour_steps) if o[1] == -1]
ONE_UP = [j for j, o in enumerate(neighbour_steps) if o[1] == 1]
SEG_ROW = S1 + 18 * len(ONE_UP)
MSG_DN = -(-(S1 + 18 * len(ONE_DN)) // 8) * 8
MSG_UP = -(-(SEG_ROW + 1) // 8) * 8


def call(kernel, out_shape, *args, flops=0, aliases=None):
    return pl.pallas_call(
        kernel,
        out_shape=out_shape,
        in_specs=[VMEM] * len(args),
        out_specs=jax.tree.map(lambda _: VMEM, out_shape),
        input_output_aliases=aliases or {},
        compiler_params=pltpu.CompilerParams(vmem_limit_bytes=LIMIT),
        cost_estimate=pl.CostEstimate(flops=flops, bytes_accessed=0, transcendentals=0),
    )(*args)


def struct(*shape):
    return jax.ShapeDtypeStruct(shape, F32)


def invert(b):
    a00, a01, a02, a11, a12, a22 = b
    c00 = a11 * a22 - a12 * a12
    c01 = a12 * a02 - a01 * a22
    c02 = a01 * a12 - a11 * a02
    c11 = a00 * a22 - a02 * a02
    c12 = a01 * a02 - a00 * a12
    c22 = a00 * a11 - a01 * a01
    det = a00 * c00 + a01 * c01 + a02 * c02
    return [c / det for c in (c00, c01, c02, c11, c12, c22)]


def pack_kernel(stencil, cands, seg, dn, up, inv):
    for p in range(2):
        blocks = [stencil[0, e, d, p] for e, d in SYM]
        for i, entry in enumerate(invert(blocks)):
            inv[i, p] = entry
    for c in range(K):
        for d in range(3):
            for p in range(2):
                i = (c * 3 + d) * 2 + p
                dn[pl.ds(V4 + 4 * i, 4), :] = cands[c, d, p, 0:4]
                up[pl.ds(V4 + 4 * i, 4), :] = cands[c, d, p, 4:8]
                dn[pl.ds(V1 + i, 1), :] = cands[c, d, p, 4:5]
                up[pl.ds(V1 + i, 1), :] = cands[c, d, p, 3:4]
    for i in range(6):
        for p in range(2):
            k = i * 2 + p
            dn[pl.ds(S4 + 4 * k, 4), :] = inv[i, p, 0:4]
            up[pl.ds(S4 + 4 * k, 4), :] = inv[i, p, 4:8]
    for j in range(13):
        for e in range(3):
            for d in range(3):
                for p in range(2):
                    k = 12 + ((j * 3 + e) * 3 + d) * 2 + p
                    dn[pl.ds(S4 + 4 * k, 4), :] = stencil[1 + j, e, d, p, 0:4]
                    up[pl.ds(S4 + 4 * k, 4), :] = stencil[1 + j, e, d, p, 4:8]
    for msg, ones, row in ((dn, ONE_DN, 4), (up, ONE_UP, 3)):
        for n, j in enumerate(ones):
            for e in range(3):
                for d in range(3):
                    for p in range(2):
                        at = S1 + n * 18 + (e * 3 + d) * 2 + p
                        msg[pl.ds(at, 1), :] = stencil[1 + j, e, d, p, row : row + 1]
    up[pl.ds(SEG_ROW, 1), :] = seg[0, 3:4].astype(F32)


def roll_z(x, by):
    return pltpu.roll(x, by % 128, x.ndim - 1)


def own_kernel(stencil, cands, inv, coef, rolled, inverse, field):
    own = pl.ds(8, 8)
    for c in range(K):
        for d in range(3):
            field[c * 3 + d, :, own, :] = cands[c, d]
    for i in range(6):
        inverse[i, :, own, :] = inv[i]
    for j in range(13):
        for e in range(3):
            for d in range(3):
                block = stencil[1 + j, e, d]
                coef[j * 9 + e * 3 + d, :, own, :] = block
                if j in ROLLED:
                    rolled[ROLLED.index(j) * 9 + e * 3 + d, :, own, :] = roll_z(
                        block, neighbour_steps[j][2]
                    )


def halo_kernel(from_up, from_dn, coef_in, rolled_in, inverse_in, field_in, coef, rolled, inverse, field):
    for msg, four, one, ones in ((from_up, 16, 20, ONE_DN), (from_dn, 4, 3, ONE_UP)):
        for i in range(24):
            for p in range(2):
                field[i, p, pl.ds(four, 4), :] = msg[pl.ds(V4 + 4 * (2 * i + p), 4), :]
                field[i, p, pl.ds(one, 1), :] = msg[pl.ds(V1 + 2 * i + p, 1), :]
        for i in range(6):
            for p in range(2):
                inverse[i, p, pl.ds(four, 4), :] = msg[pl.ds(S4 + 4 * (2 * i + p), 4), :]
        for j in range(13):
            for n in range(9):
                k = 12 + (j * 9 + n) * 2
                pair = msg[pl.ds(S4 + 4 * k, 8), :]
                coef[j * 9 + n, 0, pl.ds(four, 4), :] = pair[0:4]
                coef[j * 9 + n, 1, pl.ds(four, 4), :] = pair[4:8]
                if j in ROLLED:
                    pair = roll_z(pair, neighbour_steps[j][2])
                    rolled[ROLLED.index(j) * 9 + n, 0, pl.ds(four, 4), :] = pair[0:4]
                    rolled[ROLLED.index(j) * 9 + n, 1, pl.ds(four, 4), :] = pair[4:8]
        for m, j in enumerate(ones):
            for n in range(9):
                for p in range(2):
                    at = S1 + m * 18 + n * 2 + p
                    coef[j * 9 + n, p, pl.ds(one, 1), :] = msg[pl.ds(at, 1), :]


def gather_terms(coef, rolled, field, base, half, terms):
    lane = lax.broadcasted_iota(jnp.int32, (8, 128), 1)
    acc = {}
    loads = {}

    def value(c, d, plane, oy):
        key = (c, d, plane, oy)
        if key not in loads:
            loads[key] = field[(half * 4 + c) * 3 + d, plane, pl.ds(base + oy, 8), :]
        return loads[key]

    for cp, fp, j, transposed in sorted(terms, key=lambda t: (t[1], -neighbour_steps[t[2]][1] if t[3] else neighbour_steps[t[2]][1])):
        ox, oy, oz = neighbour_steps[j]
        for d in range(3):
            for e in range(3):
                if transposed:
                    m = coef[j * 9 + d * 3 + e, cp, pl.ds(base - oy, 8), :]
                    shift, row = -oz, -oy
                elif oz:
                    m = rolled[ROLLED.index(j) * 9 + e * 3 + d, cp, pl.ds(base, 8), :]
                    shift, row = oz, oy
                else:
                    m = coef[j * 9 + e * 3 + d, cp, pl.ds(base, 8), :]
                    shift, row = 0, oy
                for c in range(4):
                    t = m * value(c, d, fp, row)
                    key = (c, e, shift)
                    acc[key] = acc[key] + t if key in acc else t
    out = []
    for c in range(4):
        line = []
        for e in range(3):
            total = acc[c, e, 0]
            total = total + jnp.where(lane < 127, roll_z(acc[c, e, 1], -1), 0.0)
            total = total + jnp.where(lane > 0, roll_z(acc[c, e, -1], 1), 0.0)
            line.append(total)
        out.append(line)
    return out


FLAT = [j for j, o in enumerate(neighbour_steps) if o[0] == 0]
STEP = [j for j, o in enumerate(neighbour_steps) if o[0] == 1]
TERMS = [
    [(0, 0, j, t) for j in FLAT for t in (False, True)] + [(0, 1, j, False) for j in STEP],
    [(1, 1, j, t) for j in FLAT for t in (False, True)] + [(0, 0, j, True) for j in STEP],
]
OUT_TERMS = [(1, 1, j, True) for j in STEP]
IN_TERMS = [(1, 0, j, False) for j in STEP]


def outgoing(coef, field, push):
    def step(i, carry):
        tile, half = i // 2, i % 2
        base = 4 + 8 * tile
        got = gather_terms(coef, None, field, base, half, OUT_TERMS)
        for c in range(4):
            for e in range(3):
                push[(half * 4 + c) * 3 + e, pl.ds(pl.multiple_of(8 * tile, 8), 8), :] = got[c][e]
        return carry

    lax.fori_loop(0, 4, step, 0)


def plane_out(field, pull):
    for i in range(24):
        pull[i] = field[i, 0]


def first_kernel(coef, field, push, pull):
    plane_out(field, pull)
    outgoing(coef, field, push)


def local_kernel(coef, rolled, field, part):
    def step(i, carry):
        tile, half = i // 2, i % 2
        base = 4 + 8 * tile
        for p in range(2):
            got = gather_terms(coef, rolled, field, base, half, TERMS[p])
            for c in range(4):
                for e in range(3):
                    part[(half * 4 + c) * 3 + e, p, pl.ds(pl.multiple_of(8 * tile, 8), 8), :] = got[c][e]
        return carry

    lax.fori_loop(0, 4, step, 0)


def finish(coef, rolled, inverse, field, part, pushed, pulled, new):
    def step(i, carry):
        tile, half = i // 2, i % 2
        base = 4 + 8 * tile
        rows = pl.ds(pl.multiple_of(8 * tile, 8), 8)
        got = gather_terms(coef, rolled, pulled, base, half, IN_TERMS)
        for p in range(2):
            inv = [inverse[n, p, pl.ds(base, 8), :] * DAMPING for n in range(6)]
            for c in range(4):
                at = (half * 4 + c) * 3
                res = [
                    part[at + e, p, rows, :] + (got[c][e] if p else pushed[at + e, rows, :])
                    for e in range(3)
                ]
                for e in range(3):
                    v = field[at + e, p, pl.ds(base, 8), :]
                    step_ = (
                        inv[SYM_OF[e, 0]] * res[0]
                        + inv[SYM_OF[e, 1]] * res[1]
                        + inv[SYM_OF[e, 2]] * res[2]
                    )
                    new[at + e, p, pl.ds(base, 8), :] = (1.0 - DAMPING) * v - step_
        return carry

    lax.fori_loop(0, 4, step, 0)


def sweep_kernel(coef, rolled, inverse, field, part, pushed, pulled, new, push, pull):
    finish(coef, rolled, inverse, field, part, pushed, pulled, new)
    plane_out(new, pull)
    outgoing(coef, new, push)


def last_kernel(coef, rolled, inverse, field, part, pushed, pulled, new, to_dn, to_up):
    finish(coef, rolled, inverse, field, part, pushed, pulled, new)
    for i in range(24):
        to_dn[i] = new[i, 0]
        to_up[i] = new[i, 1]


def segments_kernel(seg, from_dn, frame):
    frame[0] = jnp.zeros((8, 128), F32)
    frame[0, pl.ds(0, 1), :] = from_dn[pl.ds(SEG_ROW, 1), :]
    frame[0, pl.ds(1, 4), :] = seg[0].astype(F32)


def qr_kernel(field, lower, upper_plane, seg, seg_lower, prolongator, coarse, q):
    lane = lax.broadcasted_iota(jnp.int32, (8, 128), 1)
    even = lane % 2 == 0
    valid_row = lax.broadcasted_iota(jnp.int32, (8, 128), 0) < 5

    def planes(fx):
        if fx == 0:
            return [lambda i, s: lower[i, s, :], lambda i, s: field[i, 0, s, :]]
        return [lambda i, s: field[i, 1, s, :], lambda i, s: upper_plane[i, s, :]]

    starts = None
    for fx in range(2):
        ids = (seg_lower if fx == 0 else seg)[0]
        joins_next = (ids == roll_z(ids, -2)) & (lane < 126)
        joins_prev = (ids == roll_z(ids, 2)) & (lane >= 2)

        def total(x):
            x = x + jnp.where(even, roll_z(x, -1), roll_z(x, 1))
            return x + jnp.where(joins_next, roll_z(x, -2), 0.0) + jnp.where(joins_prev, roll_z(x, 2), 0.0)

        def dot(a, b):
            s = a[0] * b[0]
            t = a[1] * b[1]
            u = a[2] * b[2]
            for n in range(3, 12, 3):
                s = s + a[n] * b[n]
                t = t + a[n + 1] * b[n + 1]
                u = u + a[n + 2] * b[n + 2]
            return total(s + t + u)

        if fx == 1:
            slot = lane.astype(F32)
            found = jnp.zeros((8, 128), jnp.int32)
            for bit in (64, 32, 16, 8, 4, 2, 1):
                before = jnp.take_along_axis(ids, found + (bit - 1), axis=1)
                found = jnp.where(before < slot, found + bit, found)
            top = jnp.max(ids, axis=1, keepdims=True)
            starts = found
            in_use = slot <= top

            def put(k, j, values):
                compact = jnp.take_along_axis(values, starts, axis=1)
                compact = jnp.where(in_use, compact, 0.0)
                coarse[k, j, 0] = compact[1:5, 0:NSEG]

        cols = []
        for i in range(K):
            col = []
            for get in planes(fx):
                for first in (7, 8):
                    for d in range(3):
                        col.append(get(i * 3 + d, pl.ds(first, 8, stride=2)))
            cols.append([jnp.where(valid_row, x, 1.0) for x in col])
        for k in range(K):
            length = jnp.sqrt(dot(cols[k], cols[k]))
            scale = 1.0 / length
            cols[k] = [x * scale for x in cols[k]]
            if fx == 1:
                put(k, k, length)
            for j in range(k + 1, K):
                r = dot(cols[k], cols[j])
                cols[j] = [x - r * y for x, y in zip(cols[j], cols[k])]
                if fx == 1:
                    put(k, j, r)
                    coarse[j, k, 0] = jnp.zeros((4, NSEG), F32)
            member = 1 - fx
            for d in range(3):
                odd_first = cols[k][member * 6 + d]
                even_first = cols[k][member * 6 + 3 + d]
                prolongator[k, d, fx, pl.ds(0, 4, stride=2), :] = even_first[0:4]
                prolongator[k, d, fx, pl.ds(1, 4, stride=2), :] = odd_first[1:5]


def moved(block, axis, by):
    size = lax.axis_size(axis)
    return lax.ppermute(block, axis, [((i + by) % size, i) for i in range(size)])


def body(stencil, cands, seg):
    msg_dn, msg_up, inv = call(
        pack_kernel,
        [struct(MSG_DN, 128), struct(MSG_UP, 128), struct(6, 2, 8, 128)],
        stencil, cands, seg,
    )
    from_up = moved(msg_dn, "gy", 1)
    from_dn = moved(msg_up, "gy", -1)
    frames = [struct(117, 2, ROWS, 128), struct(9 * len(ROLLED), 2, ROWS, 128), struct(6, 2, ROWS, 128), struct(24, 2, ROWS, 128)]
    own = call(own_kernel, frames, stencil, cands, inv, flops=10**7)
    coef, rolled, inverse, field = call(
        halo_kernel, frames, from_up, from_dn, *own, aliases={2: 0, 3: 1, 4: 2, 5: 3}
    )
    segs = call(segments_kernel, [struct(1, 8, 128)], seg, from_dn)[0]
    side = [struct(24, 16, 128), struct(24, ROWS, 128)]
    push, pull = call(first_kernel, side, coef, field)
    seg_lower = moved(segs, "gx", -1)
    for t in range(ITERS):
        pushed = moved(push, "gx", -1)
        pulled = moved(pull, "gx", 1)
        part = call(local_kernel, [struct(24, 2, 16, 128)], coef, rolled, field, flops=10**7)[0]
        pulled = pulled.reshape(24, 1, ROWS, 128)
        args = (coef, rolled, inverse, field, part, pushed, pulled)
        if t < ITERS - 1:
            field, push, pull = call(sweep_kernel, [frames[3]] + side, *args)
        else:
            field, to_dn, to_up = call(last_kernel, [frames[3]] + [struct(24, ROWS, 128)] * 2, *args)
    lower = moved(to_up, "gx", -1)
    upper_plane = moved(to_dn, "gx", 1)
    prolongator, coarse = pl.pallas_call(
        qr_kernel,
        out_shape=[struct(K, 3, 2, 8, 128), struct(K, K, 1, 4, NSEG)],
        in_specs=[VMEM] * 5,
        out_specs=[VMEM] * 2,
        scratch_shapes=[pltpu.VMEM((8, 12, 8, 128), F32)],
        compiler_params=pltpu.CompilerParams(vmem_limit_bytes=LIMIT),
    )(field, lower, upper_plane, segs, seg_lower)
    return prolongator, coarse


def solution(mesh):
    in_specs = (
        P(None, None, None, "gx", "gy", None),
        P(None, None, "gx", "gy", None),
        P("gx", "gy", None),
    )
    out_specs = (P(None, None, "gx", "gy", None), P(None, None, "gx", "gy", None))
    return jax.shard_map(body, mesh=mesh, in_specs=in_specs, out_specs=out_specs, check_vma=False)
```

profile of v0, /device:TPU:96, one launch (start us, length us, event | category | flops | bytes accessed | tf_op | source)
XLA Modules:
  0.0 85.0 jit_solution(16600667742393412605)
XLA Ops:
  0.6 1.2 %copy-done = f32[14,3,3,2,8,128]{5,4,3,2,1,0:T(8,128)S(1)} copy-done((f32[14,3,3,2,8,128]{5,4,3,2,1,0:T(8,128)S(1)}, f32[14,3,3,2,8,128]{5,4,3,2,1,0:T(8,128)}, u32[]{:S(2)}) %copy-start) | copy-done | bytes 1032216
  1.9 0.9 %copy-done.1 = f32[8,3,2,8,128]{4,3,2,1,0:T(8,128)S(1)} copy-done((f32[8,3,2,8,128]{4,3,2,1,0:T(8,128)S(1)}, f32[8,3,2,8,128]{4,3,2,1,0:T(8,128)}, u32[]{:S(2)}) %copy-start.1) | copy-done | bytes 196632
  2.8 0.7 copy-done.2
  3.5 0.3 shard_map.50
  3.8 3.2 %collective-permute-start.1 = (f32[1336,128]{1,0:T(8,128)S(1)}, f32[1336,128]{1,0:T(8,128)S(1)}, u32[]{:S(2)}, u32[]{:S(2)}) collective-permute-start(f32[1336,128]{1,0:T(8,128)S(1)} %get-tuple-element.28), channel_id=1, source_target_pairs={{7,0},{0,1},{1,2},{2,3},{3,4},{4,5},{5,6},{6,7},{15,8},{8,9},{9,10... | collective-permute-start | bytes 2052104 | tf_op jit(solution)/shard_map/ppermute | solution.py:362
  7.0 0.0 collective-permute-start
  7.0 0.2 shard_map.51
  7.2 17.2 %collective-permute-done.from_up = f32[1280,128]{1,0:T(8,128)S(1)} collective-permute-done((f32[1280,128]{1,0:T(8,128)S(1)}, f32[1280,128]{1,0:T(8,128)S(1)}, u32[]{:S(2)}, u32[]{:S(2)}) %collective-permute-start) | collective-permute-done | bytes 655392 | tf_op jit(solution)/shard_map/ppermute | solution.py:362
  24.4 0.3 shard_map.52
  24.7 0.6 shard_map.54
  25.3 3.5 %collective-permute-start.3 = (f32[24,24,128]{2,1,0:T(8,128)S(1)}, f32[24,24,128]{2,1,0:T(8,128)S(1)}, u32[]{:S(2)}, u32[]{:S(2)}) collective-permute-start(f32[24,24,128]{2,1,0:T(8,128)S(1)} %get-tuple-element.39), channel_id=1, source_target_pairs={{8,0},{16,8},{24,16},{32,24},{40,32},{48,40},{56,48},{64,56},{72,6... | collective-permute-start | bytes 884744 | tf_op jit(solution)/shard_map/ppermute | solution.py:362
  28.9 0.0 collective-permute-start.2
  28.9 1.8 %shard_map.53.part = f32[24,2,16,128]{3,2,1,0:T(8,128)S(1)} custom-call(f32[117,2,24,128]{3,2,1,0:T(8,128)S(1)} %get-tuple-element.34.coef, f32[81,2,24,128]{3,2,1,0:T(8,128)S(1)} %get-tuple-element.35.rolled, f32[24,2,24,128]{3,2,1,0:T(8,128)S(1)} %get-tuple-element.37.field), custom_call_target="tpu_custom_call" | custom-call | flops 10000000 | tf_op jit(solution)/shard_map/pallas_call | solution.py:44
  30.6 6.6 %collective-permute-done.2.pushed = f32[24,16,128]{2,1,0:T(8,128)S(1)} collective-permute-done((f32[24,16,128]{2,1,0:T(8,128)S(1)}, f32[24,16,128]{2,1,0:T(8,128)S(1)}, u32[]{:S(2)}, u32[]{:S(2)}) %collective-permute-start.2) | collective-permute-done | bytes 196640 | tf_op jit(solution)/shard_map/ppermute | solution.py:362
  37.3 1.2 %shard_map.55 = (f32[24,2,24,128]{3,2,1,0:T(8,128)S(1)}, f32[24,16,128]{2,1,0:T(8,128)S(1)}, f32[24,24,128]{2,1,0:T(8,128)S(1)}) custom-call(f32[117,2,24,128]{3,2,1,0:T(8,128)S(1)} %get-tuple-element.34.coef, f32[81,2,24,128]{3,2,1,0:T(8,128)S(1)} %get-tuple-element.35.rolled, f32[6,2,24,128]{3,2,1,0:T(8,128)S(1)} %get-tuple-element.36.inverse, ...), custom_call_target="tpu_custom_call" | custom-call | tf_op jit(solution)/shard_map/pallas_call | solution.py:44
  38.5 1.1 %collective-permute-start.5 = (f32[24,24,128]{2,1,0:T(8,128)S(1)}, f32[24,24,128]{2,1,0:T(8,128)S(1)}, u32[]{:S(2)}, u32[]{:S(2)}) collective-permute-start(f32[24,24,128]{2,1,0:T(8,128)S(1)} %get-tuple-element.42), channel_id=1, source_target_pairs={{8,0},{16,8},{24,16},{32,24},{40,32},{48,40},{56,48},{64,56},{72,6... | collective-permute-start | bytes 884744 | tf_op jit(solution)/shard_map/ppermute | solution.py:362
  39.6 1.7 %shard_map.56.part = f32[24,2,16,128]{3,2,1,0:T(8,128)S(1)} custom-call(f32[117,2,24,128]{3,2,1,0:T(8,128)S(1)} %get-tuple-element.34.coef, f32[81,2,24,128]{3,2,1,0:T(8,128)S(1)} %get-tuple-element.35.rolled, f32[24,2,24,128]{3,2,1,0:T(8,128)S(1)} %get-tuple-element.40.field), custom_call_target="tpu_custom_call" | custom-call | flops 10000000 | tf_op jit(solution)/shard_map/pallas_call | solution.py:44
  41.2 6.7 %collective-permute-done.4.pushed = f32[24,16,128]{2,1,0:T(8,128)S(1)} collective-permute-done((f32[24,16,128]{2,1,0:T(8,128)S(1)}, f32[24,16,128]{2,1,0:T(8,128)S(1)}, u32[]{:S(2)}, u32[]{:S(2)}) %collective-permute-start.4) | collective-permute-done | bytes 196640 | tf_op jit(solution)/shard_map/ppermute | solution.py:362
  48.0 0.0 collective-permute-done.5
  48.0 1.2 %shard_map.57 = (f32[24,2,24,128]{3,2,1,0:T(8,128)S(1)}, f32[24,16,128]{2,1,0:T(8,128)S(1)}, f32[24,24,128]{2,1,0:T(8,128)S(1)}) custom-call(f32[117,2,24,128]{3,2,1,0:T(8,128)S(1)} %get-tuple-element.34.coef, f32[81,2,24,128]{3,2,1,0:T(8,128)S(1)} %get-tuple-element.35.rolled, f32[6,2,24,128]{3,2,1,0:T(8,128)S(1)} %get-tuple-element.36.inverse, ...), custom_call_target="tpu_custom_call" | custom-call | tf_op jit(solution)/shard_map/pallas_call | solution.py:44
  49.2 1.1 %collective-permute-start.7 = (f32[24,24,128]{2,1,0:T(8,128)S(1)}, f32[24,24,128]{2,1,0:T(8,128)S(1)}, u32[]{:S(2)}, u32[]{:S(2)}) collective-permute-start(f32[24,24,128]{2,1,0:T(8,128)S(1)} %get-tuple-element.45), channel_id=1, source_target_pairs={{8,0},{16,8},{24,16},{32,24},{40,32},{48,40},{56,48},{64,56},{72,6... | collective-permute-start | bytes 884744 | tf_op jit(solution)/shard_map/ppermute | solution.py:362
  50.3 1.7 %shard_map.58.part = f32[24,2,16,128]{3,2,1,0:T(8,128)S(1)} custom-call(f32[117,2,24,128]{3,2,1,0:T(8,128)S(1)} %get-tuple-element.34.coef, f32[81,2,24,128]{3,2,1,0:T(8,128)S(1)} %get-tuple-element.35.rolled, f32[24,2,24,128]{3,2,1,0:T(8,128)S(1)} %get-tuple-element.43.field), custom_call_target="tpu_custom_call" | custom-call | flops 10000000 | tf_op jit(solution)/shard_map/pallas_call | solution.py:44
  52.0 6.7 %collective-permute-done.6.pushed = f32[24,16,128]{2,1,0:T(8,128)S(1)} collective-permute-done((f32[24,16,128]{2,1,0:T(8,128)S(1)}, f32[24,16,128]{2,1,0:T(8,128)S(1)}, u32[]{:S(2)}, u32[]{:S(2)}) %collective-permute-start.6) | collective-permute-done | bytes 196640 | tf_op jit(solution)/shard_map/ppermute | solution.py:362
  58.7 1.2 %shard_map.59 = (f32[24,2,24,128]{3,2,1,0:T(8,128)S(1)}, f32[24,16,128]{2,1,0:T(8,128)S(1)}, f32[24,24,128]{2,1,0:T(8,128)S(1)}) custom-call(f32[117,2,24,128]{3,2,1,0:T(8,128)S(1)} %get-tuple-element.34.coef, f32[81,2,24,128]{3,2,1,0:T(8,128)S(1)} %get-tuple-element.35.rolled, f32[6,2,24,128]{3,2,1,0:T(8,128)S(1)} %get-tuple-element.36.inverse, ...), custom_call_target="tpu_custom_call" | custom-call | tf_op jit(solution)/shard_map/pallas_call | solution.py:44
  59.9 1.1 %collective-permute-start.9 = (f32[24,24,128]{2,1,0:T(8,128)S(1)}, f32[24,24,128]{2,1,0:T(8,128)S(1)}, u32[]{:S(2)}, u32[]{:S(2)}) collective-permute-start(f32[24,24,128]{2,1,0:T(8,128)S(1)} %get-tuple-element.48), channel_id=1, source_target_pairs={{8,0},{16,8},{24,16},{32,24},{40,32},{48,40},{56,48},{64,56},{72,6... | collective-permute-start | bytes 884744 | tf_op jit(solution)/shard_map/ppermute | solution.py:362
  61.0 1.7 %shard_map.60.part = f32[24,2,16,128]{3,2,1,0:T(8,128)S(1)} custom-call(f32[117,2,24,128]{3,2,1,0:T(8,128)S(1)} %get-tuple-element.34.coef, f32[81,2,24,128]{3,2,1,0:T(8,128)S(1)} %get-tuple-element.35.rolled, f32[24,2,24,128]{3,2,1,0:T(8,128)S(1)} %get-tuple-element.46.field), custom_call_target="tpu_custom_call" | custom-call | flops 10000000 | tf_op jit(solution)/shard_map/pallas_call | solution.py:44
  62.7 6.7 %collective-permute-done.8.pushed = f32[24,16,128]{2,1,0:T(8,128)S(1)} collective-permute-done((f32[24,16,128]{2,1,0:T(8,128)S(1)}, f32[24,16,128]{2,1,0:T(8,128)S(1)}, u32[]{:S(2)}, u32[]{:S(2)}) %collective-permute-start.8) | collective-permute-done | bytes 196640 | tf_op jit(solution)/shard_map/ppermute | solution.py:362
  69.4 0.6 shard_map.61
  70.0 0.3 collective-permute-start.10
  70.3 5.1 %collective-permute-start.11 = (f32[24,24,128]{2,1,0:T(8,128)S(1)}, f32[24,24,128]{2,1,0:T(8,128)S(1)}, u32[]{:S(2)}, u32[]{:S(2)}) collective-permute-start(f32[24,24,128]{2,1,0:T(8,128)S(1)} %get-tuple-element.51), channel_id=1, source_target_pairs={{8,0},{16,8},{24,16},{32,24},{40,32},{48,40},{56,48},{64,56},{72,6... | collective-permute-start | bytes 884744 | tf_op jit(solution)/shard_map/ppermute | solution.py:362
  75.4 6.3 %collective-permute-done.12.seg_lower = f32[1,8,128]{2,1,0:T(8,128)S(1)} collective-permute-done((f32[1,8,128]{2,1,0:T(8,128)S(1)}, f32[1,8,128]{2,1,0:T(8,128)S(1)}, u32[]{:S(2)}, u32[]{:S(2)}) %collective-permute-start.12) | collective-permute-done | bytes 4128 | tf_op jit(solution)/shard_map/ppermute | solution.py:362
  81.7 3.2 %shard_map.63 = (f32[8,3,2,8,128]{4,3,2,1,0:T(8,128)}, f32[8,8,1,4,63]{4,3,2,1,0:T(4,128)}) custom-call(f32[24,2,24,128]{3,2,1,0:T(8,128)S(1)} %get-tuple-element.49.field, f32[24,24,128]{2,1,0:T(8,128)S(1)} %collective-permute-done.10.lower, f32[24,24,128]{2,1,0:T(8,128)S(1)} %collective-permute-done.11.upper_plane, f32[1,8,128]{2,1,0:T(8,128)S(1)} %shard_map.62.seg, ...), custom_call_target="tpu_custom_call" | custom-call | tf_op jit(solution)/shard_map/pallas_call | solution.py:394
  (16 shorter events, 0.0 us)
Async XLA Ops:
  0.6 1.2 %copy-start = (f32[14,3,3,2,8,128]{5,4,3,2,1,0:T(8,128)S(1)}, f32[14,3,3,2,8,128]{5,4,3,2,1,0:T(8,128)}, u32[]{:S(2)}) copy-start(f32[14,3,3,2,8,128]{5,4,3,2,1,0:T(8,128)} %stencil.3) | copy-start | bytes 3096580
  1.8 0.9 %copy-start.1 = (f32[8,3,2,8,128]{4,3,2,1,0:T(8,128)S(1)}, f32[8,3,2,8,128]{4,3,2,1,0:T(8,128)}, u32[]{:S(2)}) copy-start(f32[8,3,2,8,128]{4,3,2,1,0:T(8,128)} %cands.3) | copy-start | bytes 589828
  2.8 0.7 copy-start.2
  3.8 20.6 %collective-permute-start.1 = (f32[1336,128]{1,0:T(8,128)S(1)}, f32[1336,128]{1,0:T(8,128)S(1)}, u32[]{:S(2)}, u32[]{:S(2)}) collective-permute-start(f32[1336,128]{1,0:T(8,128)S(1)} %get-tuple-element.28), channel_id=1, source_target_pairs={{7,0},{0,1},{1,2},{2,3},{3,4},{4,5},{5,6},{6,7},{15,8},{8,9},{9,10... | collective-permute-start | bytes 2052104 | tf_op jit(solution)/shard_map/ppermute | solution.py:362
  7.0 17.4 %collective-permute-start = (f32[1280,128]{1,0:T(8,128)S(1)}, f32[1280,128]{1,0:T(8,128)S(1)}, u32[]{:S(2)}, u32[]{:S(2)}) collective-permute-start(f32[1280,128]{1,0:T(8,128)S(1)} %get-tuple-element.27), channel_id=1, source_target_pairs={{1,0},{2,1},{3,2},{4,3},{5,4},{6,5},{7,6},{0,7},{9,8},{10,9},{11,1... | collective-permute-start | bytes 1966088 | tf_op jit(solution)/shard_map/ppermute | solution.py:362
  25.3 12.0 %collective-permute-start.3 = (f32[24,24,128]{2,1,0:T(8,128)S(1)}, f32[24,24,128]{2,1,0:T(8,128)S(1)}, u32[]{:S(2)}, u32[]{:S(2)}) collective-permute-start(f32[24,24,128]{2,1,0:T(8,128)S(1)} %get-tuple-element.39), channel_id=1, source_target_pairs={{8,0},{16,8},{24,16},{32,24},{40,32},{48,40},{56,48},{64,56},{72,6... | collective-permute-start | bytes 884744 | tf_op jit(solution)/shard_map/ppermute | solution.py:362
  28.9 8.4 %collective-permute-start.2 = (f32[24,16,128]{2,1,0:T(8,128)S(1)}, f32[24,16,128]{2,1,0:T(8,128)S(1)}, u32[]{:S(2)}, u32[]{:S(2)}) collective-permute-start(f32[24,16,128]{2,1,0:T(8,128)S(1)} %get-tuple-element.38), channel_id=1, source_target_pairs={{248,0},{0,8},{8,16},{16,24},{24,32},{32,40},{40,48},{48,56},{56,6... | collective-permute-start | bytes 589832 | tf_op jit(solution)/shard_map/ppermute | solution.py:362
  38.5 9.5 %collective-permute-start.5 = (f32[24,24,128]{2,1,0:T(8,128)S(1)}, f32[24,24,128]{2,1,0:T(8,128)S(1)}, u32[]{:S(2)}, u32[]{:S(2)}) collective-permute-start(f32[24,24,128]{2,1,0:T(8,128)S(1)} %get-tuple-element.42), channel_id=1, source_target_pairs={{8,0},{16,8},{24,16},{32,24},{40,32},{48,40},{56,48},{64,56},{72,6... | collective-permute-start | bytes 884744 | tf_op jit(solution)/shard_map/ppermute | solution.py:362
  39.6 8.4 %collective-permute-start.4 = (f32[24,16,128]{2,1,0:T(8,128)S(1)}, f32[24,16,128]{2,1,0:T(8,128)S(1)}, u32[]{:S(2)}, u32[]{:S(2)}) collective-permute-start(f32[24,16,128]{2,1,0:T(8,128)S(1)} %get-tuple-element.41), channel_id=1, source_target_pairs={{248,0},{0,8},{8,16},{16,24},{24,32},{32,40},{40,48},{48,56},{56,6... | collective-permute-start | bytes 589832 | tf_op jit(solution)/shard_map/ppermute | solution.py:362
  49.2 9.5 %collective-permute-start.7 = (f32[24,24,128]{2,1,0:T(8,128)S(1)}, f32[24,24,128]{2,1,0:T(8,128)S(1)}, u32[]{:S(2)}, u32[]{:S(2)}) collective-permute-start(f32[24,24,128]{2,1,0:T(8,128)S(1)} %get-tuple-element.45), channel_id=1, source_target_pairs={{8,0},{16,8},{24,16},{32,24},{40,32},{48,40},{56,48},{64,56},{72,6... | collective-permute-start | bytes 884744 | tf_op jit(solution)/shard_map/ppermute | solution.py:362
  50.3 8.4 %collective-permute-start.6 = (f32[24,16,128]{2,1,0:T(8,128)S(1)}, f32[24,16,128]{2,1,0:T(8,128)S(1)}, u32[]{:S(2)}, u32[]{:S(2)}) collective-permute-start(f32[24,16,128]{2,1,0:T(8,128)S(1)} %get-tuple-element.44), channel_id=1, source_target_pairs={{248,0},{0,8},{8,16},{16,24},{24,32},{32,40},{40,48},{48,56},{56,6... | collective-permute-start | bytes 589832 | tf_op jit(solution)/shard_map/ppermute | solution.py:362
  59.9 9.5 %collective-permute-start.9 = (f32[24,24,128]{2,1,0:T(8,128)S(1)}, f32[24,24,128]{2,1,0:T(8,128)S(1)}, u32[]{:S(2)}, u32[]{:S(2)}) collective-permute-start(f32[24,24,128]{2,1,0:T(8,128)S(1)} %get-tuple-element.48), channel_id=1, source_target_pairs={{8,0},{16,8},{24,16},{32,24},{40,32},{48,40},{56,48},{64,56},{72,6... | collective-permute-start | bytes 884744 | tf_op jit(solution)/shard_map/ppermute | solution.py:362
  61.0 8.4 %collective-permute-start.8 = (f32[24,16,128]{2,1,0:T(8,128)S(1)}, f32[24,16,128]{2,1,0:T(8,128)S(1)}, u32[]{:S(2)}, u32[]{:S(2)}) collective-permute-start(f32[24,16,128]{2,1,0:T(8,128)S(1)} %get-tuple-element.47), channel_id=1, source_target_pairs={{248,0},{0,8},{8,16},{16,24},{24,32},{32,40},{40,48},{48,56},{56,6... | collective-permute-start | bytes 589832 | tf_op jit(solution)/shard_map/ppermute | solution.py:362
  69.4 6.0 %copy-start.3 = (s32[1,4,128]{2,1,0:T(4,128)S(1)}, s32[1,4,128]{2,1,0:T(4,128)}, u32[]{:S(2)}) copy-start(s32[1,4,128]{2,1,0:T(4,128)} %seg.3) | copy-start | bytes 6148
  70.0 11.7 %collective-permute-start.10 = (f32[24,24,128]{2,1,0:T(8,128)S(1)}, f32[24,24,128]{2,1,0:T(8,128)S(1)}, u32[]{:S(2)}, u32[]{:S(2)}) collective-permute-start(f32[24,24,128]{2,1,0:T(8,128)S(1)} %get-tuple-element.50), channel_id=1, source_target_pairs={{248,0},{0,8},{8,16},{16,24},{24,32},{32,40},{40,48},{48,56},{56,6... | collective-permute-start | bytes 884744 | tf_op jit(solution)/shard_map/ppermute | solution.py:362
  70.3 11.4 %collective-permute-start.11 = (f32[24,24,128]{2,1,0:T(8,128)S(1)}, f32[24,24,128]{2,1,0:T(8,128)S(1)}, u32[]{:S(2)}, u32[]{:S(2)}) collective-permute-start(f32[24,24,128]{2,1,0:T(8,128)S(1)} %get-tuple-element.51), channel_id=1, source_target_pairs={{8,0},{16,8},{24,16},{32,24},{40,32},{48,40},{56,48},{64,56},{72,6... | collective-permute-start | bytes 884744 | tf_op jit(solution)/shard_map/ppermute | solution.py:362
  75.4 6.4 %collective-permute-start.12 = (f32[1,8,128]{2,1,0:T(8,128)S(1)}, f32[1,8,128]{2,1,0:T(8,128)S(1)}, u32[]{:S(2)}, u32[]{:S(2)}) collective-permute-start(f32[1,8,128]{2,1,0:T(8,128)S(1)} %shard_map.62.seg), channel_id=1, source_target_pairs={{248,0},{0,8},{8,16},{16,24},{24,32},{32,40},{40,48},{48,56},{56,6... | collective-permute-start | bytes 12296 | tf_op jit(solution)/shard_map/ppermute | solution.py:362
where the time goes:
time: 85.1 us; the launch traced here: 85 us
  waiting for transfers between devices  50.4 us (59%)
  Pallas kernels  15.6 us (18%)
  starting transfers between devices  15.4 us (18%)
  local copies, waits for them, and re-layouts  2.82 us (3%)
    ppermute x13, waiting for transfers between devices, moved(): lax.ppermute(block, axis, [((i + by) % size, i) for i in range(size)])  50.4 us
    ppermute x13, starting transfers between devices, moved(): lax.ppermute(block, axis, [((i + by) % size, i) for i in range(size)])  15.4 us
    pallas_call x13, Pallas kernels, call(): pl.pallas_call(kernel, out_shape=out_shape, in_specs=[VMEM] * len(args),...  12.3 us
    pallas_call x1, Pallas kernels, body(): pl.pallas_call(qr_kernel, out_shape=[struct(K, 3, 2, 8, 128), struct(K, K...  3.23 us
    unnamed x8, local copies, waits for them, and re-layouts  2.82 us
  transfers between devices with their start and end apart: 13, of which 6 were waited for; matrix products, arithmetic and copies ran while one was open for 0% of the time, Pallas kernels for 8%

commit v1 on v0

v1 whole, which is shorter than its diff:
```python
import functools

import jax
import jax.numpy as jnp
import numpy as np
from jax import lax
from jax.experimental import pallas as pl
from jax.experimental.pallas import tpu as pltpu
from jax.sharding import PartitionSpec as P

ITERS = 4
NSEG = 63
K = 8
DAMPING = 0.8
F32 = jnp.float32
neighbour_steps = [
    (sx, sy, sz)
    for sx in (-1, 0, 1)
    for sy in (-1, 0, 1)
    for sz in (-1, 0, 1)
    if (sx, sy, sz) > (0, 0, 0)
]
ROLLED = [j for j, o in enumerate(neighbour_steps) if o[2] != 0]
SYM = [(0, 0), (0, 1), (0, 2), (1, 1), (1, 2), (2, 2)]
SYM_OF = {(e, d): SYM.index((min(e, d), max(e, d))) for e in range(3) for d in range(3)}
ROWS = 24
VMEM = pl.BlockSpec(memory_space=pltpu.VMEM)
LIMIT = 12 * 2**20

ONE_DN = [j for j, o in enumerate(neighbour_steps) if o[1] == -1]
ONE_UP = [j for j, o in enumerate(neighbour_steps) if o[1] == 1]
RIM_S = 48
RIM = 160
HALO = 4 * 2 * (6 + 117)
SEG_ROW = 4 * 48
EDGE = SEG_ROW + 8
PAD = 8


def call(kernel, out_shape, *args, flops=0, aliases=None, scratch=()):
    return pl.pallas_call(
        kernel,
        out_shape=out_shape,
        in_specs=[VMEM] * (len(args)),
        out_specs=jax.tree.map(lambda _: VMEM, out_shape),
        input_output_aliases=aliases or {},
        scratch_shapes=list(scratch),
        compiler_params=pltpu.CompilerParams(vmem_limit_bytes=LIMIT),
        cost_estimate=pl.CostEstimate(flops=flops, bytes_accessed=0, transcendentals=0),
    )(*args)


def parity():
    return lax.rem(lax.axis_index("gx"), 2)


def struct(*shape):
    return jax.ShapeDtypeStruct(shape, F32)


def invert(b):
    a00, a01, a02, a11, a12, a22 = b
    c00 = a11 * a22 - a12 * a12
    c01 = a12 * a02 - a01 * a22
    c02 = a01 * a12 - a11 * a02
    c11 = a00 * a22 - a02 * a02
    c12 = a01 * a02 - a00 * a12
    c22 = a00 * a11 - a01 * a01
    det = a00 * c00 + a01 * c01 + a02 * c02
    return [c / det for c in (c00, c01, c02, c11, c12, c22)]


def pack_kernel(stencil, cands, rim_dn, rim_up, coef, rolled, inverse, field):
    own = pl.ds(8, 8)
    for c in range(K):
        for d in range(3):
            field[c * 3 + d, :, own, :] = cands[c, d]
    for p in range(2):
        blocks = [stencil[0, e, d, p] for e, d in SYM]
        for i, entry in enumerate(invert(blocks)):
            inverse[i, p, own, :] = entry
    for j in range(13):
        for e in range(3):
            for d in range(3):
                block = stencil[1 + j, e, d]
                coef[j * 9 + e * 3 + d, :, own, :] = block
                if j in ROLLED:
                    rolled[ROLLED.index(j) * 9 + e * 3 + d, :, own, :] = roll_z(
                        block, neighbour_steps[j][2]
                    )
    for c in range(K):
        for d in range(3):
            for p in range(2):
                i = (c * 3 + d) * 2 + p
                rim_dn[pl.ds(i, 1), :] = cands[c, d, p, 0:1]
                rim_up[pl.ds(i, 1), :] = cands[c, d, p, 7:8]
    for msg, ones, row in ((rim_dn, ONE_DN, 0), (rim_up, ONE_UP, 7)):
        for n, j in enumerate(ones):
            for e in range(3):
                for d in range(3):
                    for p in range(2):
                        at = RIM_S + n * 18 + (e * 3 + d) * 2 + p
                        msg[pl.ds(at, 1), :] = stencil[1 + j, e, d, p, row : row + 1]


def roll_z(x, by):
    return pltpu.roll(x, by % 128, x.ndim - 1)


def pack_halo_kernel(stencil, inverse, halo_dn, halo_up):
    for i in range(6):
        for p in range(2):
            k = i * 2 + p
            halo_dn[pl.ds(4 * k, 4), :] = inverse[i, p, pl.ds(8, 4), :]
            halo_up[pl.ds(4 * k, 4), :] = inverse[i, p, pl.ds(12, 4), :]
    for j in range(13):
        for e in range(3):
            for d in range(3):
                for p in range(2):
                    k = 12 + ((j * 3 + e) * 3 + d) * 2 + p
                    halo_dn[pl.ds(4 * k, 4), :] = stencil[1 + j, e, d, p, 0:4]
                    halo_up[pl.ds(4 * k, 4), :] = stencil[1 + j, e, d, p, 4:8]


def halo_kernel(from_up, from_dn, coef_in, rolled_in, inverse_in, coef, rolled, inverse):
    for msg, four in ((from_up, 16), (from_dn, 4)):
        for i in range(6):
            for p in range(2):
                inverse[i, p, pl.ds(four, 4), :] = msg[pl.ds(4 * (2 * i + p), 4), :]
        for j in range(13):
            for n in range(9):
                k = 12 + (j * 9 + n) * 2
                pair = msg[pl.ds(4 * k, 8), :]
                coef[j * 9 + n, 0, pl.ds(four, 4), :] = pair[0:4]
                coef[j * 9 + n, 1, pl.ds(four, 4), :] = pair[4:8]
                if j in ROLLED:
                    pair = roll_z(pair, neighbour_steps[j][2])
                    rolled[ROLLED.index(j) * 9 + n, 0, pl.ds(four, 4), :] = pair[0:4]
                    rolled[ROLLED.index(j) * 9 + n, 1, pl.ds(four, 4), :] = pair[4:8]


def gather_terms(coef, rolled, load, base, half, terms):
    lane = lax.broadcasted_iota(jnp.int32, (8, 128), 1)
    acc = {}
    loads = {}

    def value(c, d, plane, oy):
        key = (c, d, plane, oy)
        if key not in loads:
            loads[key] = load((half * 4 + c) * 3 + d, plane, base + oy)
        return loads[key]

    for cp, fp, j, transposed in sorted(terms, key=lambda t: (t[1], -neighbour_steps[t[2]][1] if t[3] else neighbour_steps[t[2]][1])):
        ox, oy, oz = neighbour_steps[j]
        for d in range(3):
            for e in range(3):
                if transposed:
                    m = coef[j * 9 + d * 3 + e, cp, pl.ds(base - oy, 8), :]
                    shift, row = -oz, -oy
                elif oz:
                    m = rolled[ROLLED.index(j) * 9 + e * 3 + d, cp, pl.ds(base, 8), :]
                    shift, row = oz, oy
                else:
                    m = coef[j * 9 + e * 3 + d, cp, pl.ds(base, 8), :]
                    shift, row = 0, oy
                for c in range(4):
                    t = m * value(c, d, fp, row)
                    key = (c, e, shift)
                    acc[key] = acc[key] + t if key in acc else t
    out = []
    for c in range(4):
        line = []
        for e in range(3):
            total = acc[c, e, 0]
            total = total + jnp.where(lane < 127, roll_z(acc[c, e, 1], -1), 0.0)
            total = total + jnp.where(lane > 0, roll_z(acc[c, e, -1], 1), 0.0)
            line.append(total)
        out.append(line)
    return out


FLAT = [j for j, o in enumerate(neighbour_steps) if o[0] == 0]
STEP = [j for j, o in enumerate(neighbour_steps) if o[0] == 1]
TERMS = [
    [(0, 0, j, t) for j in FLAT for t in (False, True)] + [(0, 1, j, False) for j in STEP],
    [(1, 1, j, t) for j in FLAT for t in (False, True)] + [(0, 0, j, True) for j in STEP],
]
OUT_TERMS = [(1, 1, j, True) for j in STEP]
IN_TERMS = [(1, 0, j, False) for j in STEP]


def from_frame(field):
    return lambda i, plane, row: field[i, plane, pl.ds(row, 8), :]


def tiles(bases, step):
    if len(bases) == 1:
        for half in range(2):
            step(bases[0], half)
        return

    def one(i, carry):
        step(bases[0] + (i // 2) * 8, i % 2)
        return carry

    lax.fori_loop(0, 2 * len(bases), one, 0)


def side_rows(lo, hi, items):
    return PAD + items * (hi - lo) + PAD


def spot(i, row, lo, hi):
    return PAD + i * (hi - lo) + row - lo


def outgoing(coef, field, msg, slot, bases, lo, hi):
    def step(base, half):
        got = gather_terms(coef, None, from_frame(field), base, half, OUT_TERMS)
        for c in range(4):
            for e in range(3):
                i = (half * 4 + c) * 3 + e
                msg[slot, pl.ds(spot(i, base, lo, hi), 8), :] = got[c][e]

    tiles(bases, step)


def plane_out(field, plane, msg, slot, lo, hi):
    for i in range(24):
        msg[slot, pl.ds(spot(i, lo, lo, hi), hi - lo), :] = field[i, plane, pl.ds(lo, hi - lo), :]


def send(coef, field, box, same, other, bases, lo, hi):
    right = parity()
    outgoing(coef, field, box, right, bases, lo, hi)
    plane_out(field, 0, box, 1 - right, lo, hi)
    same[...] = box[0]
    other[...] = box[1]


def first_kernel(from_up, from_dn, coef_in, field_in, coef, field, same, other, box):
    for msg, row, ones in ((from_up, 16, ONE_DN), (from_dn, 7, ONE_UP)):
        for i in range(24):
            for p in range(2):
                field[i, p, pl.ds(row, 1), :] = msg[pl.ds(2 * i + p, 1), :]
        for m, j in enumerate(ones):
            for n in range(9):
                for p in range(2):
                    at = RIM_S + m * 18 + n * 2 + p
                    coef[j * 9 + n, p, pl.ds(row, 1), :] = msg[pl.ds(at, 1), :]
    send(coef, field, box, same, other, *ROUNDS[0])


def second_kernel(from_up, from_dn, coef, field_in, field, same, other, box):
    for msg, row in ((from_up, 16), (from_dn, 4)):
        for i in range(24):
            for p in range(2):
                field[i, p, pl.ds(row, 4), :] = msg[pl.ds(4 * (2 * i + p), 4), :]
    send(coef, field, box, same, other, *ROUNDS[1])


def local_kernel(bases, coef, rolled, field, part):
    def step(base, half):
        for p in range(2):
            got = gather_terms(coef, rolled, from_frame(field), base, half, TERMS[p])
            for c in range(4):
                for e in range(3):
                    part[(half * 4 + c) * 3 + e, p, pl.ds(base, 8), :] = got[c][e]

    tiles(bases, step)


def finish(coef, rolled, inverse, field, part, same, other, box, new, bases, lo, hi):
    box[0] = same[...]
    box[1] = other[...]
    right = parity()

    def load(i, plane, row):
        return box[right, pl.ds(spot(i, row, lo, hi), 8), :]

    def step(base, half):
        got = gather_terms(coef, rolled, load, base, half, IN_TERMS)
        for p in range(2):
            inv = [inverse[n, p, pl.ds(base, 8), :] * DAMPING for n in range(6)]
            for c in range(4):
                at = (half * 4 + c) * 3
                res = []
                for e in range(3):
                    far = got[c][e] if p else box[1 - right, pl.ds(spot(at + e, base, lo, hi), 8), :]
                    res.append(part[at + e, p, pl.ds(base, 8), :] + far)
                for e in range(3):
                    v = field[at + e, p, pl.ds(base, 8), :]
                    move = (
                        inv[SYM_OF[e, 0]] * res[0]
                        + inv[SYM_OF[e, 1]] * res[1]
                        + inv[SYM_OF[e, 2]] * res[2]
                    )
                    new[at + e, p, pl.ds(base, 8), :] = (1.0 - DAMPING) * v - move

    tiles(bases, step)


ROUNDS = [((8,), 7, 17), ((4, 12), 4, 20), ((4, 12), 5, 19), ((4, 12), 5, 19)]
QR_LO, QR_HI = 7, 17


def sweep_first(coef, rolled, inverse, field, part, same, other, seg, new, to_dn, to_up, box):
    finish(coef, rolled, inverse, field, part, same, other, box, new, *ROUNDS[0])
    for i in range(24):
        for p in range(2):
            to_dn[pl.ds(4 * (2 * i + p), 4), :] = new[i, p, pl.ds(8, 4), :]
            to_up[pl.ds(4 * (2 * i + p), 4), :] = new[i, p, pl.ds(12, 4), :]
    to_up[pl.ds(SEG_ROW, 1), :] = seg[0, 3:4].astype(F32)


def sweep_kernel(t, coef, rolled, inverse, field, part, same, other, new, same_out, other_out, box, box_out):
    finish(coef, rolled, inverse, field, part, same, other, box, new, *ROUNDS[t])
    send(coef, new, box_out, same_out, other_out, *ROUNDS[t + 1])


def last_kernel(coef, rolled, inverse, field, part, same, other, segs, new, same_out, other_out, box, box_out):
    finish(coef, rolled, inverse, field, part, same, other, box, new, *ROUNDS[-1])
    right = parity()
    plane_out(new, 1, box_out, right, QR_LO, QR_HI)
    plane_out(new, 0, box_out, 1 - right, QR_LO, QR_HI)
    box_out[right, pl.ds(0, 8), :] = segs[0]
    same_out[...] = box_out[0]
    other_out[...] = box_out[1]


def segments_kernel(seg, from_dn, frame):
    frame[0] = jnp.zeros((8, 128), F32)
    frame[0, pl.ds(0, 1), :] = from_dn[pl.ds(SEG_ROW, 1), :]
    frame[0, pl.ds(1, 4), :] = seg[0].astype(F32)


def qr_kernel(field, same, other, seg, prolongator, coarse, box):
    box[0] = same[...]
    box[1] = other[...]
    right = parity()
    lane = lax.broadcasted_iota(jnp.int32, (8, 128), 1)
    even = lane % 2 == 0
    valid_row = lax.broadcasted_iota(jnp.int32, (8, 128), 0) < 5

    def planes(fx):
        if fx == 0:
            return [lambda i, r: far(1 - right, i, r), lambda i, r: near(0, i, r)]
        return [lambda i, r: near(1, i, r), lambda i, r: far(right, i, r)]

    def near(p, i, row):
        return field[i, p, pl.ds(row, 8, stride=2), :]

    def far(slot, i, row):
        return box[slot, pl.ds(spot(i, row, QR_LO, QR_HI), 8, stride=2), :]

    starts = None
    for fx in range(2):
        ids = seg[0] if fx else box[1 - right, pl.ds(0, 8), :]
        joins_next = (ids == roll_z(ids, -2)) & (lane < 126)
        joins_prev = (ids == roll_z(ids, 2)) & (lane >= 2)

        def total(x):
            x = x + jnp.where(even, roll_z(x, -1), roll_z(x, 1))
            return x + jnp.where(joins_next, roll_z(x, -2), 0.0) + jnp.where(joins_prev, roll_z(x, 2), 0.0)

        def dot(a, b):
            s = a[0] * b[0]
            t = a[1] * b[1]
            u = a[2] * b[2]
            for n in range(3, 12, 3):
                s = s + a[n] * b[n]
                t = t + a[n + 1] * b[n + 1]
                u = u + a[n + 2] * b[n + 2]
            return total(s + t + u)

        if fx == 1:
            slot = lane.astype(F32)
            found = jnp.zeros((8, 128), jnp.int32)
            for bit in (64, 32, 16, 8, 4, 2, 1):
                before = jnp.take_along_axis(ids, found + (bit - 1), axis=1)
                found = jnp.where(before < slot, found + bit, found)
            top = jnp.max(ids, axis=1, keepdims=True)
            starts = found
            in_use = slot <= top

            def put(k, j, values):
                compact = jnp.take_along_axis(values, starts, axis=1)
                compact = jnp.where(in_use, compact, 0.0)
                coarse[k, j, 0] = compact[1:5, 0:NSEG]

        cols = []
        for i in range(K):
            col = []
            for get in planes(fx):
                for first in (7, 8):
                    for d in range(3):
                        col.append(get(i * 3 + d, first))
            cols.append([jnp.where(valid_row, x, 1.0) for x in col])
        for k in range(K):
            length = jnp.sqrt(dot(cols[k], cols[k]))
            scale = 1.0 / length
            cols[k] = [x * scale for x in cols[k]]
            if fx == 1:
                put(k, k, length)
            for j in range(k + 1, K):
                r = dot(cols[k], cols[j])
                cols[j] = [x - r * y for x, y in zip(cols[j], cols[k])]
                if fx == 1:
                    put(k, j, r)
                    coarse[j, k, 0] = jnp.zeros((4, NSEG), F32)
            member = 1 - fx
            for d in range(3):
                odd_first = cols[k][member * 6 + d]
                even_first = cols[k][member * 6 + 3 + d]
                prolongator[k, d, fx, pl.ds(0, 4, stride=2), :] = even_first[0:4]
                prolongator[k, d, fx, pl.ds(1, 4, stride=2), :] = odd_first[1:5]


def moved(block, axis, by):
    size = lax.axis_size(axis)
    return lax.ppermute(block, axis, [((i + by) % size, i) for i in range(size)])


def swapped(same, other):
    size = lax.axis_size("gx")
    pairs = [(i, i + 1) for i in range(0, size, 2)]
    around = [(i, (i + 1) % size) for i in range(1, size, 2)]
    return [
        lax.ppermute(block, "gx", two + [(j, i) for i, j in two])
        for block, two in ((same, pairs), (other, around))
    ]


def body(stencil, cands, seg):
    frame = struct(24, 2, ROWS, 128)
    operator = [struct(117, 2, ROWS, 128), struct(9 * len(ROLLED), 2, ROWS, 128), struct(6, 2, ROWS, 128)]
    rim_dn, rim_up, coef, rolled, inverse, field = call(
        pack_kernel, [struct(RIM, 128)] * 2 + operator + [frame], stencil, cands
    )
    rim_from_up = moved(rim_dn, "gy", 1)
    rim_from_dn = moved(rim_up, "gy", -1)
    halo_dn, halo_up = call(pack_halo_kernel, [struct(HALO, 128)] * 2, stencil, inverse)
    halo_dn, halo_up, rim_from_up, rim_from_dn = lax.optimization_barrier(
        (halo_dn, halo_up, rim_from_up, rim_from_dn)
    )
    halo_from_up = moved(halo_dn, "gy", 1)
    halo_from_dn = moved(halo_up, "gy", -1)

    def side(t):
        return [struct(side_rows(*ROUNDS[t][1:], 24), 128)] * 2

    def box(t, hi=None):
        lo, hi = ROUNDS[t][1:] if t is not None else (QR_LO, QR_HI)
        return pltpu.VMEM((2, side_rows(lo, hi, 24), 128), F32)

    coef, field, same, other = call(
        first_kernel, [operator[0], frame] + side(0), rim_from_up, rim_from_dn, coef, field,
        aliases={2: 0, 3: 1}, scratch=[box(0)],
    )
    for t in range(ITERS):
        same, other = swapped(same, other)
        part = call(functools.partial(local_kernel, ROUNDS[t][0]), [frame], coef, rolled, field, flops=10**7)[0]
        args = (coef, rolled, inverse, field, part, same, other)
        if t == 0:
            edge = struct(EDGE, 128)
            field, to_dn, to_up = call(sweep_first, [frame, edge, edge], *args, seg, scratch=[box(0)])
            from_up = moved(to_dn, "gy", 1)
            from_dn = moved(to_up, "gy", -1)
            segs = call(segments_kernel, [struct(1, 8, 128)], seg, from_dn)[0]
            coef, rolled, inverse = call(
                halo_kernel, operator, halo_from_up, halo_from_dn, coef, rolled, inverse, aliases={2: 0, 3: 1, 4: 2}
            )
            field, same, other = call(
                second_kernel, [frame] + side(1), from_up, from_dn, coef, field,
                aliases={3: 0}, scratch=[box(1)],
            )
        elif t < ITERS - 1:
            field, same, other = call(
                functools.partial(sweep_kernel, t), [frame] + side(t + 1), *args, scratch=[box(t), box(t + 1)]
            )
        else:
            last = struct(side_rows(QR_LO, QR_HI, 24), 128)
            field, same, other = call(
                last_kernel, [frame, last, last], *args, segs, scratch=[box(t), box(None)]
            )
    same, other = swapped(same, other)
    prolongator, coarse = call(
        qr_kernel, [struct(K, 3, 2, 8, 128), struct(K, K, 1, 4, NSEG)], field, same, other, segs,
        scratch=[box(None)],
    )
    return prolongator, coarse


def solution(mesh):
    in_specs = (
        P(None, None, None, "gx", "gy", None),
        P(None, None, "gx", "gy", None),
        P("gx", "gy", None),
    )
    out_specs = (P(None, None, "gx", "gy", None), P(None, None, "gx", "gy", None))
    return jax.shard_map(body, mesh=mesh, in_specs=in_specs, out_specs=out_specs, check_vma=False)
```

time: 85.1 us -> 72.7 us (0.85)
  the two profiles are of different devices: /device:TPU:96 before, /device:TPU:1 now
where the time goes in v1:
time: 72.7 us; the launch traced here: 71.6 us
  starting transfers between devices  28.8 us (40%)
  waiting for transfers between devices  25.3 us (35%)
  Pallas kernels  14.7 us (20%)
  local copies, waits for them, and re-layouts  2.14 us (3%)
  between operations  0.74 us (1%)
    ppermute x10, starting transfers between devices, swapped(): lax.ppermute(block, 'gx', two + [(j, i) for i, j in two])  19.3 us
    ppermute x10, waiting for transfers between devices, swapped(): lax.ppermute(block, 'gx', two + [(j, i) for i, j in two])  16.7 us
    pallas_call x15, Pallas kernels, call(): pl.pallas_call(kernel, out_shape=out_shape, in_specs=[VMEM] * len(args),...  14.7 us
    ppermute x6, starting transfers between devices, moved(): lax.ppermute(block, axis, [((i + by) % size, i) for i in range(size)])  9.49 us
    ppermute x6, waiting for transfers between devices, moved(): lax.ppermute(block, axis, [((i + by) % size, i) for i in range(size)])  8.52 us
    unnamed x6, local copies, waits for them, and re-layouts  2.14 us
  transfers between devices with their start and end apart: 16, of which 11 were waited for; matrix products, arithmetic and copies ran while one was open for 0% of the time, Pallas kernels for 10%

profile of v1, /device:TPU:1, one launch (start us, length us, event | category | flops | bytes accessed | tf_op | source)
XLA Modules:
  0.0 71.6 jit_solution(18090951240371859507)
XLA Ops:
  0.6 1.2 %copy-done = f32[14,3,3,2,8,128]{5,4,3,2,1,0:T(8,128)S(1)} copy-done((f32[14,3,3,2,8,128]{5,4,3,2,1,0:T(8,128)S(1)}, f32[14,3,3,2,8,128]{5,4,3,2,1,0:T(8,128)}, u32[]{:S(2)}) %copy-start) | copy-done | bytes 1032216
  1.9 0.9 %copy-done.1 = f32[8,3,2,8,128]{4,3,2,1,0:T(8,128)S(1)} copy-done((f32[8,3,2,8,128]{4,3,2,1,0:T(8,128)S(1)}, f32[8,3,2,8,128]{4,3,2,1,0:T(8,128)}, u32[]{:S(2)}) %copy-start.1) | copy-done | bytes 196632
  3.1 6.5 %collective-permute-start = (f32[160,128]{1,0:T(8,128)S(1)}, f32[160,128]{1,0:T(8,128)S(1)}, u32[]{:S(2)}, u32[]{:S(2)}) collective-permute-start(f32[160,128]{1,0:T(8,128)S(1)} %get-tuple-element.39), channel_id=1, source_target_pairs={{1,0},{2,1},{3,2},{4,3},{5,4},{6,5},{7,6},{0,7},{9,8},{10,9},{11,1... | collective-permute-start | bytes 245768 | tf_op jit(solution)/shard_map/ppermute | solution.py:421
  9.7 1.3 %collective-permute-done.from_up = f32[160,128]{1,0:T(8,128)S(1)} collective-permute-done((f32[160,128]{1,0:T(8,128)S(1)}, f32[160,128]{1,0:T(8,128)S(1)}, u32[]{:S(2)}, u32[]{:S(2)}) %collective-permute-start) | collective-permute-done | bytes 81952 | tf_op jit(solution)/shard_map/ppermute | solution.py:421
  11.0 3.0 %collective-permute-done.1.from_dn = f32[160,128]{1,0:T(8,128)S(1)} collective-permute-done((f32[160,128]{1,0:T(8,128)S(1)}, f32[160,128]{1,0:T(8,128)S(1)}, u32[]{:S(2)}, u32[]{:S(2)}) %collective-permute-start.1) | collective-permute-done | bytes 81952 | tf_op jit(solution)/shard_map/ppermute | solution.py:421
  14.1 1.5 %collective-permute-start.3 = (f32[984,128]{1,0:T(8,128)S(1)}, f32[984,128]{1,0:T(8,128)S(1)}, u32[]{:S(2)}, u32[]{:S(2)}) collective-permute-start(f32[984,128]{1,0:T(8,128)S(1)} %get-tuple-element.42), channel_id=1, source_target_pairs={{7,0},{0,1},{1,2},{2,3},{3,4},{4,5},{5,6},{6,7},{15,8},{8,9},{9,10... | collective-permute-start | bytes 1511432 | tf_op jit(solution)/shard_map/ppermute | solution.py:421
  15.8 2.8 %collective-permute-start.4 = (f32[256,128]{1,0:T(8,128)S(1)}, f32[256,128]{1,0:T(8,128)S(1)}, u32[]{:S(2)}, u32[]{:S(2)}) collective-permute-start(f32[256,128]{1,0:T(8,128)S(1)} %get-tuple-element.53), channel_id=1, source_target_pairs={{0,8},{16,24},{32,40},{48,56},{64,72},{80,88},{96,104},{112,120},{... | collective-permute-start | bytes 393224 | tf_op jit(solution)/shard_map/ppermute | solution.py:429
  18.6 1.3 %collective-permute-start.5 = (f32[256,128]{1,0:T(8,128)S(1)}, f32[256,128]{1,0:T(8,128)S(1)}, u32[]{:S(2)}, u32[]{:S(2)}) collective-permute-start(f32[256,128]{1,0:T(8,128)S(1)} %get-tuple-element.54), channel_id=1, source_target_pairs={{8,16},{24,32},{40,48},{56,64},{72,80},{88,96},{104,112},{120,128}... | collective-permute-start | bytes 393224 | tf_op jit(solution)/shard_map/ppermute | solution.py:429
  19.9 0.9 %shard_map.54.part = f32[24,2,24,128]{3,2,1,0:T(8,128)S(1)} custom-call(f32[117,2,24,128]{3,2,1,0:T(8,128)S(1)} %get-tuple-element.47.coef_in.coef, f32[81,2,24,128]{3,2,1,0:T(8,128)S(1)} %get-tuple-element.48.rolled_in.rolled, f32[24,2,24,128]{3,2,1,0:T(8,128)S(1)} %get-tuple-element.52.field), custom_call_target="tpu_custom_call" | custom-call | flops 10000000 | tf_op jit(solution)/shard_map/pallas_call | solution.py:41
  20.8 2.5 %collective-permute-done.5.other = f32[256,128]{1,0:T(8,128)S(1)} collective-permute-done((f32[256,128]{1,0:T(8,128)S(1)}, f32[256,128]{1,0:T(8,128)S(1)}, u32[]{:S(2)}, u32[]{:S(2)}) %collective-permute-start.5) | collective-permute-done | bytes 131104 | tf_op jit(solution)/shard_map/ppermute | solution.py:429
  23.6 1.0 %collective-permute-start.6 = (f32[200,128]{1,0:T(8,128)S(1)}, f32[200,128]{1,0:T(8,128)S(1)}, u32[]{:S(2)}, u32[]{:S(2)}) collective-permute-start(f32[200,128]{1,0:T(8,128)S(1)} %get-tuple-element.55), channel_id=1, source_target_pairs={{1,0},{2,1},{3,2},{4,3},{5,4},{6,5},{7,6},{0,7},{9,8},{10,9},{11,1... | collective-permute-start | bytes 307208 | tf_op jit(solution)/shard_map/ppermute | solution.py:421
  24.6 0.5 collective-permute-start.7
  25.1 1.0 %collective-permute-done.3.from_dn = f32[984,128]{1,0:T(8,128)S(1)} collective-permute-done((f32[984,128]{1,0:T(8,128)S(1)}, f32[984,128]{1,0:T(8,128)S(1)}, u32[]{:S(2)}, u32[]{:S(2)}) %collective-permute-start.3) | collective-permute-done | bytes 503840 | tf_op jit(solution)/shard_map/ppermute | solution.py:421
  26.4 2.2 %collective-permute-done.6.from_up = f32[200,128]{1,0:T(8,128)S(1)} collective-permute-done((f32[200,128]{1,0:T(8,128)S(1)}, f32[200,128]{1,0:T(8,128)S(1)}, u32[]{:S(2)}, u32[]{:S(2)}) %collective-permute-start.6) | collective-permute-done | bytes 102432 | tf_op jit(solution)/shard_map/ppermute | solution.py:421
  28.6 0.9 %collective-permute-done.7.from_dn = f32[200,128]{1,0:T(8,128)S(1)} collective-permute-done((f32[200,128]{1,0:T(8,128)S(1)}, f32[200,128]{1,0:T(8,128)S(1)}, u32[]{:S(2)}, u32[]{:S(2)}) %collective-permute-start.7) | collective-permute-done | bytes 102432 | tf_op jit(solution)/shard_map/ppermute | solution.py:421
  29.6 0.6 shard_map.56
  30.2 4.5 %collective-permute-start.8 = (f32[400,128]{1,0:T(8,128)S(1)}, f32[400,128]{1,0:T(8,128)S(1)}, u32[]{:S(2)}, u32[]{:S(2)}) collective-permute-start(f32[400,128]{1,0:T(8,128)S(1)} %get-tuple-element.59), channel_id=1, source_target_pairs={{0,8},{16,24},{32,40},{48,56},{64,72},{80,88},{96,104},{112,120},{... | collective-permute-start | bytes 614408 | tf_op jit(solution)/shard_map/ppermute | solution.py:429
  34.8 1.7 %shard_map.57.part = f32[24,2,24,128]{3,2,1,0:T(8,128)S(1)} custom-call(f32[117,2,24,128]{3,2,1,0:T(8,128)S(1)} %get-tuple-element.49.coef, f32[81,2,24,128]{3,2,1,0:T(8,128)S(1)} %get-tuple-element.50.rolled, f32[24,2,24,128]{3,2,1,0:T(8,128)S(1)} %get-tuple-element.58.field), custom_call_target="tpu_custom_call" | custom-call | flops 10000000 | tf_op jit(solution)/shard_map/pallas_call | solution.py:41
  36.5 3.5 %collective-permute-done.9.other = f32[400,128]{1,0:T(8,128)S(1)} collective-permute-done((f32[400,128]{1,0:T(8,128)S(1)}, f32[400,128]{1,0:T(8,128)S(1)}, u32[]{:S(2)}, u32[]{:S(2)}) %collective-permute-start.9) | collective-permute-done | bytes 204832 | tf_op jit(solution)/shard_map/ppermute | solution.py:429
  39.9 1.4 %shard_map.58 = (f32[24,2,24,128]{3,2,1,0:T(8,128)S(1)}, f32[352,128]{1,0:T(8,128)S(1)}, f32[352,128]{1,0:T(8,128)S(1)}) custom-call(f32[117,2,24,128]{3,2,1,0:T(8,128)S(1)} %get-tuple-element.49.coef, f32[81,2,24,128]{3,2,1,0:T(8,128)S(1)} %get-tuple-element.50.rolled, f32[6,2,24,128]{3,2,1,0:T(8,128)S(1)} %get-tuple-element.51.inverse, ...), custom_call_target="tpu_custom_call" | custom-call | tf_op jit(solution)/shard_map/pallas_call | solution.py:41
  41.3 3.5 %collective-permute-start.10 = (f32[352,128]{1,0:T(8,128)S(1)}, f32[352,128]{1,0:T(8,128)S(1)}, u32[]{:S(2)}, u32[]{:S(2)}) collective-permute-start(f32[352,128]{1,0:T(8,128)S(1)} %get-tuple-element.62), channel_id=1, source_target_pairs={{0,8},{16,24},{32,40},{48,56},{64,72},{80,88},{96,104},{112,120},{... | collective-permute-start | bytes 540680 | tf_op jit(solution)/shard_map/ppermute | solution.py:429
  44.8 1.8 %shard_map.59.part = f32[24,2,24,128]{3,2,1,0:T(8,128)S(1)} custom-call(f32[117,2,24,128]{3,2,1,0:T(8,128)S(1)} %get-tuple-element.49.coef, f32[81,2,24,128]{3,2,1,0:T(8,128)S(1)} %get-tuple-element.50.rolled, f32[24,2,24,128]{3,2,1,0:T(8,128)S(1)} %get-tuple-element.61.field), custom_call_target="tpu_custom_call" | custom-call | flops 10000000 | tf_op jit(solution)/shard_map/pallas_call | solution.py:41
  46.6 3.1 %collective-permute-done.11.other = f32[352,128]{1,0:T(8,128)S(1)} collective-permute-done((f32[352,128]{1,0:T(8,128)S(1)}, f32[352,128]{1,0:T(8,128)S(1)}, u32[]{:S(2)}, u32[]{:S(2)}) %collective-permute-start.11) | collective-permute-done | bytes 180256 | tf_op jit(solution)/shard_map/ppermute | solution.py:429
  49.7 1.3 %shard_map.60 = (f32[24,2,24,128]{3,2,1,0:T(8,128)S(1)}, f32[352,128]{1,0:T(8,128)S(1)}, f32[352,128]{1,0:T(8,128)S(1)}) custom-call(f32[117,2,24,128]{3,2,1,0:T(8,128)S(1)} %get-tuple-element.49.coef, f32[81,2,24,128]{3,2,1,0:T(8,128)S(1)} %get-tuple-element.50.rolled, f32[6,2,24,128]{3,2,1,0:T(8,128)S(1)} %get-tuple-element.51.inverse, ...), custom_call_target="tpu_custom_call" | custom-call | tf_op jit(solution)/shard_map/pallas_call | solution.py:41
  51.1 3.7 %collective-permute-start.12 = (f32[352,128]{1,0:T(8,128)S(1)}, f32[352,128]{1,0:T(8,128)S(1)}, u32[]{:S(2)}, u32[]{:S(2)}) collective-permute-start(f32[352,128]{1,0:T(8,128)S(1)} %get-tuple-element.65), channel_id=1, source_target_pairs={{0,8},{16,24},{32,40},{48,56},{64,72},{80,88},{96,104},{112,120},{... | collective-permute-start | bytes 540680 | tf_op jit(solution)/shard_map/ppermute | solution.py:429
  54.8 1.7 %shard_map.61.part = f32[24,2,24,128]{3,2,1,0:T(8,128)S(1)} custom-call(f32[117,2,24,128]{3,2,1,0:T(8,128)S(1)} %get-tuple-element.49.coef, f32[81,2,24,128]{3,2,1,0:T(8,128)S(1)} %get-tuple-element.50.rolled, f32[24,2,24,128]{3,2,1,0:T(8,128)S(1)} %get-tuple-element.64.field), custom_call_target="tpu_custom_call" | custom-call | flops 10000000 | tf_op jit(solution)/shard_map/pallas_call | solution.py:41
  56.5 3.2 %collective-permute-done.13.other = f32[352,128]{1,0:T(8,128)S(1)} collective-permute-done((f32[352,128]{1,0:T(8,128)S(1)}, f32[352,128]{1,0:T(8,128)S(1)}, u32[]{:S(2)}, u32[]{:S(2)}) %collective-permute-start.13) | collective-permute-done | bytes 180256 | tf_op jit(solution)/shard_map/ppermute | solution.py:429
  59.7 0.8 %shard_map.63 = (f32[24,2,24,128]{3,2,1,0:T(8,128)S(1)}, f32[256,128]{1,0:T(8,128)S(1)}, f32[256,128]{1,0:T(8,128)S(1)}) custom-call(f32[117,2,24,128]{3,2,1,0:T(8,128)S(1)} %get-tuple-element.49.coef, f32[81,2,24,128]{3,2,1,0:T(8,128)S(1)} %get-tuple-element.50.rolled, f32[6,2,24,128]{3,2,1,0:T(8,128)S(1)} %get-tuple-element.51.inverse, ...), custom_call_target="tpu_custom_call" | custom-call | tf_op jit(solution)/shard_map/pallas_call | solution.py:41
  60.5 3.5 %collective-permute-start.14 = (f32[256,128]{1,0:T(8,128)S(1)}, f32[256,128]{1,0:T(8,128)S(1)}, u32[]{:S(2)}, u32[]{:S(2)}) collective-permute-start(f32[256,128]{1,0:T(8,128)S(1)} %get-tuple-element.68), channel_id=1, source_target_pairs={{0,8},{16,24},{32,40},{48,56},{64,72},{80,88},{96,104},{112,120},{... | collective-permute-start | bytes 393224 | tf_op jit(solution)/shard_map/ppermute | solution.py:429
  64.0 1.0 %collective-permute-done.14.same = f32[256,128]{1,0:T(8,128)S(1)} collective-permute-done((f32[256,128]{1,0:T(8,128)S(1)}, f32[256,128]{1,0:T(8,128)S(1)}, u32[]{:S(2)}, u32[]{:S(2)}) %collective-permute-start.14) | collective-permute-done | bytes 131104 | tf_op jit(solution)/shard_map/ppermute | solution.py:429
  65.0 3.4 %collective-permute-done.15.other = f32[256,128]{1,0:T(8,128)S(1)} collective-permute-done((f32[256,128]{1,0:T(8,128)S(1)}, f32[256,128]{1,0:T(8,128)S(1)}, u32[]{:S(2)}, u32[]{:S(2)}) %collective-permute-start.15) | collective-permute-done | bytes 131104 | tf_op jit(solution)/shard_map/ppermute | solution.py:429
  68.4 3.3 %shard_map.64 = (f32[8,3,2,8,128]{4,3,2,1,0:T(8,128)}, f32[8,8,1,4,63]{4,3,2,1,0:T(4,128)}) custom-call(f32[24,2,24,128]{3,2,1,0:T(8,128)S(1)} %get-tuple-element.67.field, f32[256,128]{1,0:T(8,128)S(1)} %collective-permute-done.14.same, f32[256,128]{1,0:T(8,128)S(1)} %collective-permute-done.15.other, f32[1,8,128]{2,1,0:T(8,128)S(1)} %shard_map.62.segs.seg), custom_call_target="tpu_custom_call" | custom-call | tf_op jit(solution)/shard_map/pallas_call | solution.py:41
  (21 shorter events, 1.4 us)
Async XLA Ops:
  0.6 1.2 %copy-start = (f32[14,3,3,2,8,128]{5,4,3,2,1,0:T(8,128)S(1)}, f32[14,3,3,2,8,128]{5,4,3,2,1,0:T(8,128)}, u32[]{:S(2)}) copy-start(f32[14,3,3,2,8,128]{5,4,3,2,1,0:T(8,128)} %stencil.3) | copy-start | bytes 3096580
  1.8 0.9 %copy-start.1 = (f32[8,3,2,8,128]{4,3,2,1,0:T(8,128)S(1)}, f32[8,3,2,8,128]{4,3,2,1,0:T(8,128)}, u32[]{:S(2)}) copy-start(f32[8,3,2,8,128]{4,3,2,1,0:T(8,128)} %cands.1) | copy-start | bytes 589828
  3.1 8.0 %collective-permute-start = (f32[160,128]{1,0:T(8,128)S(1)}, f32[160,128]{1,0:T(8,128)S(1)}, u32[]{:S(2)}, u32[]{:S(2)}) collective-permute-start(f32[160,128]{1,0:T(8,128)S(1)} %get-tuple-element.39), channel_id=1, source_target_pairs={{1,0},{2,1},{3,2},{4,3},{5,4},{6,5},{7,6},{0,7},{9,8},{10,9},{11,1... | collective-permute-start | bytes 245768 | tf_op jit(solution)/shard_map/ppermute | solution.py:421
  9.6 4.5 %collective-permute-start.1 = (f32[160,128]{1,0:T(8,128)S(1)}, f32[160,128]{1,0:T(8,128)S(1)}, u32[]{:S(2)}, u32[]{:S(2)}) collective-permute-start(f32[160,128]{1,0:T(8,128)S(1)} %get-tuple-element.40), channel_id=1, source_target_pairs={{7,0},{0,1},{1,2},{2,3},{3,4},{4,5},{5,6},{6,7},{15,8},{8,9},{9,10... | collective-permute-start | bytes 245768 | tf_op jit(solution)/shard_map/ppermute | solution.py:421
  14.1 11.1 %collective-permute-start.2 = (f32[984,128]{1,0:T(8,128)S(1)}, f32[984,128]{1,0:T(8,128)S(1)}, u32[]{:S(2)}, u32[]{:S(2)}) collective-permute-start(f32[984,128]{1,0:T(8,128)S(1)} %get-tuple-element.41), channel_id=1, source_target_pairs={{1,0},{2,1},{3,2},{4,3},{5,4},{6,5},{7,6},{0,7},{9,8},{10,9},{11,1... | collective-permute-start | bytes 1511432 | tf_op jit(solution)/shard_map/ppermute | solution.py:421
  14.1 12.1 %collective-permute-start.3 = (f32[984,128]{1,0:T(8,128)S(1)}, f32[984,128]{1,0:T(8,128)S(1)}, u32[]{:S(2)}, u32[]{:S(2)}) collective-permute-start(f32[984,128]{1,0:T(8,128)S(1)} %get-tuple-element.42), channel_id=1, source_target_pairs={{7,0},{0,1},{1,2},{2,3},{3,4},{4,5},{5,6},{6,7},{15,8},{8,9},{9,10... | collective-permute-start | bytes 1511432 | tf_op jit(solution)/shard_map/ppermute | solution.py:421
  15.8 4.9 %collective-permute-start.4 = (f32[256,128]{1,0:T(8,128)S(1)}, f32[256,128]{1,0:T(8,128)S(1)}, u32[]{:S(2)}, u32[]{:S(2)}) collective-permute-start(f32[256,128]{1,0:T(8,128)S(1)} %get-tuple-element.53), channel_id=1, source_target_pairs={{0,8},{16,24},{32,40},{48,56},{64,72},{80,88},{96,104},{112,120},{... | collective-permute-start | bytes 393224 | tf_op jit(solution)/shard_map/ppermute | solution.py:429
  18.6 4.7 %collective-permute-start.5 = (f32[256,128]{1,0:T(8,128)S(1)}, f32[256,128]{1,0:T(8,128)S(1)}, u32[]{:S(2)}, u32[]{:S(2)}) collective-permute-start(f32[256,128]{1,0:T(8,128)S(1)} %get-tuple-element.54), channel_id=1, source_target_pairs={{8,16},{24,32},{40,48},{56,64},{72,80},{88,96},{104,112},{120,128}... | collective-permute-start | bytes 393224 | tf_op jit(solution)/shard_map/ppermute | solution.py:429
  19.9 3.4 %copy-start.2 = (s32[1,4,128]{2,1,0:T(4,128)S(1)}, s32[1,4,128]{2,1,0:T(4,128)}, u32[]{:S(2)}) copy-start(s32[1,4,128]{2,1,0:T(4,128)} %seg.3) | copy-start | bytes 6148
  23.6 5.0 %collective-permute-start.6 = (f32[200,128]{1,0:T(8,128)S(1)}, f32[200,128]{1,0:T(8,128)S(1)}, u32[]{:S(2)}, u32[]{:S(2)}) collective-permute-start(f32[200,128]{1,0:T(8,128)S(1)} %get-tuple-element.55), channel_id=1, source_target_pairs={{1,0},{2,1},{3,2},{4,3},{5,4},{6,5},{7,6},{0,7},{9,8},{10,9},{11,1... | collective-permute-start | bytes 307208 | tf_op jit(solution)/shard_map/ppermute | solution.py:421
  24.6 5.0 %collective-permute-start.7 = (f32[200,128]{1,0:T(8,128)S(1)}, f32[200,128]{1,0:T(8,128)S(1)}, u32[]{:S(2)}, u32[]{:S(2)}) collective-permute-start(f32[200,128]{1,0:T(8,128)S(1)} %get-tuple-element.56), channel_id=1, source_target_pairs={{7,0},{0,1},{1,2},{2,3},{3,4},{4,5},{5,6},{6,7},{15,8},{8,9},{9,10... | collective-permute-start | bytes 307208 | tf_op jit(solution)/shard_map/ppermute | solution.py:421
  30.2 6.2 %collective-permute-start.8 = (f32[400,128]{1,0:T(8,128)S(1)}, f32[400,128]{1,0:T(8,128)S(1)}, u32[]{:S(2)}, u32[]{:S(2)}) collective-permute-start(f32[400,128]{1,0:T(8,128)S(1)} %get-tuple-element.59), channel_id=1, source_target_pairs={{0,8},{16,24},{32,40},{48,56},{64,72},{80,88},{96,104},{112,120},{... | collective-permute-start | bytes 614408 | tf_op jit(solution)/shard_map/ppermute | solution.py:429
  34.8 5.2 %collective-permute-start.9 = (f32[400,128]{1,0:T(8,128)S(1)}, f32[400,128]{1,0:T(8,128)S(1)}, u32[]{:S(2)}, u32[]{:S(2)}) collective-permute-start(f32[400,128]{1,0:T(8,128)S(1)} %get-tuple-element.60), channel_id=1, source_target_pairs={{8,16},{24,32},{40,48},{56,64},{72,80},{88,96},{104,112},{120,128}... | collective-permute-start | bytes 614408 | tf_op jit(solution)/shard_map/ppermute | solution.py:429
  41.3 5.3 %collective-permute-start.10 = (f32[352,128]{1,0:T(8,128)S(1)}, f32[352,128]{1,0:T(8,128)S(1)}, u32[]{:S(2)}, u32[]{:S(2)}) collective-permute-start(f32[352,128]{1,0:T(8,128)S(1)} %get-tuple-element.62), channel_id=1, source_target_pairs={{0,8},{16,24},{32,40},{48,56},{64,72},{80,88},{96,104},{112,120},{... | collective-permute-start | bytes 540680 | tf_op jit(solution)/shard_map/ppermute | solution.py:429
  44.8 4.9 %collective-permute-start.11 = (f32[352,128]{1,0:T(8,128)S(1)}, f32[352,128]{1,0:T(8,128)S(1)}, u32[]{:S(2)}, u32[]{:S(2)}) collective-permute-start(f32[352,128]{1,0:T(8,128)S(1)} %get-tuple-element.63), channel_id=1, source_target_pairs={{8,16},{24,32},{40,48},{56,64},{72,80},{88,96},{104,112},{120,128}... | collective-permute-start | bytes 540680 | tf_op jit(solution)/shard_map/ppermute | solution.py:429
  51.1 5.4 %collective-permute-start.12 = (f32[352,128]{1,0:T(8,128)S(1)}, f32[352,128]{1,0:T(8,128)S(1)}, u32[]{:S(2)}, u32[]{:S(2)}) collective-permute-start(f32[352,128]{1,0:T(8,128)S(1)} %get-tuple-element.65), channel_id=1, source_target_pairs={{0,8},{16,24},{32,40},{48,56},{64,72},{80,88},{96,104},{112,120},{... | collective-permute-start | bytes 540680 | tf_op jit(solution)/shard_map/ppermute | solution.py:429
  54.8 4.9 %collective-permute-start.13 = (f32[352,128]{1,0:T(8,128)S(1)}, f32[352,128]{1,0:T(8,128)S(1)}, u32[]{:S(2)}, u32[]{:S(2)}) collective-permute-start(f32[352,128]{1,0:T(8,128)S(1)} %get-tuple-element.66), channel_id=1, source_target_pairs={{8,16},{24,32},{40,48},{56,64},{72,80},{88,96},{104,112},{120,128}... | collective-permute-start | bytes 540680 | tf_op jit(solution)/shard_map/ppermute | solution.py:429
  60.5 4.5 %collective-permute-start.14 = (f32[256,128]{1,0:T(8,128)S(1)}, f32[256,128]{1,0:T(8,128)S(1)}, u32[]{:S(2)}, u32[]{:S(2)}) collective-permute-start(f32[256,128]{1,0:T(8,128)S(1)} %get-tuple-element.68), channel_id=1, source_target_pairs={{0,8},{16,24},{32,40},{48,56},{64,72},{80,88},{96,104},{112,120},{... | collective-permute-start | bytes 393224 | tf_op jit(solution)/shard_map/ppermute | solution.py:429
  64.0 4.4 %collective-permute-start.15 = (f32[256,128]{1,0:T(8,128)S(1)}, f32[256,128]{1,0:T(8,128)S(1)}, u32[]{:S(2)}, u32[]{:S(2)}) collective-permute-start(f32[256,128]{1,0:T(8,128)S(1)} %get-tuple-element.69), channel_id=1, source_target_pairs={{8,16},{24,32},{40,48},{56,64},{72,80},{88,96},{104,112},{120,128}... | collective-permute-start | bytes 393224 | tf_op jit(solution)/shard_map/ppermute | solution.py:429

commit v2 on v1

v2 whole, which is shorter than its diff:
```python
import functools

import jax
import jax.numpy as jnp
import numpy as np
from jax import lax
from jax.experimental import pallas as pl
from jax.experimental.pallas import tpu as pltpu
from jax.sharding import PartitionSpec as P

ITERS = 4
NSEG = 63
K = 8
DAMPING = 0.8
F32 = jnp.float32
neighbour_steps = [
    (sx, sy, sz)
    for sx in (-1, 0, 1)
    for sy in (-1, 0, 1)
    for sz in (-1, 0, 1)
    if (sx, sy, sz) > (0, 0, 0)
]
ROLLED = [j for j, o in enumerate(neighbour_steps) if o[2] != 0]
SYM = [(0, 0), (0, 1), (0, 2), (1, 1), (1, 2), (2, 2)]
SYM_OF = {(e, d): SYM.index((min(e, d), max(e, d))) for e in range(3) for d in range(3)}
ROWS = 24
VMEM = pl.BlockSpec(memory_space=pltpu.VMEM)
ANY = pl.BlockSpec(memory_space=pl.ANY)
LIMIT = 12 * 2**20

ONE_DN = [j for j, o in enumerate(neighbour_steps) if o[1] == -1]
ONE_UP = [j for j, o in enumerate(neighbour_steps) if o[1] == 1]
RIM_S = 48
RIM = 160
HALO = 4 * 2 * (6 + 117)
SEG_ROW = 4 * 48
EDGE = SEG_ROW + 8
PAD = 8
FLOPS_PER_US = 1.1e9
BYTES_PER_US = 3.6e6


def call(kernel, out_shape, *args, us=0.3, aliases=None, scratch=(), after=0):
    return pl.pallas_call(
        kernel,
        out_shape=out_shape,
        in_specs=[VMEM] * (len(args) - after) + [ANY] * after,
        out_specs=jax.tree.map(lambda _: VMEM, out_shape),
        input_output_aliases=aliases or {},
        scratch_shapes=list(scratch),
        compiler_params=pltpu.CompilerParams(vmem_limit_bytes=LIMIT),
        cost_estimate=pl.CostEstimate(flops=int(us * FLOPS_PER_US), bytes_accessed=int(us * BYTES_PER_US), transcendentals=0),
    )(*args)


def parity():
    return lax.rem(lax.axis_index("gx"), 2)


def struct(*shape):
    return jax.ShapeDtypeStruct(shape, F32)


def invert(b):
    a00, a01, a02, a11, a12, a22 = b
    c00 = a11 * a22 - a12 * a12
    c01 = a12 * a02 - a01 * a22
    c02 = a01 * a12 - a11 * a02
    c11 = a00 * a22 - a02 * a02
    c12 = a01 * a02 - a00 * a12
    c22 = a00 * a11 - a01 * a01
    det = a00 * c00 + a01 * c01 + a02 * c02
    return [c / det for c in (c00, c01, c02, c11, c12, c22)]


def pack_kernel(stencil, cands, rim_dn, rim_up, coef, rolled, inverse, field):
    own = pl.ds(8, 8)
    for c in range(K):
        for d in range(3):
            field[c * 3 + d, :, own, :] = cands[c, d]
    for p in range(2):
        blocks = [stencil[0, e, d, p] for e, d in SYM]
        for i, entry in enumerate(invert(blocks)):
            inverse[i, p, own, :] = entry
    for j in range(13):
        for e in range(3):
            for d in range(3):
                block = stencil[1 + j, e, d]
                coef[j * 9 + e * 3 + d, :, own, :] = block
                if j in ROLLED:
                    rolled[ROLLED.index(j) * 9 + e * 3 + d, :, own, :] = roll_z(
                        block, neighbour_steps[j][2]
                    )
    for c in range(K):
        for d in range(3):
            for p in range(2):
                i = (c * 3 + d) * 2 + p
                rim_dn[pl.ds(i, 1), :] = cands[c, d, p, 0:1]
                rim_up[pl.ds(i, 1), :] = cands[c, d, p, 7:8]
    for msg, ones, row in ((rim_dn, ONE_DN, 0), (rim_up, ONE_UP, 7)):
        for n, j in enumerate(ones):
            for e in range(3):
                for d in range(3):
                    for p in range(2):
                        at = RIM_S + n * 18 + (e * 3 + d) * 2 + p
                        msg[pl.ds(at, 1), :] = stencil[1 + j, e, d, p, row : row + 1]


def roll_z(x, by):
    return pltpu.roll(x, by % 128, x.ndim - 1)


def pack_halo_kernel(stencil, inverse, _, _2, halo_dn, halo_up):
    for i in range(6):
        for p in range(2):
            k = i * 2 + p
            halo_dn[pl.ds(4 * k, 4), :] = inverse[i, p, pl.ds(8, 4), :]
            halo_up[pl.ds(4 * k, 4), :] = inverse[i, p, pl.ds(12, 4), :]
    for j in range(13):
        for e in range(3):
            for d in range(3):
                for p in range(2):
                    k = 12 + ((j * 3 + e) * 3 + d) * 2 + p
                    halo_dn[pl.ds(4 * k, 4), :] = stencil[1 + j, e, d, p, 0:4]
                    halo_up[pl.ds(4 * k, 4), :] = stencil[1 + j, e, d, p, 4:8]


def halo_kernel(from_up, from_dn, coef_in, rolled_in, inverse_in, coef, rolled, inverse):
    for msg, four in ((from_up, 16), (from_dn, 4)):
        for i in range(6):
            for p in range(2):
                inverse[i, p, pl.ds(four, 4), :] = msg[pl.ds(4 * (2 * i + p), 4), :]
        for j in range(13):
            for n in range(9):
                k = 12 + (j * 9 + n) * 2
                pair = msg[pl.ds(4 * k, 8), :]
                coef[j * 9 + n, 0, pl.ds(four, 4), :] = pair[0:4]
                coef[j * 9 + n, 1, pl.ds(four, 4), :] = pair[4:8]
                if j in ROLLED:
                    pair = roll_z(pair, neighbour_steps[j][2])
                    rolled[ROLLED.index(j) * 9 + n, 0, pl.ds(four, 4), :] = pair[0:4]
                    rolled[ROLLED.index(j) * 9 + n, 1, pl.ds(four, 4), :] = pair[4:8]


def matrices(coef, rolled, far_coef=None, far_rolled=None):
    def get(j, e, d, plane, row, turned):
        n = (ROLLED.index(j) if turned else j) * 9 + e * 3 + d
        if plane >= 0:
            return (rolled if turned else coef)[n, plane, pl.ds(row, 8), :]
        n = (STEP_ROLLED.index(j) if turned else STEP.index(j)) * 9 + e * 3 + d
        return (far_rolled if turned else far_coef)[n, pl.ds(row, 8), :]

    return get


def gather_terms(matrix, load, base, half, terms):
    lane = lax.broadcasted_iota(jnp.int32, (8, 128), 1)
    acc = {}
    loads = {}

    def value(c, d, plane, oy):
        key = (c, d, plane, oy)
        if key not in loads:
            loads[key] = load((half * 4 + c) * 3 + d, plane, base + oy)
        return loads[key]

    def order(term):
        oy = neighbour_steps[term[2]][1]
        return term[1], -oy if term[3] else oy

    for cp, fp, j, transposed in sorted(terms, key=order):
        oy, oz = neighbour_steps[j][1:]
        for d in range(3):
            for e in range(3):
                if transposed:
                    m = matrix(j, d, e, cp, base - oy, False)
                    shift, row = -oz, -oy
                else:
                    m = matrix(j, e, d, cp, base, oz != 0)
                    shift, row = oz, oy
                for c in range(4):
                    t = m * value(c, d, fp, row)
                    key = (c, e, shift)
                    acc[key] = acc[key] + t if key in acc else t
    out = []
    for c in range(4):
        line = []
        for e in range(3):
            total = acc[c, e, 0]
            total = total + jnp.where(lane < 127, roll_z(acc[c, e, 1], -1), 0.0)
            total = total + jnp.where(lane > 0, roll_z(acc[c, e, -1], 1), 0.0)
            line.append(total)
        out.append(line)
    return out


FLAT = [j for j, o in enumerate(neighbour_steps) if o[0] == 0]
STEP = [j for j, o in enumerate(neighbour_steps) if o[0] == 1]
STEP_ROLLED = [j for j in STEP if j in ROLLED]
TERMS = [
    [(0, 0, j, t) for j in FLAT for t in (False, True)] + [(0, 1, j, False) for j in STEP],
    [(1, 1, j, t) for j in FLAT for t in (False, True)] + [(0, 0, j, True) for j in STEP],
]
OUT_TERMS = [(1, 1, j, True) for j in STEP]
IN_TERMS = [(1, 2, j, False) for j in STEP]
LEFT_TERMS = [(-1, -1, j, True) for j in STEP]
FAR_TERMS = [(-1, 0, j, False) for j in STEP]


def from_frame(field):
    return lambda i, plane, row: field[i, plane, pl.ds(row, 8), :]


def tiles(bases, step):
    if len(bases) == 1:
        for half in range(2):
            step(bases[0], half)
        return

    def one(i, carry):
        step(bases[0] + (i // 2) * 8, i % 2)
        return carry

    lax.fori_loop(0, 2 * len(bases), one, 0)


def side_rows(lo, hi, items):
    return PAD + items * (hi - lo) + PAD


def spot(i, row, lo, hi):
    return PAD + i * (hi - lo) + row - lo


def outgoing(coef, field, msg, slot, bases, lo, hi):
    def step(base, half):
        got = gather_terms(matrices(coef, None), from_frame(field), base, half, OUT_TERMS)
        for c in range(4):
            for e in range(3):
                i = (half * 4 + c) * 3 + e
                msg[slot, pl.ds(spot(i, base, lo, hi), 8), :] = got[c][e]

    tiles(bases, step)


def plane_out(field, plane, msg, slot, lo, hi):
    for i in range(24):
        msg[slot, pl.ds(spot(i, lo, lo, hi), hi - lo), :] = field[i, plane, pl.ds(lo, hi - lo), :]


def send(coef, field, box, same, other, bases, lo, hi):
    right = parity()
    outgoing(coef, field, box, right, bases, lo, hi)
    plane_out(field, 0, box, 1 - right, lo, hi)
    same[...] = box[0]
    other[...] = box[1]


def first_kernel(from_up, from_dn, coef_in, field_in, coef, field, same, other, box):
    for msg, row, ones in ((from_up, 16, ONE_DN), (from_dn, 7, ONE_UP)):
        for i in range(24):
            for p in range(2):
                field[i, p, pl.ds(row, 1), :] = msg[pl.ds(2 * i + p, 1), :]
        for m, j in enumerate(ones):
            for n in range(9):
                for p in range(2):
                    at = RIM_S + m * 18 + n * 2 + p
                    coef[j * 9 + n, p, pl.ds(row, 1), :] = msg[pl.ds(at, 1), :]
    send(coef, field, box, same, other, *ROUNDS[0])


def second_kernel(from_up, from_dn, coef, field_in, field, same, other, box):
    for msg, row in ((from_up, 16), (from_dn, 4)):
        for i in range(24):
            for p in range(2):
                field[i, p, pl.ds(row, 4), :] = msg[pl.ds(4 * (2 * i + p), 4), :]
    send(coef, field, box, same, other, *ROUNDS[1])


def both_kernel(lo, hi, field, part, segs, same, other, box):
    right = parity()
    for plane, slot in ((1, right), (0, 1 - right)):
        for i in range(24):
            for n, ref in ((i, field), (24 + i, part)):
                box[slot, pl.ds(spot(n, lo, lo, hi), hi - lo), :] = ref[i, plane, pl.ds(lo, hi - lo), :]
    box[right, pl.ds(0, 8), :] = segs[0]
    same[...] = box[0]
    other[...] = box[1]


def pack_far_kernel(coef, inverse, same, other, box):
    right = parity()
    for i in range(81):
        box[right, pl.ds(16 * i, 16), :] = coef[9 * STEP[0] + i, 1, pl.ds(4, 16), :]
    for i in range(6):
        box[right, pl.ds(16 * (81 + i), 16), :] = inverse[i, 1, pl.ds(4, 16), :]
        box[1 - right, pl.ds(16 * (81 + i), 16), :] = inverse[i, 0, pl.ds(4, 16), :]
    same[...] = box[0]
    other[...] = box[1]


def far_kernel(same, other, far_coef, far_rolled, far_inverse, box):
    box[0] = same[...]
    box[1] = other[...]
    right = parity()
    rows = pl.ds(4, 16)
    for k, j in enumerate(STEP):
        for n in range(9):
            block = box[1 - right, pl.ds(16 * (9 * k + n), 16), :]
            far_coef[9 * k + n, rows, :] = block
            if j in ROLLED:
                far_rolled[9 * STEP_ROLLED.index(j) + n, rows, :] = roll_z(block, neighbour_steps[j][2])
    for i in range(6):
        far_inverse[i, 0, rows, :] = box[1 - right, pl.ds(16 * (81 + i), 16), :]
        far_inverse[i, 1, rows, :] = box[right, pl.ds(16 * (81 + i), 16), :]


def beyond_kernel(bases, coef, far_coef, far_rolled, field, far_part):
    get = matrices(coef, None, far_coef, far_rolled)

    def step(base, half):
        for n, terms in enumerate((FAR_TERMS, OUT_TERMS)):
            got = gather_terms(get, from_frame(field), base, half, terms)
            for c in range(4):
                for e in range(3):
                    far_part[(half * 4 + c) * 3 + e, n, pl.ds(base, 8), :] = got[c][e]

    tiles(bases, step)


def relax(inverse, p, base, v, res):
    inv = [inverse[n, p, pl.ds(base, 8), :] * DAMPING for n in range(6)]
    out = []
    for e in range(3):
        move = inv[SYM_OF[e, 0]] * res[0] + inv[SYM_OF[e, 1]] * res[1] + inv[SYM_OF[e, 2]] * res[2]
        out.append((1.0 - DAMPING) * v[e] - move)
    return out


def four_kernel(lo, hi, bases, coef, rolled, far_coef, inverse, far_inverse, field, part, far_part, same, other, new, far, far_seg, box):
    box[0] = same[...]
    box[1] = other[...]
    right = parity()
    get = matrices(coef, rolled, far_coef)

    far_seg[0] = box[1 - right, pl.ds(0, 8), :]

    def message(side, i, row):
        return box[right if side else 1 - right, pl.ds(spot(i, row, lo, hi), 8), :]

    def load(i, plane, row):
        return message(plane == 2, i, row)

    def step(base, half):
        here = pl.ds(base, 8)
        for p, terms in enumerate((LEFT_TERMS, IN_TERMS)):
            got = gather_terms(get, load, base, half, terms)
            for c in range(4):
                at = (half * 4 + c) * 3
                res = [part[at + e, p, here, :] + got[c][e] for e in range(3)]
                out = relax(inverse, p, base, [field[at + e, p, here, :] for e in range(3)], res)
                for e in range(3):
                    new[at + e, p, here, :] = out[e]
                res = [message(p, 24 + at + e, base) + far_part[at + e, p, here, :] for e in range(3)]
                out = relax(far_inverse, p, base, [message(p, at + e, base) for e in range(3)], res)
                for e in range(3):
                    far[at + e, p, here, :] = out[e]

    tiles(bases, step)


def local_kernel(bases, coef, rolled, field, part):
    def step(base, half):
        for p in range(2):
            got = gather_terms(matrices(coef, rolled), from_frame(field), base, half, TERMS[p])
            for c in range(4):
                for e in range(3):
                    part[(half * 4 + c) * 3 + e, p, pl.ds(base, 8), :] = got[c][e]

    tiles(bases, step)


def finish(coef, rolled, inverse, field, part, same, other, box, new, bases, lo, hi):
    box[0] = same[...]
    box[1] = other[...]
    right = parity()

    def load(i, plane, row):
        return box[right, pl.ds(spot(i, row, lo, hi), 8), :]

    def step(base, half):
        got = gather_terms(matrices(coef, rolled), load, base, half, IN_TERMS)
        for p in range(2):
            for c in range(4):
                at = (half * 4 + c) * 3
                res = []
                for e in range(3):
                    far = got[c][e] if p else box[1 - right, pl.ds(spot(at + e, base, lo, hi), 8), :]
                    res.append(part[at + e, p, pl.ds(base, 8), :] + far)
                out = relax(inverse, p, base, [field[at + e, p, pl.ds(base, 8), :] for e in range(3)], res)
                for e in range(3):
                    new[at + e, p, pl.ds(base, 8), :] = out[e]

    tiles(bases, step)


ROUNDS = [((8,), 7, 17), ((4, 12), 4, 20), ((4, 12), 5, 19)]
ALL = (4, 12)
LO, HI = 6, 18


def sweep_first(coef, rolled, inverse, field, part, same, other, seg, new, to_dn, to_up, box):
    finish(coef, rolled, inverse, field, part, same, other, box, new, *ROUNDS[0])
    for i in range(24):
        for p in range(2):
            to_dn[pl.ds(4 * (2 * i + p), 4), :] = new[i, p, pl.ds(8, 4), :]
            to_up[pl.ds(4 * (2 * i + p), 4), :] = new[i, p, pl.ds(12, 4), :]
    to_up[pl.ds(SEG_ROW, 1), :] = seg[0, 3:4].astype(F32)


def sweep_second(coef, rolled, inverse, field, part, same, other, new, same_out, other_out, box, box_out):
    finish(coef, rolled, inverse, field, part, same, other, box, new, *ROUNDS[1])
    send(coef, new, box_out, same_out, other_out, *ROUNDS[2])


def sweep_third(coef, rolled, inverse, field, part, same, other, new, box):
    finish(coef, rolled, inverse, field, part, same, other, box, new, *ROUNDS[2])


def segments_kernel(seg, from_dn, frame):
    frame[0] = jnp.zeros((8, 128), F32)
    frame[0, pl.ds(0, 1), :] = from_dn[pl.ds(SEG_ROW, 1), :]
    frame[0, pl.ds(1, 4), :] = seg[0].astype(F32)


def qr_kernel(field, far, seg, far_seg, prolongator, coarse):
    lane = lax.broadcasted_iota(jnp.int32, (8, 128), 1)
    even = lane % 2 == 0
    valid_row = lax.broadcasted_iota(jnp.int32, (8, 128), 0) < 5
    numbers = [far_seg[0], seg[0]]
    joins_next = [(ids == roll_z(ids, -2)) & (lane < 126) for ids in numbers]
    joins_prev = [(ids == roll_z(ids, 2)) & (lane >= 2) for ids in numbers]

    def dot(fx, a, b):
        parts = [x * y for x, y in zip(a, b)]
        while len(parts) > 1:
            parts = [x + y for x, y in zip(parts[::2], parts[1::2])] + parts[len(parts) // 2 * 2 :]
        x = parts[0]
        x = x + jnp.where(even, roll_z(x, -1), roll_z(x, 1))
        return x + (
            jnp.where(joins_next[fx], roll_z(x, -2), 0.0) + jnp.where(joins_prev[fx], roll_z(x, 2), 0.0)
        )

    ids = numbers[1]
    slot = lane.astype(F32)
    starts = jnp.zeros((8, 128), jnp.int32)
    for bit in (64, 32, 16, 8, 4, 2, 1):
        before = jnp.take_along_axis(ids, starts + (bit - 1), axis=1)
        starts = jnp.where(before < slot, starts + bit, starts)
    in_use = slot <= jnp.max(ids, axis=1, keepdims=True)

    def put(k, j, values):
        compact = jnp.take_along_axis(values, starts, axis=1)
        coarse[k, j, 0] = jnp.where(in_use, compact, 0.0)[1:5, 0:NSEG]

    cols = []
    for order in (((far, 0), (field, 0)), ((field, 1), (far, 1))):
        cols.append(
            [
                [
                    jnp.where(valid_row, ref[i * 3 + d, p, pl.ds(first, 8, stride=2), :], 1.0)
                    for ref, p in order
                    for first in (7, 8)
                    for d in range(3)
                ]
                for i in range(K)
            ]
        )
    for k in range(K):
        squares = [dot(fx, cols[fx][k], cols[fx][k]) for fx in range(2)]
        for fx in range(2):
            scale = lax.rsqrt(squares[fx])
            cols[fx][k] = [x * scale for x in cols[fx][k]]
        for j in range(k + 1, K):
            for fx in range(2):
                r = dot(fx, cols[fx][k], cols[fx][j])
                cols[fx][j] = [x - r * y for x, y in zip(cols[fx][j], cols[fx][k])]
                if fx == 1:
                    put(k, j, r)
                    coarse[j, k, 0] = jnp.zeros((4, NSEG), F32)
        put(k, k, jnp.sqrt(squares[1]))
        for fx in range(2):
            at = 6 * (1 - fx)
            for d in range(3):
                prolongator[k, d, fx, pl.ds(0, 4, stride=2), :] = cols[fx][k][at + 3 + d][0:4]
                prolongator[k, d, fx, pl.ds(1, 4, stride=2), :] = cols[fx][k][at + d][1:5]


def moved(block, axis, by):
    size = lax.axis_size(axis)
    return lax.ppermute(block, axis, [((i + by) % size, i) for i in range(size)])


def swapped(same, other):
    size = lax.axis_size("gx")
    pairs = [(i, i + 1) for i in range(0, size, 2)]
    around = [(i, (i + 1) % size) for i in range(1, size, 2)]
    return [
        lax.ppermute(block, "gx", two + [(j, i) for i, j in two])
        for block, two in ((same, pairs), (other, around))
    ]


def body(stencil, cands, seg):
    frame = struct(24, 2, ROWS, 128)
    operator = [struct(117, 2, ROWS, 128), struct(9 * len(ROLLED), 2, ROWS, 128), struct(6, 2, ROWS, 128)]
    rim_dn, rim_up, coef, rolled, inverse, field = call(
        pack_kernel, [struct(RIM, 128)] * 2 + operator + [frame], stencil, cands
    )
    rim_from_up = moved(rim_dn, "gy", 1)
    rim_from_dn = moved(rim_up, "gy", -1)

    edge = struct(EDGE, 128)
    sides = [struct(side_rows(lo, hi, 24), 128) for _, lo, hi in ROUNDS]
    boxes = [pltpu.VMEM((2, *side.shape), F32) for side in sides]

    def local(t):
        bases = ROUNDS[t][0] if t < 3 else ALL
        return call(functools.partial(local_kernel, bases), [frame], coef, rolled, field, us=1.7 if t else 0.9)[0]

    coef, field, same, other = call(
        first_kernel, [operator[0], frame, sides[0], sides[0]], rim_from_up, rim_from_dn, coef, field,
        aliases={2: 0, 3: 1}, scratch=boxes[:1],
    )
    same, other = swapped(same, other)
    halo_dn, halo_up = call(
        pack_halo_kernel, [struct(HALO, 128)] * 2, stencil, inverse, rim_from_up, rim_from_dn, after=2
    )
    halo_from_up = moved(halo_dn, "gy", 1)
    halo_from_dn = moved(halo_up, "gy", -1)
    part = local(0)
    field, to_dn, to_up = call(
        sweep_first, [frame, edge, edge], coef, rolled, inverse, field, part, same, other, seg, scratch=boxes[:1]
    )
    from_up = moved(to_dn, "gy", 1)
    from_dn = moved(to_up, "gy", -1)
    segs = call(segments_kernel, [struct(1, 8, 128)], seg, from_dn)[0]
    coef, rolled, inverse = call(
        halo_kernel, operator, halo_from_up, halo_from_dn, coef, rolled, inverse,
        aliases={2: 0, 3: 1, 4: 2},
    )
    field, same, other = call(
        second_kernel, [frame, sides[1], sides[1]], from_up, from_dn, coef, field, aliases={3: 0}, scratch=boxes[1:2], us=0.6
    )
    same, other = swapped(same, other)
    part = local(1)
    across = struct(16 * 87, 128)
    across_box = pltpu.VMEM((2, *across.shape), F32)
    across_same, across_other = swapped(
        *call(pack_far_kernel, [across, across], coef, inverse, scratch=[across_box])
    )
    field, same, other = call(
        sweep_second, [frame, sides[2], sides[2]], coef, rolled, inverse, field, part, same, other, scratch=boxes[1:], us=1.3
    )
    same, other = swapped(same, other)
    part = local(2)
    far_coef, far_rolled, far_inverse = call(
        far_kernel,
        [struct(81, ROWS, 128), struct(9 * len(STEP_ROLLED), ROWS, 128), operator[2]],
        across_same, across_other, scratch=[across_box],
    )
    field = call(
        sweep_third, [frame], coef, rolled, inverse, field, part, same, other, scratch=boxes[2:], us=0.8
    )[0]
    part = local(3)
    side = struct(side_rows(LO, HI, 48), 128)
    box = pltpu.VMEM((2, *side.shape), F32)
    same, other = swapped(
        *call(functools.partial(both_kernel, LO, HI), [side, side], field, part, segs, scratch=[box])
    )
    far_part = call(
        functools.partial(beyond_kernel, ALL), [frame], coef, far_coef, far_rolled, field, us=0.8
    )[0]
    field, far, far_seg = call(
        functools.partial(four_kernel, LO, HI, ALL), [frame, frame, struct(1, 8, 128)],
        coef, rolled, far_coef, inverse, far_inverse, field, part, far_part, same, other, scratch=[box],
    )
    prolongator, coarse = call(
        qr_kernel, [struct(K, 3, 2, 8, 128), struct(K, K, 1, 4, NSEG)], field, far, segs, far_seg, us=3.0
    )
    return prolongator, coarse


def solution(mesh):
    in_specs = (
        P(None, None, None, "gx", "gy", None),
        P(None, None, "gx", "gy", None),
        P("gx", "gy", None),
    )
    out_specs = (P(None, None, "gx", "gy", None), P(None, None, "gx", "gy", None))
    return jax.shard_map(body, mesh=mesh, in_specs=in_specs, out_specs=out_specs, check_vma=False)
```

time: 72.7 us -> 69 us (0.949); the launches traced: 71.6 us -> 68.9 us
  waiting for transfers between devices: 25.3 us -> 21.8 us
  Pallas kernels: 14.7 us -> 15.9 us
    ppermute x10, waiting for transfers between devices: 16.7 us -> 13 us  [swapped(): lax.ppermute(block, 'gx', two + [(j, i) for i, j in two])]
    pallas_call x15 -> x19, Pallas kernels: 14.7 us -> 15.9 us  [call(): pl.pallas_call(kernel, out_shape=out_shape, in_specs=[VMEM] * (len(args)...]
  transfers between devices with their start and end apart: 16 -> 16, of which waited for: 11 -> 9; matrix products, arithmetic and copies ran while one was open for 0% -> 0% of each run, Pallas kernels for 10% -> 15%
where the time goes in v2:
time: 69 us; the launch traced here: 68.9 us
  starting transfers between devices  28.2 us (41%)
  waiting for transfers between devices  21.8 us (32%)
  Pallas kernels  15.9 us (23%)
  local copies, waits for them, and re-layouts  2.14 us (3%)
  between operations  0.76 us (1%)
    ppermute x10, starting transfers between devices, swapped(): lax.ppermute(block, 'gx', two + [(j, i) for i, j in two])  18.6 us
    pallas_call x19, Pallas kernels, call(): pl.pallas_call(kernel, out_shape=out_shape, in_specs=[VMEM] * (len(args)...  15.9 us
    ppermute x10, waiting for transfers between devices, swapped(): lax.ppermute(block, 'gx', two + [(j, i) for i, j in two])  13 us
    ppermute x6, starting transfers between devices, moved(): lax.ppermute(block, axis, [((i + by) % size, i) for i in range(size)])  9.56 us
    ppermute x6, waiting for transfers between devices, moved(): lax.ppermute(block, axis, [((i + by) % size, i) for i in range(size)])  8.76 us
    unnamed x6, local copies, waits for them, and re-layouts  2.14 us
  transfers between devices with their start and end apart: 16, of which 9 were waited for; matrix products, arithmetic and copies ran while one was open for 0% of the time, Pallas kernels for 15%

profile of v2, /device:TPU:1, one launch (start us, length us, event | category | flops | bytes accessed | tf_op | source)
XLA Modules:
  0.0 68.9 jit_solution(9219204355705209022)
XLA Ops:
  0.6 1.2 %copy-done = f32[14,3,3,2,8,128]{5,4,3,2,1,0:T(8,128)S(1)} copy-done((f32[14,3,3,2,8,128]{5,4,3,2,1,0:T(8,128)S(1)}, f32[14,3,3,2,8,128]{5,4,3,2,1,0:T(8,128)}, u32[]{:S(2)}) %copy-start) | copy-done | bytes 1032216
  1.9 0.9 %copy-done.1 = f32[8,3,2,8,128]{4,3,2,1,0:T(8,128)S(1)} copy-done((f32[8,3,2,8,128]{4,3,2,1,0:T(8,128)S(1)}, f32[8,3,2,8,128]{4,3,2,1,0:T(8,128)}, u32[]{:S(2)}) %copy-start.1) | copy-done | bytes 196632
  3.1 6.5 %collective-permute-start = (f32[160,128]{1,0:T(8,128)S(1)}, f32[160,128]{1,0:T(8,128)S(1)}, u32[]{:S(2)}, u32[]{:S(2)}) collective-permute-start(f32[160,128]{1,0:T(8,128)S(1)} %get-tuple-element.37), channel_id=1, source_target_pairs={{1,0},{2,1},{3,2},{4,3},{5,4},{6,5},{7,6},{0,7},{9,8},{10,9},{11,1... | collective-permute-start | bytes 245768 | tf_op jit(solution)/shard_map/ppermute | solution.py:501
  9.6 1.5 %collective-permute-done._.from_up = f32[160,128]{1,0:T(8,128)S(1)} collective-permute-done((f32[160,128]{1,0:T(8,128)S(1)}, f32[160,128]{1,0:T(8,128)S(1)}, u32[]{:S(2)}, u32[]{:S(2)}) %collective-permute-start) | collective-permute-done | bytes 81952 | tf_op jit(solution)/shard_map/ppermute | solution.py:501
  11.0 3.0 %collective-permute-done.1._2.from_dn = f32[160,128]{1,0:T(8,128)S(1)} collective-permute-done((f32[160,128]{1,0:T(8,128)S(1)}, f32[160,128]{1,0:T(8,128)S(1)}, u32[]{:S(2)}, u32[]{:S(2)}) %collective-permute-start.1) | collective-permute-done | bytes 81952 | tf_op jit(solution)/shard_map/ppermute | solution.py:501
  14.3 1.5 %collective-permute-start.3 = (f32[984,128]{1,0:T(8,128)S(1)}, f32[984,128]{1,0:T(8,128)S(1)}, u32[]{:S(2)}, u32[]{:S(2)}) collective-permute-start(f32[984,128]{1,0:T(8,128)S(1)} %get-tuple-element.40), channel_id=1, source_target_pairs={{7,0},{0,1},{1,2},{2,3},{3,4},{4,5},{5,6},{6,7},{15,8},{8,9},{9,10... | collective-permute-start | bytes 1511432 | tf_op jit(solution)/shard_map/ppermute | solution.py:501
  15.8 0.3 shard_map.52
  16.1 2.8 %collective-permute-start.6 = (f32[256,128]{1,0:T(8,128)S(1)}, f32[256,128]{1,0:T(8,128)S(1)}, u32[]{:S(2)}, u32[]{:S(2)}) collective-permute-start(f32[256,128]{1,0:T(8,128)S(1)} %get-tuple-element.53), channel_id=1, source_target_pairs={{0,8},{16,24},{32,40},{48,56},{64,72},{80,88},{96,104},{112,120},{... | collective-permute-start | bytes 393224 | tf_op jit(solution)/shard_map/ppermute | solution.py:509
  18.8 1.3 %collective-permute-start.7 = (f32[256,128]{1,0:T(8,128)S(1)}, f32[256,128]{1,0:T(8,128)S(1)}, u32[]{:S(2)}, u32[]{:S(2)}) collective-permute-start(f32[256,128]{1,0:T(8,128)S(1)} %get-tuple-element.54), channel_id=1, source_target_pairs={{8,16},{24,32},{40,48},{56,64},{72,80},{88,96},{104,112},{120,128}... | collective-permute-start | bytes 393224 | tf_op jit(solution)/shard_map/ppermute | solution.py:509
  20.1 0.9 %shard_map.56.part = f32[24,2,24,128]{3,2,1,0:T(8,128)S(1)} custom-call(f32[117,2,24,128]{3,2,1,0:T(8,128)S(1)} %get-tuple-element.43.coef_in.coef, f32[81,2,24,128]{3,2,1,0:T(8,128)S(1)} %get-tuple-element.44.rolled_in.rolled, f32[24,2,24,128]{3,2,1,0:T(8,128)S(1)} %get-tuple-element.52.field), custom_call_target="tpu_custom_call" | custom-call | flops 990000000 | bytes 3240000 | tf_op jit(solution)/shard_map/pallas_call | solution.py:44
  21.1 2.5 %collective-permute-done.7.other = f32[256,128]{1,0:T(8,128)S(1)} collective-permute-done((f32[256,128]{1,0:T(8,128)S(1)}, f32[256,128]{1,0:T(8,128)S(1)}, u32[]{:S(2)}, u32[]{:S(2)}) %collective-permute-start.7) | collective-permute-done | bytes 131104 | tf_op jit(solution)/shard_map/ppermute | solution.py:509
  23.5 0.3 shard_map.57
  23.9 1.1 %collective-permute-start.8 = (f32[200,128]{1,0:T(8,128)S(1)}, f32[200,128]{1,0:T(8,128)S(1)}, u32[]{:S(2)}, u32[]{:S(2)}) collective-permute-start(f32[200,128]{1,0:T(8,128)S(1)} %get-tuple-element.55), channel_id=1, source_target_pairs={{1,0},{2,1},{3,2},{4,3},{5,4},{6,5},{7,6},{0,7},{9,8},{10,9},{11,1... | collective-permute-start | bytes 307208 | tf_op jit(solution)/shard_map/ppermute | solution.py:501
  25.0 0.4 collective-permute-start.9
  25.4 1.1 %collective-permute-done.3.from_dn = f32[984,128]{1,0:T(8,128)S(1)} collective-permute-done((f32[984,128]{1,0:T(8,128)S(1)}, f32[984,128]{1,0:T(8,128)S(1)}, u32[]{:S(2)}, u32[]{:S(2)}) %collective-permute-start.3) | collective-permute-done | bytes 503840 | tf_op jit(solution)/shard_map/ppermute | solution.py:501
  26.7 2.2 %collective-permute-done.8.from_up = f32[200,128]{1,0:T(8,128)S(1)} collective-permute-done((f32[200,128]{1,0:T(8,128)S(1)}, f32[200,128]{1,0:T(8,128)S(1)}, u32[]{:S(2)}, u32[]{:S(2)}) %collective-permute-start.8) | collective-permute-done | bytes 102432 | tf_op jit(solution)/shard_map/ppermute | solution.py:501
  28.9 1.0 %collective-permute-done.9.from_dn = f32[200,128]{1,0:T(8,128)S(1)} collective-permute-done((f32[200,128]{1,0:T(8,128)S(1)}, f32[200,128]{1,0:T(8,128)S(1)}, u32[]{:S(2)}, u32[]{:S(2)}) %collective-permute-start.9) | collective-permute-done | bytes 102432 | tf_op jit(solution)/shard_map/ppermute | solution.py:501
  29.9 0.6 shard_map.58
  30.6 4.6 %collective-permute-start.10 = (f32[400,128]{1,0:T(8,128)S(1)}, f32[400,128]{1,0:T(8,128)S(1)}, u32[]{:S(2)}, u32[]{:S(2)}) collective-permute-start(f32[400,128]{1,0:T(8,128)S(1)} %get-tuple-element.59), channel_id=1, source_target_pairs={{0,8},{16,24},{32,40},{48,56},{64,72},{80,88},{96,104},{112,120},{... | collective-permute-start | bytes 614408 | tf_op jit(solution)/shard_map/ppermute | solution.py:509
  35.3 3.8 %collective-permute-start.4 = (f32[1392,128]{1,0:T(8,128)S(1)}, f32[1392,128]{1,0:T(8,128)S(1)}, u32[]{:S(2)}, u32[]{:S(2)}) collective-permute-start(f32[1392,128]{1,0:T(8,128)S(1)} %get-tuple-element.48), channel_id=1, source_target_pairs={{0,8},{16,24},{32,40},{48,56},{64,72},{80,88},{96,104},{112,120},{... | collective-permute-start | bytes 2138120 | tf_op jit(solution)/shard_map/ppermute | solution.py:509
  39.1 1.7 %shard_map.59.part = f32[24,2,24,128]{3,2,1,0:T(8,128)S(1)} custom-call(f32[117,2,24,128]{3,2,1,0:T(8,128)S(1)} %get-tuple-element.45.coef, f32[81,2,24,128]{3,2,1,0:T(8,128)S(1)} %get-tuple-element.46.rolled, f32[24,2,24,128]{3,2,1,0:T(8,128)S(1)} %get-tuple-element.58.field), custom_call_target="tpu_custom_call" | custom-call | flops 1870000000 | bytes 6120000 | tf_op jit(solution)/shard_map/pallas_call | solution.py:44
  40.8 1.3 %shard_map.60 = (f32[24,2,24,128]{3,2,1,0:T(8,128)S(1)}, f32[352,128]{1,0:T(8,128)S(1)}, f32[352,128]{1,0:T(8,128)S(1)}) custom-call(f32[117,2,24,128]{3,2,1,0:T(8,128)S(1)} %get-tuple-element.45.coef, f32[81,2,24,128]{3,2,1,0:T(8,128)S(1)} %get-tuple-element.46.rolled, f32[6,2,24,128]{3,2,1,0:T(8,128)S(1)} %get-tuple-element.47.inverse, ...), custom_call_target="tpu_custom_call" | custom-call | flops 1430000000 | bytes 4680000 | tf_op jit(solution)/shard_map/pallas_call | solution.py:44
  42.1 3.0 %collective-permute-start.12 = (f32[352,128]{1,0:T(8,128)S(1)}, f32[352,128]{1,0:T(8,128)S(1)}, u32[]{:S(2)}, u32[]{:S(2)}) collective-permute-start(f32[352,128]{1,0:T(8,128)S(1)} %get-tuple-element.62), channel_id=1, source_target_pairs={{0,8},{16,24},{32,40},{48,56},{64,72},{80,88},{96,104},{112,120},{... | collective-permute-start | bytes 540680 | tf_op jit(solution)/shard_map/ppermute | solution.py:509
  45.2 1.7 %shard_map.61.part = f32[24,2,24,128]{3,2,1,0:T(8,128)S(1)} custom-call(f32[117,2,24,128]{3,2,1,0:T(8,128)S(1)} %get-tuple-element.45.coef, f32[81,2,24,128]{3,2,1,0:T(8,128)S(1)} %get-tuple-element.46.rolled, f32[24,2,24,128]{3,2,1,0:T(8,128)S(1)} %get-tuple-element.61.field), custom_call_target="tpu_custom_call" | custom-call | flops 1870000000 | bytes 6120000 | tf_op jit(solution)/shard_map/pallas_call | solution.py:44
  46.9 5.1 %collective-permute-done.13.other = f32[352,128]{1,0:T(8,128)S(1)} collective-permute-done((f32[352,128]{1,0:T(8,128)S(1)}, f32[352,128]{1,0:T(8,128)S(1)}, u32[]{:S(2)}, u32[]{:S(2)}) %collective-permute-start.13) | collective-permute-done | bytes 180256 | tf_op jit(solution)/shard_map/ppermute | solution.py:509
  52.0 0.7 %shard_map.62.field = f32[24,2,24,128]{3,2,1,0:T(8,128)S(1)} custom-call(f32[117,2,24,128]{3,2,1,0:T(8,128)S(1)} %get-tuple-element.45.coef, f32[81,2,24,128]{3,2,1,0:T(8,128)S(1)} %get-tuple-element.46.rolled, f32[6,2,24,128]{3,2,1,0:T(8,128)S(1)} %get-tuple-element.47.inverse, f32[24,2,24,128]{3,2,1,0:T(8,128)S(1)} %get-tuple-element.61.field, ...), custom_call_target="tpu_custom_call" | custom-call | flops 880000000 | bytes 2880000 | tf_op jit(solution)/shard_map/pallas_call | solution.py:44
  52.7 1.7 %shard_map.63.part = f32[24,2,24,128]{3,2,1,0:T(8,128)S(1)} custom-call(f32[117,2,24,128]{3,2,1,0:T(8,128)S(1)} %get-tuple-element.45.coef, f32[81,2,24,128]{3,2,1,0:T(8,128)S(1)} %get-tuple-element.46.rolled, f32[24,2,24,128]{3,2,1,0:T(8,128)S(1)} %shard_map.62.field), custom_call_target="tpu_custom_call" | custom-call | flops 1870000000 | bytes 6120000 | tf_op jit(solution)/shard_map/pallas_call | solution.py:44
  54.5 3.2 %collective-permute-start.14 = (f32[592,128]{1,0:T(8,128)S(1)}, f32[592,128]{1,0:T(8,128)S(1)}, u32[]{:S(2)}, u32[]{:S(2)}) collective-permute-start(f32[592,128]{1,0:T(8,128)S(1)} %get-tuple-element.65), channel_id=1, source_target_pairs={{0,8},{16,24},{32,40},{48,56},{64,72},{80,88},{96,104},{112,120},{... | collective-permute-start | bytes 909320 | tf_op jit(solution)/shard_map/ppermute | solution.py:509
  58.0 0.8 %shard_map.64.far_part = f32[24,2,24,128]{3,2,1,0:T(8,128)S(1)} custom-call(f32[117,2,24,128]{3,2,1,0:T(8,128)S(1)} %get-tuple-element.45.coef, f32[81,24,128]{2,1,0:T(8,128)S(1)} %get-tuple-element.50.far_coef, f32[54,24,128]{2,1,0:T(8,128)S(1)} %get-tuple-element.64.far_rolled, f32[24,2,24,128]{3,2,1,0:T(8,128)S(1)} %shard_map.62.field), custom_call_target="tpu_custom_call" | custom-call | flops 880000000 | bytes 2880000 | tf_op jit(solution)/shard_map/pallas_call | solution.py:44
  58.9 5.3 %collective-permute-done.15.other = f32[592,128]{1,0:T(8,128)S(1)} collective-permute-done((f32[592,128]{1,0:T(8,128)S(1)}, f32[592,128]{1,0:T(8,128)S(1)}, u32[]{:S(2)}, u32[]{:S(2)}) %collective-permute-start.15) | collective-permute-done | bytes 303136 | tf_op jit(solution)/shard_map/ppermute | solution.py:509
  64.3 1.4 %shard_map.67 = (f32[24,2,24,128]{3,2,1,0:T(8,128)S(1)}, f32[24,2,24,128]{3,2,1,0:T(8,128)S(1)}, f32[1,8,128]{2,1,0:T(8,128)S(1)}) custom-call(f32[117,2,24,128]{3,2,1,0:T(8,128)S(1)} %get-tuple-element.45.coef, f32[81,2,24,128]{3,2,1,0:T(8,128)S(1)} %get-tuple-element.46.rolled, f32[81,24,128]{2,1,0:T(8,128)S(1)} %get-tuple-element.50.far_coef, ...), custom_call_target="tpu_custom_call" | custom-call | flops 330000000 | bytes 1080000 | tf_op jit(solution)/shard_map/pallas_call | solution.py:44
  65.7 3.2 %shard_map.68 = (f32[8,3,2,8,128]{4,3,2,1,0:T(8,128)}, f32[8,8,1,4,63]{4,3,2,1,0:T(4,128)}) custom-call(f32[24,2,24,128]{3,2,1,0:T(8,128)S(1)} %get-tuple-element.67.field, f32[24,2,24,128]{3,2,1,0:T(8,128)S(1)} %get-tuple-element.68.far, f32[1,8,128]{2,1,0:T(8,128)S(1)} %shard_map.65.segs.seg, f32[1,8,128]{2,1,0:T(8,128)S(1)} %get-tuple-element.69.far_seg), custom_call_target="tpu_custom_call" | custom-call | flops 3300000000 | bytes 10800000 | tf_op jit(solution)/shard_map/pallas_call | solution.py:44
  (25 shorter events, 1.5 us)
Async XLA Ops:
  0.6 1.2 %copy-start = (f32[14,3,3,2,8,128]{5,4,3,2,1,0:T(8,128)S(1)}, f32[14,3,3,2,8,128]{5,4,3,2,1,0:T(8,128)}, u32[]{:S(2)}) copy-start(f32[14,3,3,2,8,128]{5,4,3,2,1,0:T(8,128)} %stencil.3) | copy-start | bytes 3096580
  1.8 0.9 %copy-start.1 = (f32[8,3,2,8,128]{4,3,2,1,0:T(8,128)S(1)}, f32[8,3,2,8,128]{4,3,2,1,0:T(8,128)}, u32[]{:S(2)}) copy-start(f32[8,3,2,8,128]{4,3,2,1,0:T(8,128)} %cands.1) | copy-start | bytes 589828
  3.1 8.0 %collective-permute-start = (f32[160,128]{1,0:T(8,128)S(1)}, f32[160,128]{1,0:T(8,128)S(1)}, u32[]{:S(2)}, u32[]{:S(2)}) collective-permute-start(f32[160,128]{1,0:T(8,128)S(1)} %get-tuple-element.37), channel_id=1, source_target_pairs={{1,0},{2,1},{3,2},{4,3},{5,4},{6,5},{7,6},{0,7},{9,8},{10,9},{11,1... | collective-permute-start | bytes 245768 | tf_op jit(solution)/shard_map/ppermute | solution.py:501
  9.6 4.5 %collective-permute-start.1 = (f32[160,128]{1,0:T(8,128)S(1)}, f32[160,128]{1,0:T(8,128)S(1)}, u32[]{:S(2)}, u32[]{:S(2)}) collective-permute-start(f32[160,128]{1,0:T(8,128)S(1)} %get-tuple-element.38), channel_id=1, source_target_pairs={{7,0},{0,1},{1,2},{2,3},{3,4},{4,5},{5,6},{6,7},{15,8},{8,9},{9,10... | collective-permute-start | bytes 245768 | tf_op jit(solution)/shard_map/ppermute | solution.py:501
  14.2 11.2 %collective-permute-start.2 = (f32[984,128]{1,0:T(8,128)S(1)}, f32[984,128]{1,0:T(8,128)S(1)}, u32[]{:S(2)}, u32[]{:S(2)}) collective-permute-start(f32[984,128]{1,0:T(8,128)S(1)} %get-tuple-element.39), channel_id=1, source_target_pairs={{1,0},{2,1},{3,2},{4,3},{5,4},{6,5},{7,6},{0,7},{9,8},{10,9},{11,1... | collective-permute-start | bytes 1511432 | tf_op jit(solution)/shard_map/ppermute | solution.py:501
  14.3 12.2 %collective-permute-start.3 = (f32[984,128]{1,0:T(8,128)S(1)}, f32[984,128]{1,0:T(8,128)S(1)}, u32[]{:S(2)}, u32[]{:S(2)}) collective-permute-start(f32[984,128]{1,0:T(8,128)S(1)} %get-tuple-element.40), channel_id=1, source_target_pairs={{7,0},{0,1},{1,2},{2,3},{3,4},{4,5},{5,6},{6,7},{15,8},{8,9},{9,10... | collective-permute-start | bytes 1511432 | tf_op jit(solution)/shard_map/ppermute | solution.py:501
  16.1 5.0 %collective-permute-start.6 = (f32[256,128]{1,0:T(8,128)S(1)}, f32[256,128]{1,0:T(8,128)S(1)}, u32[]{:S(2)}, u32[]{:S(2)}) collective-permute-start(f32[256,128]{1,0:T(8,128)S(1)} %get-tuple-element.53), channel_id=1, source_target_pairs={{0,8},{16,24},{32,40},{48,56},{64,72},{80,88},{96,104},{112,120},{... | collective-permute-start | bytes 393224 | tf_op jit(solution)/shard_map/ppermute | solution.py:509
  18.8 4.7 %collective-permute-start.7 = (f32[256,128]{1,0:T(8,128)S(1)}, f32[256,128]{1,0:T(8,128)S(1)}, u32[]{:S(2)}, u32[]{:S(2)}) collective-permute-start(f32[256,128]{1,0:T(8,128)S(1)} %get-tuple-element.54), channel_id=1, source_target_pairs={{8,16},{24,32},{40,48},{56,64},{72,80},{88,96},{104,112},{120,128}... | collective-permute-start | bytes 393224 | tf_op jit(solution)/shard_map/ppermute | solution.py:509
  20.1 3.4 %copy-start.2 = (s32[1,4,128]{2,1,0:T(4,128)S(1)}, s32[1,4,128]{2,1,0:T(4,128)}, u32[]{:S(2)}) copy-start(s32[1,4,128]{2,1,0:T(4,128)} %seg.3) | copy-start | bytes 6148
  23.9 5.0 %collective-permute-start.8 = (f32[200,128]{1,0:T(8,128)S(1)}, f32[200,128]{1,0:T(8,128)S(1)}, u32[]{:S(2)}, u32[]{:S(2)}) collective-permute-start(f32[200,128]{1,0:T(8,128)S(1)} %get-tuple-element.55), channel_id=1, source_target_pairs={{1,0},{2,1},{3,2},{4,3},{5,4},{6,5},{7,6},{0,7},{9,8},{10,9},{11,1... | collective-permute-start | bytes 307208 | tf_op jit(solution)/shard_map/ppermute | solution.py:501
  25.0 5.0 %collective-permute-start.9 = (f32[200,128]{1,0:T(8,128)S(1)}, f32[200,128]{1,0:T(8,128)S(1)}, u32[]{:S(2)}, u32[]{:S(2)}) collective-permute-start(f32[200,128]{1,0:T(8,128)S(1)} %get-tuple-element.56), channel_id=1, source_target_pairs={{7,0},{0,1},{1,2},{2,3},{3,4},{4,5},{5,6},{6,7},{15,8},{8,9},{9,10... | collective-permute-start | bytes 307208 | tf_op jit(solution)/shard_map/ppermute | solution.py:501
  30.6 10.2 %collective-permute-start.10 = (f32[400,128]{1,0:T(8,128)S(1)}, f32[400,128]{1,0:T(8,128)S(1)}, u32[]{:S(2)}, u32[]{:S(2)}) collective-permute-start(f32[400,128]{1,0:T(8,128)S(1)} %get-tuple-element.59), channel_id=1, source_target_pairs={{0,8},{16,24},{32,40},{48,56},{64,72},{80,88},{96,104},{112,120},{... | collective-permute-start | bytes 614408 | tf_op jit(solution)/shard_map/ppermute | solution.py:509
  35.1 5.7 %collective-permute-start.11 = (f32[400,128]{1,0:T(8,128)S(1)}, f32[400,128]{1,0:T(8,128)S(1)}, u32[]{:S(2)}, u32[]{:S(2)}) collective-permute-start(f32[400,128]{1,0:T(8,128)S(1)} %get-tuple-element.60), channel_id=1, source_target_pairs={{8,16},{24,32},{40,48},{56,64},{72,80},{88,96},{104,112},{120,128}... | collective-permute-start | bytes 614408 | tf_op jit(solution)/shard_map/ppermute | solution.py:509
  35.3 22.4 %collective-permute-start.4 = (f32[1392,128]{1,0:T(8,128)S(1)}, f32[1392,128]{1,0:T(8,128)S(1)}, u32[]{:S(2)}, u32[]{:S(2)}) collective-permute-start(f32[1392,128]{1,0:T(8,128)S(1)} %get-tuple-element.48), channel_id=1, source_target_pairs={{0,8},{16,24},{32,40},{48,56},{64,72},{80,88},{96,104},{112,120},{... | collective-permute-start | bytes 2138120 | tf_op jit(solution)/shard_map/ppermute | solution.py:509
  39.1 18.6 %collective-permute-start.5 = (f32[1392,128]{1,0:T(8,128)S(1)}, f32[1392,128]{1,0:T(8,128)S(1)}, u32[]{:S(2)}, u32[]{:S(2)}) collective-permute-start(f32[1392,128]{1,0:T(8,128)S(1)} %get-tuple-element.49), channel_id=1, source_target_pairs={{8,16},{24,32},{40,48},{56,64},{72,80},{88,96},{104,112},{120,128}... | collective-permute-start | bytes 2138120 | tf_op jit(solution)/shard_map/ppermute | solution.py:509
  42.1 4.7 %collective-permute-start.12 = (f32[352,128]{1,0:T(8,128)S(1)}, f32[352,128]{1,0:T(8,128)S(1)}, u32[]{:S(2)}, u32[]{:S(2)}) collective-permute-start(f32[352,128]{1,0:T(8,128)S(1)} %get-tuple-element.62), channel_id=1, source_target_pairs={{0,8},{16,24},{32,40},{48,56},{64,72},{80,88},{96,104},{112,120},{... | collective-permute-start | bytes 540680 | tf_op jit(solution)/shard_map/ppermute | solution.py:509
  45.2 6.8 %collective-permute-start.13 = (f32[352,128]{1,0:T(8,128)S(1)}, f32[352,128]{1,0:T(8,128)S(1)}, u32[]{:S(2)}, u32[]{:S(2)}) collective-permute-start(f32[352,128]{1,0:T(8,128)S(1)} %get-tuple-element.63), channel_id=1, source_target_pairs={{8,16},{24,32},{40,48},{56,64},{72,80},{88,96},{104,112},{120,128}... | collective-permute-start | bytes 540680 | tf_op jit(solution)/shard_map/ppermute | solution.py:509
  54.5 4.4 %collective-permute-start.14 = (f32[592,128]{1,0:T(8,128)S(1)}, f32[592,128]{1,0:T(8,128)S(1)}, u32[]{:S(2)}, u32[]{:S(2)}) collective-permute-start(f32[592,128]{1,0:T(8,128)S(1)} %get-tuple-element.65), channel_id=1, source_target_pairs={{0,8},{16,24},{32,40},{48,56},{64,72},{80,88},{96,104},{112,120},{... | collective-permute-start | bytes 909320 | tf_op jit(solution)/shard_map/ppermute | solution.py:509
  57.7 6.5 %collective-permute-start.15 = (f32[592,128]{1,0:T(8,128)S(1)}, f32[592,128]{1,0:T(8,128)S(1)}, u32[]{:S(2)}, u32[]{:S(2)}) collective-permute-start(f32[592,128]{1,0:T(8,128)S(1)} %get-tuple-element.66), channel_id=1, source_target_pairs={{8,16},{24,32},{40,48},{56,64},{72,80},{88,96},{104,112},{120,128}... | collective-permute-start | bytes 909320 | tf_op jit(solution)/shard_map/ppermute | solution.py:509

commit v3 on v2

--- a/solution.py
+++ b/solution.py
@@ -21,6 +21,9 @@
     if (sx, sy, sz) > (0, 0, 0)
 ]
 ROLLED = [j for j, o in enumerate(neighbour_steps) if o[2] != 0]
+FLAT = [j for j, o in enumerate(neighbour_steps) if o[0] == 0]
+STEP = [j for j, o in enumerate(neighbour_steps) if o[0] == 1]
+STEP_ROLLED = [j for j in STEP if j in ROLLED]
 SYM = [(0, 0), (0, 1), (0, 2), (1, 1), (1, 2), (2, 2)]
 SYM_OF = {(e, d): SYM.index((min(e, d), max(e, d))) for e in range(3) for d in range(3)}
 ROWS = 24
@@ -32,7 +35,6 @@
 ONE_UP = [j for j, o in enumerate(neighbour_steps) if o[1] == 1]
 RIM_S = 48
 RIM = 160
-HALO = 4 * 2 * (6 + 117)
 SEG_ROW = 4 * 48
 EDGE = SEG_ROW + 8
 PAD = 8
@@ -110,36 +112,48 @@
     return pltpu.roll(x, by % 128, x.ndim - 1)
 
 
-def pack_halo_kernel(stencil, inverse, _, _2, halo_dn, halo_up):
-    for i in range(6):
-        for p in range(2):
-            k = i * 2 + p
-            halo_dn[pl.ds(4 * k, 4), :] = inverse[i, p, pl.ds(8, 4), :]
-            halo_up[pl.ds(4 * k, 4), :] = inverse[i, p, pl.ds(12, 4), :]
-    for j in range(13):
-        for e in range(3):
-            for d in range(3):
-                for p in range(2):
-                    k = 12 + ((j * 3 + e) * 3 + d) * 2 + p
-                    halo_dn[pl.ds(4 * k, 4), :] = stencil[1 + j, e, d, p, 0:4]
-                    halo_up[pl.ds(4 * k, 4), :] = stencil[1 + j, e, d, p, 4:8]
-
-
-def halo_kernel(from_up, from_dn, coef_in, rolled_in, inverse_in, coef, rolled, inverse):
+HALO_A = [(j, n, 1) for j in STEP for n in range(9)]
+HALO_B = (
+    [(None, i, p) for i in range(6) for p in range(2)]
+    + [(j, n, p) for j in FLAT for n in range(9) for p in range(2)]
+    + [(j, n, 0) for j in STEP for n in range(9)]
+)
+
+
+def halo_shape(items):
+    return struct(-(-4 * len(items) // 8) * 8, 128)
+
+
+def pack_halo_kernel(items, stencil, inverse, halo_dn, halo_up):
+    for k, (j, n, p) in enumerate(items):
+        rows = pl.ds(4 * k, 4)
+        if j is None:
+            halo_dn[rows, :] = inverse[n, p, pl.ds(8, 4), :]
+            halo_up[rows, :] = inverse[n, p, pl.ds(12, 4), :]
+        else:
+            halo_dn[rows, :] = stencil[1 + j, n // 3, n % 3, p, 0:4]
+            halo_up[rows, :] = stencil[1 + j, n // 3, n % 3, p, 4:8]
+
+
+def halo_rows(items, from_up, from_dn, coef, rolled, inverse):
     for msg, four in ((from_up, 16), (from_dn, 4)):
-        for i in range(6):
-            for p in range(2):
-                inverse[i, p, pl.ds(four, 4), :] = msg[pl.ds(4 * (2 * i + p), 4), :]
-        for j in range(13):
-            for n in range(9):
-                k = 12 + (j * 9 + n) * 2
-                pair = msg[pl.ds(4 * k, 8), :]
-                coef[j * 9 + n, 0, pl.ds(four, 4), :] = pair[0:4]
-                coef[j * 9 + n, 1, pl.ds(four, 4), :] = pair[4:8]
-                if j in ROLLED:
-                    pair = roll_z(pair, neighbour_steps[j][2])
-                    rolled[ROLLED.index(j) * 9 + n, 0, pl.ds(four, 4), :] = pair[0:4]
-                    rolled[ROLLED.index(j) * 9 + n, 1, pl.ds(four, 4), :] = pair[4:8]
+        for k, (j, n, p) in enumerate(items):
+            block = msg[pl.ds(4 * k, 4), :]
+            if j is None:
+                inverse[n, p, pl.ds(four, 4), :] = block
+                continue
+            coef[j * 9 + n, p, pl.ds(four, 4), :] = block
+            if j in ROLLED:
+                at = ROLLED.index(j) * 9 + n
+                rolled[at, p, pl.ds(four, 4), :] = roll_z(block, neighbour_steps[j][2])
+
+
+def halo_a_kernel(from_up, from_dn, coef_in, rolled_in, coef, rolled):
+    halo_rows(HALO_A, from_up, from_dn, coef, rolled, None)
+
+
+def halo_b_kernel(from_up, from_dn, coef_in, rolled_in, inverse_in, _, coef, rolled, inverse):
+    halo_rows(HALO_B, from_up, from_dn, coef, rolled, inverse)
 
 
 def matrices(coef, rolled, far_coef=None, far_rolled=None):
@@ -194,9 +208,6 @@
     return out
 
 
-FLAT = [j for j, o in enumerate(neighbour_steps) if o[0] == 0]
-STEP = [j for j, o in enumerate(neighbour_steps) if o[0] == 1]
-STEP_ROLLED = [j for j in STEP if j in ROLLED]
 TERMS = [
     [(0, 0, j, t) for j in FLAT for t in (False, True)] + [(0, 1, j, False) for j in STEP],
     [(1, 1, j, t) for j in FLAT for t in (False, True)] + [(0, 0, j, True) for j in STEP],
@@ -291,10 +302,10 @@
 def pack_far_kernel(coef, inverse, same, other, box):
     right = parity()
     for i in range(81):
-        box[right, pl.ds(16 * i, 16), :] = coef[9 * STEP[0] + i, 1, pl.ds(4, 16), :]
+        box[right, pl.ds(TALL * i, TALL), :] = coef[9 * STEP[0] + i, 1, pl.ds(LO, TALL), :]
     for i in range(6):
-        box[right, pl.ds(16 * (81 + i), 16), :] = inverse[i, 1, pl.ds(4, 16), :]
-        box[1 - right, pl.ds(16 * (81 + i), 16), :] = inverse[i, 0, pl.ds(4, 16), :]
+        box[right, pl.ds(TALL * (81 + i), TALL), :] = inverse[i, 1, pl.ds(LO, TALL), :]
+        box[1 - right, pl.ds(TALL * (81 + i), TALL), :] = inverse[i, 0, pl.ds(LO, TALL), :]
     same[...] = box[0]
     other[...] = box[1]
 
@@ -303,16 +314,16 @@
     box[0] = same[...]
     box[1] = other[...]
     right = parity()
-    rows = pl.ds(4, 16)
+    rows = pl.ds(LO, TALL)
     for k, j in enumerate(STEP):
         for n in range(9):
-            block = box[1 - right, pl.ds(16 * (9 * k + n), 16), :]
+            block = box[1 - right, pl.ds(TALL * (9 * k + n), TALL), :]
             far_coef[9 * k + n, rows, :] = block
             if j in ROLLED:
                 far_rolled[9 * STEP_ROLLED.index(j) + n, rows, :] = roll_z(block, neighbour_steps[j][2])
     for i in range(6):
-        far_inverse[i, 0, rows, :] = box[1 - right, pl.ds(16 * (81 + i), 16), :]
-        far_inverse[i, 1, rows, :] = box[right, pl.ds(16 * (81 + i), 16), :]
+        far_inverse[i, 0, rows, :] = box[1 - right, pl.ds(TALL * (81 + i), TALL), :]
+        far_inverse[i, 1, rows, :] = box[right, pl.ds(TALL * (81 + i), TALL), :]
 
 
 def beyond_kernel(bases, coef, far_coef, far_rolled, field, far_part):
@@ -407,6 +418,7 @@
 ROUNDS = [((8,), 7, 17), ((4, 12), 4, 20), ((4, 12), 5, 19)]
 ALL = (4, 12)
 LO, HI = 6, 18
+TALL = HI - LO
 
 
 def sweep_first(coef, rolled, inverse, field, part, same, other, seg, new, to_dn, to_up, box):
@@ -435,21 +447,20 @@
 
 def qr_kernel(field, far, seg, far_seg, prolongator, coarse):
     lane = lax.broadcasted_iota(jnp.int32, (8, 128), 1)
-    even = lane % 2 == 0
     valid_row = lax.broadcasted_iota(jnp.int32, (8, 128), 0) < 5
     numbers = [far_seg[0], seg[0]]
-    joins_next = [(ids == roll_z(ids, -2)) & (lane < 126) for ids in numbers]
-    joins_prev = [(ids == roll_z(ids, 2)) & (lane >= 2) for ids in numbers]
+    joins = [
+        [(by, (ids == roll_z(ids, -by)) & (lane + by >= 0) & (lane + by < 128)) for by in (-3, -2, -1, 1, 2, 3)]
+        for ids in numbers
+    ]
 
     def dot(fx, a, b):
         parts = [x * y for x, y in zip(a, b)]
         while len(parts) > 1:
             parts = [x + y for x, y in zip(parts[::2], parts[1::2])] + parts[len(parts) // 2 * 2 :]
         x = parts[0]
-        x = x + jnp.where(even, roll_z(x, -1), roll_z(x, 1))
-        return x + (
-            jnp.where(joins_next[fx], roll_z(x, -2), 0.0) + jnp.where(joins_prev[fx], roll_z(x, 2), 0.0)
-        )
+        a, b, c, d, e, f = [jnp.where(mask, roll_z(x, -by), 0.0) for by, mask in joins[fx]]
+        return ((x + a) + (b + c)) + ((d + e) + f)
 
     ids = numbers[1]
     slot = lane.astype(F32)
@@ -533,28 +544,30 @@
         aliases={2: 0, 3: 1}, scratch=boxes[:1],
     )
     same, other = swapped(same, other)
-    halo_dn, halo_up = call(
-        pack_halo_kernel, [struct(HALO, 128)] * 2, stencil, inverse, rim_from_up, rim_from_dn, after=2
-    )
-    halo_from_up = moved(halo_dn, "gy", 1)
-    halo_from_dn = moved(halo_up, "gy", -1)
+    halo = []
+    for items in (HALO_A, HALO_B):
+        halo_dn, halo_up = call(
+            functools.partial(pack_halo_kernel, items), [halo_shape(items)] * 2, stencil, inverse, us=0.1
+        )
+        halo.append((moved(halo_dn, "gy", 1), moved(halo_up, "gy", -1)))
     part = local(0)
     field, to_dn, to_up = call(
-        sweep_first, [frame, edge, edge], coef, rolled, inverse, field, part, same, other, seg, scratch=boxes[:1]
+        sweep_first, [frame, edge, edge], coef, rolled, inverse, field, part, same, other, seg, scratch=boxes[:1], us=4
     )
     from_up = moved(to_dn, "gy", 1)
     from_dn = moved(to_up, "gy", -1)
     segs = call(segments_kernel, [struct(1, 8, 128)], seg, from_dn)[0]
+    coef, rolled = call(halo_a_kernel, operator[:2], *halo[0], coef, rolled, aliases={2: 0, 3: 1})
+    field, same, other = call(
+        second_kernel, [frame, sides[1], sides[1]], from_up, from_dn, coef, field,
+        aliases={3: 0}, scratch=boxes[1:2], us=3,
+    )
     coef, rolled, inverse = call(
-        halo_kernel, operator, halo_from_up, halo_from_dn, coef, rolled, inverse,
-        aliases={2: 0, 3: 1, 4: 2},
-    )
-    field, same, other = call(
-        second_kernel, [frame, sides[1], sides[1]], from_up, from_dn, coef, field, aliases={3: 0}, scratch=boxes[1:2], us=0.6
+        halo_b_kernel, operator, *halo[1], coef, rolled, inverse, field, aliases={2: 0, 3: 1, 4: 2}, after=1
     )
     same, other = swapped(same, other)
     part = local(1)
-    across = struct(16 * 87, 128)
+    across = struct(-(-TALL * 87 // 8) * 8, 128)
     across_box = pltpu.VMEM((2, *across.shape), F32)
     across_same, across_other = swapped(
         *call(pack_far_kernel, [across, across], coef, inverse, scratch=[across_box])

time: 69 us -> 66.1 us (0.958)
  waiting for transfers between devices: 21.8 us -> 17.5 us
  starting transfers between devices: 28.2 us -> 30.2 us
    ppermute x10, waiting for transfers between devices: 13 us -> 10.4 us  [swapped(): lax.ppermute(block, 'gx', two + [(j, i) for i, j in two])]
    ppermute x6 -> x8, starting transfers between devices: 9.56 us -> 11.6 us  [moved(): lax.ppermute(block, axis, [((i + by) % size, i) for i in range(size)])]
    ppermute x6 -> x8, waiting for transfers between devices: 8.76 us -> 7.14 us  [moved(): lax.ppermute(block, axis, [((i + by) % size, i) for i in range(size)])]
    pallas_call x19 -> x21, Pallas kernels: 15.9 us -> 15.3 us  [call(): pl.pallas_call(kernel, out_shape=out_shape, in_specs=[VMEM] * (len(args)...]
  transfers between devices with their start and end apart: 16 -> 18, of which waited for: 9 -> 8; matrix products, arithmetic and copies ran while one was open for 0% -> 0% of each run, Pallas kernels for 15% -> 15%
where the time goes in v3:
time: 66.1 us; the launch traced here: 65.9 us
  starting transfers between devices  30.2 us (46%)
  waiting for transfers between devices  17.5 us (26%)
  Pallas kernels  15.3 us (23%)
  local copies, waits for them, and re-layouts  2.14 us (3%)
  between operations  0.78 us (1%)
    ppermute x10, starting transfers between devices, swapped(): lax.ppermute(block, 'gx', two + [(j, i) for i, j in two])  18.6 us
    pallas_call x21, Pallas kernels, call(): pl.pallas_call(kernel, out_shape=out_shape, in_specs=[VMEM] * (len(args)...  15.3 us
    ppermute x8, starting transfers between devices, moved(): lax.ppermute(block, axis, [((i + by) % size, i) for i in range(size)])  11.6 us
    ppermute x10, waiting for transfers between devices, swapped(): lax.ppermute(block, 'gx', two + [(j, i) for i, j in two])  10.4 us
    ppermute x8, waiting for transfers between devices, moved(): lax.ppermute(block, axis, [((i + by) % size, i) for i in range(size)])  7.14 us
    unnamed x6, local copies, waits for them, and re-layouts  2.14 us
  transfers between devices with their start and end apart: 18, of which 8 were waited for; matrix products, arithmetic and copies ran while one was open for 0% of the time, Pallas kernels for 15%

profile of v3, /device:TPU:1, one launch (start us, length us, event | category | flops | bytes accessed | tf_op | source)
XLA Modules:
  0.0 65.9 jit_solution(3390487735323059380)
XLA Ops:
  0.6 1.2 %copy-done = f32[14,3,3,2,8,128]{5,4,3,2,1,0:T(8,128)S(1)} copy-done((f32[14,3,3,2,8,128]{5,4,3,2,1,0:T(8,128)S(1)}, f32[14,3,3,2,8,128]{5,4,3,2,1,0:T(8,128)}, u32[]{:S(2)}) %copy-start) | copy-done | bytes 1032216
  1.9 0.9 %copy-done.1 = f32[8,3,2,8,128]{4,3,2,1,0:T(8,128)S(1)} copy-done((f32[8,3,2,8,128]{4,3,2,1,0:T(8,128)S(1)}, f32[8,3,2,8,128]{4,3,2,1,0:T(8,128)}, u32[]{:S(2)}) %copy-start.1) | copy-done | bytes 196632
  3.1 6.5 %collective-permute-start.4 = (f32[160,128]{1,0:T(8,128)S(1)}, f32[160,128]{1,0:T(8,128)S(1)}, u32[]{:S(2)}, u32[]{:S(2)}) collective-permute-start(f32[160,128]{1,0:T(8,128)S(1)} %get-tuple-element.45), channel_id=1, source_target_pairs={{1,0},{2,1},{3,2},{4,3},{5,4},{6,5},{7,6},{0,7},{9,8},{10,9},{11,1... | collective-permute-start | bytes 245768 | tf_op jit(solution)/shard_map/ppermute | solution.py:512
  9.6 1.5 %collective-permute-done.4.from_up = f32[160,128]{1,0:T(8,128)S(1)} collective-permute-done((f32[160,128]{1,0:T(8,128)S(1)}, f32[160,128]{1,0:T(8,128)S(1)}, u32[]{:S(2)}, u32[]{:S(2)}) %collective-permute-start.4) | collective-permute-done | bytes 81952 | tf_op jit(solution)/shard_map/ppermute | solution.py:512
  11.0 3.0 %collective-permute-done.5.from_dn = f32[160,128]{1,0:T(8,128)S(1)} collective-permute-done((f32[160,128]{1,0:T(8,128)S(1)}, f32[160,128]{1,0:T(8,128)S(1)}, u32[]{:S(2)}, u32[]{:S(2)}) %collective-permute-start.5) | collective-permute-done | bytes 81952 | tf_op jit(solution)/shard_map/ppermute | solution.py:512
  14.4 2.2 %collective-permute-start.6 = (f32[256,128]{1,0:T(8,128)S(1)}, f32[256,128]{1,0:T(8,128)S(1)}, u32[]{:S(2)}, u32[]{:S(2)}) collective-permute-start(f32[256,128]{1,0:T(8,128)S(1)} %get-tuple-element.54), channel_id=1, source_target_pairs={{0,8},{16,24},{32,40},{48,56},{64,72},{80,88},{96,104},{112,120},{... | collective-permute-start | bytes 393224 | tf_op jit(solution)/shard_map/ppermute | solution.py:520
  16.5 1.3 %collective-permute-start.7 = (f32[256,128]{1,0:T(8,128)S(1)}, f32[256,128]{1,0:T(8,128)S(1)}, u32[]{:S(2)}, u32[]{:S(2)}) collective-permute-start(f32[256,128]{1,0:T(8,128)S(1)} %get-tuple-element.55), channel_id=1, source_target_pairs={{8,16},{24,32},{40,48},{56,64},{72,80},{88,96},{104,112},{120,128}... | collective-permute-start | bytes 393224 | tf_op jit(solution)/shard_map/ppermute | solution.py:520
  18.0 1.5 %collective-permute-start.3 = (f32[328,128]{1,0:T(8,128)S(1)}, f32[328,128]{1,0:T(8,128)S(1)}, u32[]{:S(2)}, u32[]{:S(2)}) collective-permute-start(f32[328,128]{1,0:T(8,128)S(1)} %get-tuple-element.44), channel_id=1, source_target_pairs={{7,0},{0,1},{1,2},{2,3},{3,4},{4,5},{5,6},{6,7},{15,8},{8,9},{9,10... | collective-permute-start | bytes 503816 | tf_op jit(solution)/shard_map/ppermute | solution.py:512
  19.4 0.9 %shard_map.55.part = f32[24,2,24,128]{3,2,1,0:T(8,128)S(1)} custom-call(f32[117,2,24,128]{3,2,1,0:T(8,128)S(1)} %get-tuple-element.49.coef_in.coef, f32[81,2,24,128]{3,2,1,0:T(8,128)S(1)} %get-tuple-element.50.rolled_in.rolled, f32[24,2,24,128]{3,2,1,0:T(8,128)S(1)} %get-tuple-element.53.field), custom_call_target="tpu_custom_call" | custom-call | flops 990000000 | bytes 3240000 | tf_op jit(solution)/shard_map/pallas_call | solution.py:46
  20.4 0.6 collective-permute-done.7.other
  20.9 0.3 shard_map.56
  21.3 0.8 %collective-permute-start.8 = (f32[200,128]{1,0:T(8,128)S(1)}, f32[200,128]{1,0:T(8,128)S(1)}, u32[]{:S(2)}, u32[]{:S(2)}) collective-permute-start(f32[200,128]{1,0:T(8,128)S(1)} %get-tuple-element.56), channel_id=1, source_target_pairs={{1,0},{2,1},{3,2},{4,3},{5,4},{6,5},{7,6},{0,7},{9,8},{10,9},{11,1... | collective-permute-start | bytes 307208 | tf_op jit(solution)/shard_map/ppermute | solution.py:512
  22.1 0.7 %collective-permute-start.9 = (f32[200,128]{1,0:T(8,128)S(1)}, f32[200,128]{1,0:T(8,128)S(1)}, u32[]{:S(2)}, u32[]{:S(2)}) collective-permute-start(f32[200,128]{1,0:T(8,128)S(1)} %get-tuple-element.57), channel_id=1, source_target_pairs={{7,0},{0,1},{1,2},{2,3},{3,4},{4,5},{5,6},{6,7},{15,8},{8,9},{9,10... | collective-permute-start | bytes 307208 | tf_op jit(solution)/shard_map/ppermute | solution.py:512
  22.9 2.0 %collective-permute-start = (f32[664,128]{1,0:T(8,128)S(1)}, f32[664,128]{1,0:T(8,128)S(1)}, u32[]{:S(2)}, u32[]{:S(2)}) collective-permute-start(f32[664,128]{1,0:T(8,128)S(1)} %get-tuple-element.41), channel_id=1, source_target_pairs={{1,0},{2,1},{3,2},{4,3},{5,4},{6,5},{7,6},{0,7},{9,8},{10,9},{11,1... | collective-permute-start | bytes 1019912 | tf_op jit(solution)/shard_map/ppermute | solution.py:512
  25.2 2.6 %collective-permute-done.9.from_dn = f32[200,128]{1,0:T(8,128)S(1)} collective-permute-done((f32[200,128]{1,0:T(8,128)S(1)}, f32[200,128]{1,0:T(8,128)S(1)}, u32[]{:S(2)}, u32[]{:S(2)}) %collective-permute-start.9) | collective-permute-done | bytes 102432 | tf_op jit(solution)/shard_map/ppermute | solution.py:512
  27.8 0.6 shard_map.57
  28.4 6.0 %collective-permute-start.12 = (f32[400,128]{1,0:T(8,128)S(1)}, f32[400,128]{1,0:T(8,128)S(1)}, u32[]{:S(2)}, u32[]{:S(2)}) collective-permute-start(f32[400,128]{1,0:T(8,128)S(1)} %get-tuple-element.67), channel_id=1, source_target_pairs={{0,8},{16,24},{32,40},{48,56},{64,72},{80,88},{96,104},{112,120},{... | collective-permute-start | bytes 614408 | tf_op jit(solution)/shard_map/ppermute | solution.py:520
  34.8 1.7 %shard_map.61.part = f32[24,2,24,128]{3,2,1,0:T(8,128)S(1)} custom-call(f32[117,2,24,128]{3,2,1,0:T(8,128)S(1)} %get-tuple-element.60.coef, f32[81,2,24,128]{3,2,1,0:T(8,128)S(1)} %get-tuple-element.61.rolled, f32[24,2,24,128]{3,2,1,0:T(8,128)S(1)} %get-tuple-element.59._.field), custom_call_target="tpu_custom_call" | custom-call | flops 1870000000 | bytes 6120000 | tf_op jit(solution)/shard_map/pallas_call | solution.py:46
  36.5 3.2 %collective-permute-done.13.other = f32[400,128]{1,0:T(8,128)S(1)} collective-permute-done((f32[400,128]{1,0:T(8,128)S(1)}, f32[400,128]{1,0:T(8,128)S(1)}, u32[]{:S(2)}, u32[]{:S(2)}) %collective-permute-start.13) | collective-permute-done | bytes 204832 | tf_op jit(solution)/shard_map/ppermute | solution.py:520
  39.6 1.3 %shard_map.62 = (f32[24,2,24,128]{3,2,1,0:T(8,128)S(1)}, f32[352,128]{1,0:T(8,128)S(1)}, f32[352,128]{1,0:T(8,128)S(1)}) custom-call(f32[117,2,24,128]{3,2,1,0:T(8,128)S(1)} %get-tuple-element.60.coef, f32[81,2,24,128]{3,2,1,0:T(8,128)S(1)} %get-tuple-element.61.rolled, f32[6,2,24,128]{3,2,1,0:T(8,128)S(1)} %get-tuple-element.62.inverse, ...), custom_call_target="tpu_custom_call" | custom-call | flops 1430000000 | bytes 4680000 | tf_op jit(solution)/shard_map/pallas_call | solution.py:46
  41.0 3.7 %collective-permute-start.14 = (f32[352,128]{1,0:T(8,128)S(1)}, f32[352,128]{1,0:T(8,128)S(1)}, u32[]{:S(2)}, u32[]{:S(2)}) collective-permute-start(f32[352,128]{1,0:T(8,128)S(1)} %get-tuple-element.70), channel_id=1, source_target_pairs={{0,8},{16,24},{32,40},{48,56},{64,72},{80,88},{96,104},{112,120},{... | collective-permute-start | bytes 540680 | tf_op jit(solution)/shard_map/ppermute | solution.py:520
  44.8 1.5 %collective-permute-start.10 = (f32[1048,128]{1,0:T(8,128)S(1)}, f32[1048,128]{1,0:T(8,128)S(1)}, u32[]{:S(2)}, u32[]{:S(2)}) collective-permute-start(f32[1048,128]{1,0:T(8,128)S(1)} %get-tuple-element.63), channel_id=1, source_target_pairs={{0,8},{16,24},{32,40},{48,56},{64,72},{80,88},{96,104},{112,120},{... | collective-permute-start | bytes 1609736 | tf_op jit(solution)/shard_map/ppermute | solution.py:520
  46.3 0.5 collective-permute-start.11
  46.7 1.7 %shard_map.63.part = f32[24,2,24,128]{3,2,1,0:T(8,128)S(1)} custom-call(f32[117,2,24,128]{3,2,1,0:T(8,128)S(1)} %get-tuple-element.60.coef, f32[81,2,24,128]{3,2,1,0:T(8,128)S(1)} %get-tuple-element.61.rolled, f32[24,2,24,128]{3,2,1,0:T(8,128)S(1)} %get-tuple-element.69.field), custom_call_target="tpu_custom_call" | custom-call | flops 1870000000 | bytes 6120000 | tf_op jit(solution)/shard_map/pallas_call | solution.py:46
  48.4 1.2 %collective-permute-done.15.other = f32[352,128]{1,0:T(8,128)S(1)} collective-permute-done((f32[352,128]{1,0:T(8,128)S(1)}, f32[352,128]{1,0:T(8,128)S(1)}, u32[]{:S(2)}, u32[]{:S(2)}) %collective-permute-start.15) | collective-permute-done | bytes 180256 | tf_op jit(solution)/shard_map/ppermute | solution.py:520
  49.6 0.7 %shard_map.64.field = f32[24,2,24,128]{3,2,1,0:T(8,128)S(1)} custom-call(f32[117,2,24,128]{3,2,1,0:T(8,128)S(1)} %get-tuple-element.60.coef, f32[81,2,24,128]{3,2,1,0:T(8,128)S(1)} %get-tuple-element.61.rolled, f32[6,2,24,128]{3,2,1,0:T(8,128)S(1)} %get-tuple-element.62.inverse, f32[24,2,24,128]{3,2,1,0:T(8,128)S(1)} %get-tuple-element.69.field, ...), custom_call_target="tpu_custom_call" | custom-call | flops 880000000 | bytes 2880000 | tf_op jit(solution)/shard_map/pallas_call | solution.py:46
  50.3 1.7 %shard_map.65.part = f32[24,2,24,128]{3,2,1,0:T(8,128)S(1)} custom-call(f32[117,2,24,128]{3,2,1,0:T(8,128)S(1)} %get-tuple-element.60.coef, f32[81,2,24,128]{3,2,1,0:T(8,128)S(1)} %get-tuple-element.61.rolled, f32[24,2,24,128]{3,2,1,0:T(8,128)S(1)} %shard_map.64.field), custom_call_target="tpu_custom_call" | custom-call | flops 1870000000 | bytes 6120000 | tf_op jit(solution)/shard_map/pallas_call | solution.py:46
  52.1 3.5 %collective-permute-start.16 = (f32[592,128]{1,0:T(8,128)S(1)}, f32[592,128]{1,0:T(8,128)S(1)}, u32[]{:S(2)}, u32[]{:S(2)}) collective-permute-start(f32[592,128]{1,0:T(8,128)S(1)} %get-tuple-element.73), channel_id=1, source_target_pairs={{0,8},{16,24},{32,40},{48,56},{64,72},{80,88},{96,104},{112,120},{... | collective-permute-start | bytes 909320 | tf_op jit(solution)/shard_map/ppermute | solution.py:520
  55.9 0.8 %shard_map.66.far_part = f32[24,2,24,128]{3,2,1,0:T(8,128)S(1)} custom-call(f32[117,2,24,128]{3,2,1,0:T(8,128)S(1)} %get-tuple-element.60.coef, f32[81,24,128]{2,1,0:T(8,128)S(1)} %get-tuple-element.65.far_coef, f32[54,24,128]{2,1,0:T(8,128)S(1)} %get-tuple-element.72.far_rolled, f32[24,2,24,128]{3,2,1,0:T(8,128)S(1)} %shard_map.64.field), custom_call_target="tpu_custom_call" | custom-call | flops 880000000 | bytes 2880000 | tf_op jit(solution)/shard_map/pallas_call | solution.py:46
  56.9 5.3 %collective-permute-done.17.other = f32[592,128]{1,0:T(8,128)S(1)} collective-permute-done((f32[592,128]{1,0:T(8,128)S(1)}, f32[592,128]{1,0:T(8,128)S(1)}, u32[]{:S(2)}, u32[]{:S(2)}) %collective-permute-start.17) | collective-permute-done | bytes 303136 | tf_op jit(solution)/shard_map/ppermute | solution.py:520
  62.2 1.4 %shard_map.69 = (f32[24,2,24,128]{3,2,1,0:T(8,128)S(1)}, f32[24,2,24,128]{3,2,1,0:T(8,128)S(1)}, f32[1,8,128]{2,1,0:T(8,128)S(1)}) custom-call(f32[117,2,24,128]{3,2,1,0:T(8,128)S(1)} %get-tuple-element.60.coef, f32[81,2,24,128]{3,2,1,0:T(8,128)S(1)} %get-tuple-element.61.rolled, f32[81,24,128]{2,1,0:T(8,128)S(1)} %get-tuple-element.65.far_coef, ...), custom_call_target="tpu_custom_call" | custom-call | flops 330000000 | bytes 1080000 | tf_op jit(solution)/shard_map/pallas_call | solution.py:46
  63.6 2.3 %shard_map.70 = (f32[8,3,2,8,128]{4,3,2,1,0:T(8,128)}, f32[8,8,1,4,63]{4,3,2,1,0:T(4,128)}) custom-call(f32[24,2,24,128]{3,2,1,0:T(8,128)S(1)} %get-tuple-element.75.field, f32[24,2,24,128]{3,2,1,0:T(8,128)S(1)} %get-tuple-element.76.far, f32[1,8,128]{2,1,0:T(8,128)S(1)} %shard_map.67.segs.seg, f32[1,8,128]{2,1,0:T(8,128)S(1)} %get-tuple-element.77.far_seg), custom_call_target="tpu_custom_call" | custom-call | flops 3300000000 | bytes 10800000 | tf_op jit(solution)/shard_map/pallas_call | solution.py:46
  (31 shorter events, 2.0 us)
Async XLA Ops:
  0.6 1.2 %copy-start = (f32[14,3,3,2,8,128]{5,4,3,2,1,0:T(8,128)S(1)}, f32[14,3,3,2,8,128]{5,4,3,2,1,0:T(8,128)}, u32[]{:S(2)}) copy-start(f32[14,3,3,2,8,128]{5,4,3,2,1,0:T(8,128)} %stencil.5) | copy-start | bytes 3096580
  1.8 0.9 %copy-start.1 = (f32[8,3,2,8,128]{4,3,2,1,0:T(8,128)S(1)}, f32[8,3,2,8,128]{4,3,2,1,0:T(8,128)}, u32[]{:S(2)}) copy-start(f32[8,3,2,8,128]{4,3,2,1,0:T(8,128)} %cands.1) | copy-start | bytes 589828
  3.1 8.0 %collective-permute-start.4 = (f32[160,128]{1,0:T(8,128)S(1)}, f32[160,128]{1,0:T(8,128)S(1)}, u32[]{:S(2)}, u32[]{:S(2)}) collective-permute-start(f32[160,128]{1,0:T(8,128)S(1)} %get-tuple-element.45), channel_id=1, source_target_pairs={{1,0},{2,1},{3,2},{4,3},{5,4},{6,5},{7,6},{0,7},{9,8},{10,9},{11,1... | collective-permute-start | bytes 245768 | tf_op jit(solution)/shard_map/ppermute | solution.py:512
  9.6 4.5 %collective-permute-start.5 = (f32[160,128]{1,0:T(8,128)S(1)}, f32[160,128]{1,0:T(8,128)S(1)}, u32[]{:S(2)}, u32[]{:S(2)}) collective-permute-start(f32[160,128]{1,0:T(8,128)S(1)} %get-tuple-element.46), channel_id=1, source_target_pairs={{7,0},{0,1},{1,2},{2,3},{3,4},{4,5},{5,6},{6,7},{15,8},{8,9},{9,10... | collective-permute-start | bytes 245768 | tf_op jit(solution)/shard_map/ppermute | solution.py:512
  14.4 6.0 %collective-permute-start.6 = (f32[256,128]{1,0:T(8,128)S(1)}, f32[256,128]{1,0:T(8,128)S(1)}, u32[]{:S(2)}, u32[]{:S(2)}) collective-permute-start(f32[256,128]{1,0:T(8,128)S(1)} %get-tuple-element.54), channel_id=1, source_target_pairs={{0,8},{16,24},{32,40},{48,56},{64,72},{80,88},{96,104},{112,120},{... | collective-permute-start | bytes 393224 | tf_op jit(solution)/shard_map/ppermute | solution.py:520
  16.5 4.4 %collective-permute-start.7 = (f32[256,128]{1,0:T(8,128)S(1)}, f32[256,128]{1,0:T(8,128)S(1)}, u32[]{:S(2)}, u32[]{:S(2)}) collective-permute-start(f32[256,128]{1,0:T(8,128)S(1)} %get-tuple-element.55), channel_id=1, source_target_pairs={{8,16},{24,32},{40,48},{56,64},{72,80},{88,96},{104,112},{120,128}... | collective-permute-start | bytes 393224 | tf_op jit(solution)/shard_map/ppermute | solution.py:520
  17.9 7.1 %collective-permute-start.2 = (f32[328,128]{1,0:T(8,128)S(1)}, f32[328,128]{1,0:T(8,128)S(1)}, u32[]{:S(2)}, u32[]{:S(2)}) collective-permute-start(f32[328,128]{1,0:T(8,128)S(1)} %get-tuple-element.43), channel_id=1, source_target_pairs={{1,0},{2,1},{3,2},{4,3},{5,4},{6,5},{7,6},{0,7},{9,8},{10,9},{11,1... | collective-permute-start | bytes 503816 | tf_op jit(solution)/shard_map/ppermute | solution.py:512
  18.0 7.0 %collective-permute-start.3 = (f32[328,128]{1,0:T(8,128)S(1)}, f32[328,128]{1,0:T(8,128)S(1)}, u32[]{:S(2)}, u32[]{:S(2)}) collective-permute-start(f32[328,128]{1,0:T(8,128)S(1)} %get-tuple-element.44), channel_id=1, source_target_pairs={{7,0},{0,1},{1,2},{2,3},{3,4},{4,5},{5,6},{6,7},{15,8},{8,9},{9,10... | collective-permute-start | bytes 503816 | tf_op jit(solution)/shard_map/ppermute | solution.py:512
  19.4 1.5 %copy-start.2 = (s32[1,4,128]{2,1,0:T(4,128)S(1)}, s32[1,4,128]{2,1,0:T(4,128)}, u32[]{:S(2)}) copy-start(s32[1,4,128]{2,1,0:T(4,128)} %seg.3) | copy-start | bytes 6148
  21.3 3.9 %collective-permute-start.8 = (f32[200,128]{1,0:T(8,128)S(1)}, f32[200,128]{1,0:T(8,128)S(1)}, u32[]{:S(2)}, u32[]{:S(2)}) collective-permute-start(f32[200,128]{1,0:T(8,128)S(1)} %get-tuple-element.56), channel_id=1, source_target_pairs={{1,0},{2,1},{3,2},{4,3},{5,4},{6,5},{7,6},{0,7},{9,8},{10,9},{11,1... | collective-permute-start | bytes 307208 | tf_op jit(solution)/shard_map/ppermute | solution.py:512
  22.1 5.7 %collective-permute-start.9 = (f32[200,128]{1,0:T(8,128)S(1)}, f32[200,128]{1,0:T(8,128)S(1)}, u32[]{:S(2)}, u32[]{:S(2)}) collective-permute-start(f32[200,128]{1,0:T(8,128)S(1)} %get-tuple-element.57), channel_id=1, source_target_pairs={{7,0},{0,1},{1,2},{2,3},{3,4},{4,5},{5,6},{6,7},{15,8},{8,9},{9,10... | collective-permute-start | bytes 307208 | tf_op jit(solution)/shard_map/ppermute | solution.py:512
  22.9 11.5 %collective-permute-start = (f32[664,128]{1,0:T(8,128)S(1)}, f32[664,128]{1,0:T(8,128)S(1)}, u32[]{:S(2)}, u32[]{:S(2)}) collective-permute-start(f32[664,128]{1,0:T(8,128)S(1)} %get-tuple-element.41), channel_id=1, source_target_pairs={{1,0},{2,1},{3,2},{4,3},{5,4},{6,5},{7,6},{0,7},{9,8},{10,9},{11,1... | collective-permute-start | bytes 1019912 | tf_op jit(solution)/shard_map/ppermute | solution.py:512
  25.0 9.5 %collective-permute-start.1 = (f32[664,128]{1,0:T(8,128)S(1)}, f32[664,128]{1,0:T(8,128)S(1)}, u32[]{:S(2)}, u32[]{:S(2)}) collective-permute-start(f32[664,128]{1,0:T(8,128)S(1)} %get-tuple-element.42), channel_id=1, source_target_pairs={{7,0},{0,1},{1,2},{2,3},{3,4},{4,5},{5,6},{6,7},{15,8},{8,9},{9,10... | collective-permute-start | bytes 1019912 | tf_op jit(solution)/shard_map/ppermute | solution.py:512
  28.4 8.0 %collective-permute-start.12 = (f32[400,128]{1,0:T(8,128)S(1)}, f32[400,128]{1,0:T(8,128)S(1)}, u32[]{:S(2)}, u32[]{:S(2)}) collective-permute-start(f32[400,128]{1,0:T(8,128)S(1)} %get-tuple-element.67), channel_id=1, source_target_pairs={{0,8},{16,24},{32,40},{48,56},{64,72},{80,88},{96,104},{112,120},{... | collective-permute-start | bytes 614408 | tf_op jit(solution)/shard_map/ppermute | solution.py:520
  34.4 5.2 %collective-permute-start.13 = (f32[400,128]{1,0:T(8,128)S(1)}, f32[400,128]{1,0:T(8,128)S(1)}, u32[]{:S(2)}, u32[]{:S(2)}) collective-permute-start(f32[400,128]{1,0:T(8,128)S(1)} %get-tuple-element.68), channel_id=1, source_target_pairs={{8,16},{24,32},{40,48},{56,64},{72,80},{88,96},{104,112},{120,128}... | collective-permute-start | bytes 614408 | tf_op jit(solution)/shard_map/ppermute | solution.py:520
  41.0 7.4 %collective-permute-start.14 = (f32[352,128]{1,0:T(8,128)S(1)}, f32[352,128]{1,0:T(8,128)S(1)}, u32[]{:S(2)}, u32[]{:S(2)}) collective-permute-start(f32[352,128]{1,0:T(8,128)S(1)} %get-tuple-element.70), channel_id=1, source_target_pairs={{0,8},{16,24},{32,40},{48,56},{64,72},{80,88},{96,104},{112,120},{... | collective-permute-start | bytes 540680 | tf_op jit(solution)/shard_map/ppermute | solution.py:520
  44.7 4.9 %collective-permute-start.15 = (f32[352,128]{1,0:T(8,128)S(1)}, f32[352,128]{1,0:T(8,128)S(1)}, u32[]{:S(2)}, u32[]{:S(2)}) collective-permute-start(f32[352,128]{1,0:T(8,128)S(1)} %get-tuple-element.71), channel_id=1, source_target_pairs={{8,16},{24,32},{40,48},{56,64},{72,80},{88,96},{104,112},{120,128}... | collective-permute-start | bytes 540680 | tf_op jit(solution)/shard_map/ppermute | solution.py:520
  44.8 10.8 %collective-permute-start.10 = (f32[1048,128]{1,0:T(8,128)S(1)}, f32[1048,128]{1,0:T(8,128)S(1)}, u32[]{:S(2)}, u32[]{:S(2)}) collective-permute-start(f32[1048,128]{1,0:T(8,128)S(1)} %get-tuple-element.63), channel_id=1, source_target_pairs={{0,8},{16,24},{32,40},{48,56},{64,72},{80,88},{96,104},{112,120},{... | collective-permute-start | bytes 1609736 | tf_op jit(solution)/shard_map/ppermute | solution.py:520
  46.3 9.4 %collective-permute-start.11 = (f32[1048,128]{1,0:T(8,128)S(1)}, f32[1048,128]{1,0:T(8,128)S(1)}, u32[]{:S(2)}, u32[]{:S(2)}) collective-permute-start(f32[1048,128]{1,0:T(8,128)S(1)} %get-tuple-element.64), channel_id=1, source_target_pairs={{8,16},{24,32},{40,48},{56,64},{72,80},{88,96},{104,112},{120,128}... | collective-permute-start | bytes 1609736 | tf_op jit(solution)/shard_map/ppermute | solution.py:520
  52.1 4.7 %collective-permute-start.16 = (f32[592,128]{1,0:T(8,128)S(1)}, f32[592,128]{1,0:T(8,128)S(1)}, u32[]{:S(2)}, u32[]{:S(2)}) collective-permute-start(f32[592,128]{1,0:T(8,128)S(1)} %get-tuple-element.73), channel_id=1, source_target_pairs={{0,8},{16,24},{32,40},{48,56},{64,72},{80,88},{96,104},{112,120},{... | collective-permute-start | bytes 909320 | tf_op jit(solution)/shard_map/ppermute | solution.py:520
  55.6 6.5 %collective-permute-start.17 = (f32[592,128]{1,0:T(8,128)S(1)}, f32[592,128]{1,0:T(8,128)S(1)}, u32[]{:S(2)}, u32[]{:S(2)}) collective-permute-start(f32[592,128]{1,0:T(8,128)S(1)} %get-tuple-element.74), channel_id=1, source_target_pairs={{8,16},{24,32},{40,48},{56,64},{72,80},{88,96},{104,112},{120,128}... | collective-permute-start | bytes 909320 | tf_op jit(solution)/shard_map/ppermute | solution.py:520

commit v4 on v3

--- a/solution.py
+++ b/solution.py
@@ -38,6 +38,8 @@
 SEG_ROW = 4 * 48
 EDGE = SEG_ROW + 8
 PAD = 8
+LO, HI = 6, 18
+TALL = HI - LO
 FLOPS_PER_US = 1.1e9
 BYTES_PER_US = 3.6e6
 
@@ -222,17 +224,21 @@
     return lambda i, plane, row: field[i, plane, pl.ds(row, 8), :]
 
 
-def tiles(bases, step):
+def tiles(bases, step, unrolled=2):
     if len(bases) == 1:
         for half in range(2):
             step(bases[0], half)
         return
 
     def one(i, carry):
-        step(bases[0] + (i // 2) * 8, i % 2)
+        if unrolled == 2:
+            step(bases[0] + i * 8, 0)
+            step(bases[0] + i * 8, 1)
+        else:
+            step(bases[0] + (i // 2) * 8, i % 2)
         return carry
 
-    lax.fori_loop(0, 2 * len(bases), one, 0)
+    lax.fori_loop(0, 2 * len(bases) // unrolled, one, 0)
 
 
 def side_rows(lo, hi, items):
@@ -288,12 +294,20 @@
     send(coef, field, box, same, other, *ROUNDS[1])
 
 
-def both_kernel(lo, hi, field, part, segs, same, other, box):
+SUMS = PAD + 24 * TALL
+BOTH = SUMS + 24 * (TALL - 2) + PAD
+
+
+def sum_spot(i, row):
+    return SUMS + i * (TALL - 2) + row - LO - 1
+
+
+def both_kernel(field, part, segs, same, other, box):
     right = parity()
     for plane, slot in ((1, right), (0, 1 - right)):
         for i in range(24):
-            for n, ref in ((i, field), (24 + i, part)):
-                box[slot, pl.ds(spot(n, lo, lo, hi), hi - lo), :] = ref[i, plane, pl.ds(lo, hi - lo), :]
+            box[slot, pl.ds(spot(i, LO, LO, HI), TALL), :] = field[i, plane, pl.ds(LO, TALL), :]
+            box[slot, pl.ds(sum_spot(i, LO + 1), TALL - 2), :] = part[i, plane, pl.ds(LO + 1, TALL - 2), :]
     box[right, pl.ds(0, 8), :] = segs[0]
     same[...] = box[0]
     other[...] = box[1]
@@ -348,7 +362,7 @@
     return out
 
 
-def four_kernel(lo, hi, bases, coef, rolled, far_coef, inverse, far_inverse, field, part, far_part, same, other, new, far, far_seg, box):
+def four_kernel(bases, coef, rolled, far_coef, inverse, far_inverse, field, part, far_part, same, other, new, far, far_seg, box):
     box[0] = same[...]
     box[1] = other[...]
     right = parity()
@@ -356,11 +370,11 @@
 
     far_seg[0] = box[1 - right, pl.ds(0, 8), :]
 
-    def message(side, i, row):
-        return box[right if side else 1 - right, pl.ds(spot(i, row, lo, hi), 8), :]
+    def message(side, at):
+        return box[right if side else 1 - right, pl.ds(at, 8), :]
 
     def load(i, plane, row):
-        return message(plane == 2, i, row)
+        return message(plane == 2, spot(i, row, LO, HI))
 
     def step(base, half):
         here = pl.ds(base, 8)
@@ -372,8 +386,8 @@
                 out = relax(inverse, p, base, [field[at + e, p, here, :] for e in range(3)], res)
                 for e in range(3):
                     new[at + e, p, here, :] = out[e]
-                res = [message(p, 24 + at + e, base) + far_part[at + e, p, here, :] for e in range(3)]
-                out = relax(far_inverse, p, base, [message(p, at + e, base) for e in range(3)], res)
+                res = [message(p, sum_spot(at + e, base)) + far_part[at + e, p, here, :] for e in range(3)]
+                out = relax(far_inverse, p, base, [load(at + e, 2 if p else -1, base) for e in range(3)], res)
                 for e in range(3):
                     far[at + e, p, here, :] = out[e]
 
@@ -388,7 +402,7 @@
                 for e in range(3):
                     part[(half * 4 + c) * 3 + e, p, pl.ds(base, 8), :] = got[c][e]
 
-    tiles(bases, step)
+    tiles(bases, step, 1)
 
 
 def finish(coef, rolled, inverse, field, part, same, other, box, new, bases, lo, hi):
@@ -417,8 +431,6 @@
 
 ROUNDS = [((8,), 7, 17), ((4, 12), 4, 20), ((4, 12), 5, 19)]
 ALL = (4, 12)
-LO, HI = 6, 18
-TALL = HI - LO
 
 
 def sweep_first(coef, rolled, inverse, field, part, same, other, seg, new, to_dn, to_up, box):
@@ -454,13 +466,19 @@
         for ids in numbers
     ]
 
+    def tree(op, parts):
+        while len(parts) > 1:
+            parts = [op(x, y) for x, y in zip(parts[::2], parts[1::2])] + parts[len(parts) // 2 * 2 :]
+        return parts[0]
+
+    def over_z(fx, op, x):
+        return tree(op, [x] + [jnp.where(mask, roll_z(x, -by), 0.0) for by, mask in joins[fx]])
+
     def dot(fx, a, b):
-        parts = [x * y for x, y in zip(a, b)]
-        while len(parts) > 1:
-            parts = [x + y for x, y in zip(parts[::2], parts[1::2])] + parts[len(parts) // 2 * 2 :]
-        x = parts[0]
-        a, b, c, d, e, f = [jnp.where(mask, roll_z(x, -by), 0.0) for by, mask in joins[fx]]
-        return ((x + a) + (b + c)) + ((d + e) + f)
+        return over_z(fx, jnp.add, tree(jnp.add, [x * y for x, y in zip(a, b)]))
+
+    def largest(fx, a):
+        return over_z(fx, jnp.maximum, tree(jnp.maximum, [jnp.abs(x) for x in a]))
 
     ids = numbers[1]
     slot = lane.astype(F32)
@@ -487,19 +505,23 @@
                 for i in range(K)
             ]
         )
+    tops = [largest(fx, cols[fx][0]) for fx in range(2)]
     for k in range(K):
-        squares = [dot(fx, cols[fx][k], cols[fx][k]) for fx in range(2)]
+        near = [[x * (0.125 / tops[fx]) for x in cols[fx][k]] for fx in range(2)]
+        squares = [dot(fx, near[fx], near[fx]) for fx in range(2)]
+        products = {(fx, j): dot(fx, near[fx], cols[fx][j]) for j in range(k + 1, K) for fx in range(2)}
+        put(k, k, jnp.sqrt(squares[1]) * 8.0 * tops[1])
+        if k < K - 1:
+            tops = [largest(fx, cols[fx][k + 1]) for fx in range(2)]
         for fx in range(2):
             scale = lax.rsqrt(squares[fx])
-            cols[fx][k] = [x * scale for x in cols[fx][k]]
-        for j in range(k + 1, K):
-            for fx in range(2):
-                r = dot(fx, cols[fx][k], cols[fx][j])
+            cols[fx][k] = [x * scale for x in near[fx]]
+            for j in range(k + 1, K):
+                r = products[fx, j] * scale
                 cols[fx][j] = [x - r * y for x, y in zip(cols[fx][j], cols[fx][k])]
                 if fx == 1:
                     put(k, j, r)
                     coarse[j, k, 0] = jnp.zeros((4, NSEG), F32)
-        put(k, k, jnp.sqrt(squares[1]))
         for fx in range(2):
             at = 6 * (1 - fx)
             for d in range(3):
@@ -586,16 +608,16 @@
         sweep_third, [frame], coef, rolled, inverse, field, part, same, other, scratch=boxes[2:], us=0.8
     )[0]
     part = local(3)
-    side = struct(side_rows(LO, HI, 48), 128)
+    side = struct(BOTH, 128)
     box = pltpu.VMEM((2, *side.shape), F32)
     same, other = swapped(
-        *call(functools.partial(both_kernel, LO, HI), [side, side], field, part, segs, scratch=[box])
+        *call(both_kernel, [side, side], field, part, segs, scratch=[box])
     )
     far_part = call(
         functools.partial(beyond_kernel, ALL), [frame], coef, far_coef, far_rolled, field, us=0.8
     )[0]
     field, far, far_seg = call(
-        functools.partial(four_kernel, LO, HI, ALL), [frame, frame, struct(1, 8, 128)],
+        functools.partial(four_kernel, ALL), [frame, frame, struct(1, 8, 128)],
         coef, rolled, far_coef, inverse, far_inverse, field, part, far_part, same, other, scratch=[box],
     )
     prolongator, coarse = call(

time: 66.1 us -> 64.5 us (0.976)
  Pallas kernels: 15.3 us -> 14 us
    pallas_call x21, Pallas kernels: 15.3 us -> 14 us  [call(): pl.pallas_call(kernel, out_shape=out_shape, in_specs=[VMEM] * (len(args)...]
  transfers between devices with their start and end apart: 18 -> 18, of which waited for: 8 -> 8; matrix products, arithmetic and copies ran while one was open for 0% -> 0% of each run, Pallas kernels for 15% -> 14%
where the time goes in v4:
time: 64.5 us; the launch traced here: 64.4 us
  starting transfers between devices  30.2 us (47%)
  waiting for transfers between devices  17.3 us (27%)
  Pallas kernels  14 us (22%)
  local copies, waits for them, and re-layouts  2.14 us (3%)
  between operations  0.79 us (1%)
    ppermute x10, starting transfers between devices, swapped(): lax.ppermute(block, 'gx', two + [(j, i) for i, j in two])  18.6 us
    pallas_call x21, Pallas kernels, call(): pl.pallas_call(kernel, out_shape=out_shape, in_specs=[VMEM] * (len(args)...  14 us
    ppermute x8, starting transfers between devices, moved(): lax.ppermute(block, axis, [((i + by) % size, i) for i in range(size)])  11.6 us
    ppermute x10, waiting for transfers between devices, swapped(): lax.ppermute(block, 'gx', two + [(j, i) for i, j in two])  10.1 us
    ppermute x8, waiting for transfers between devices, moved(): lax.ppermute(block, axis, [((i + by) % size, i) for i in range(size)])  7.14 us
    unnamed x6, local copies, waits for them, and re-layouts  2.14 us
  transfers between devices with their start and end apart: 18, of which 8 were waited for; matrix products, arithmetic and copies ran while one was open for 0% of the time, Pallas kernels for 14%

profile of v4, /device:TPU:1, one launch (start us, length us, event | category | flops | bytes accessed | tf_op | source)
XLA Modules:
  0.0 64.4 jit_solution(1144174649283482229)
XLA Ops:
  0.6 1.2 %copy-done = f32[14,3,3,2,8,128]{5,4,3,2,1,0:T(8,128)S(1)} copy-done((f32[14,3,3,2,8,128]{5,4,3,2,1,0:T(8,128)S(1)}, f32[14,3,3,2,8,128]{5,4,3,2,1,0:T(8,128)}, u32[]{:S(2)}) %copy-start) | copy-done | bytes 1032216
  1.9 0.9 %copy-done.1 = f32[8,3,2,8,128]{4,3,2,1,0:T(8,128)S(1)} copy-done((f32[8,3,2,8,128]{4,3,2,1,0:T(8,128)S(1)}, f32[8,3,2,8,128]{4,3,2,1,0:T(8,128)}, u32[]{:S(2)}) %copy-start.1) | copy-done | bytes 196632
  3.1 6.5 %collective-permute-start.4 = (f32[160,128]{1,0:T(8,128)S(1)}, f32[160,128]{1,0:T(8,128)S(1)}, u32[]{:S(2)}, u32[]{:S(2)}) collective-permute-start(f32[160,128]{1,0:T(8,128)S(1)} %get-tuple-element.45), channel_id=1, source_target_pairs={{1,0},{2,1},{3,2},{4,3},{5,4},{6,5},{7,6},{0,7},{9,8},{10,9},{11,1... | collective-permute-start | bytes 245768 | tf_op jit(solution)/shard_map/ppermute | solution.py:534
  9.6 1.5 %collective-permute-done.4.from_up = f32[160,128]{1,0:T(8,128)S(1)} collective-permute-done((f32[160,128]{1,0:T(8,128)S(1)}, f32[160,128]{1,0:T(8,128)S(1)}, u32[]{:S(2)}, u32[]{:S(2)}) %collective-permute-start.4) | collective-permute-done | bytes 81952 | tf_op jit(solution)/shard_map/ppermute | solution.py:534
  11.0 3.0 %collective-permute-done.5.from_dn = f32[160,128]{1,0:T(8,128)S(1)} collective-permute-done((f32[160,128]{1,0:T(8,128)S(1)}, f32[160,128]{1,0:T(8,128)S(1)}, u32[]{:S(2)}, u32[]{:S(2)}) %collective-permute-start.5) | collective-permute-done | bytes 81952 | tf_op jit(solution)/shard_map/ppermute | solution.py:534
  14.4 2.2 %collective-permute-start.6 = (f32[256,128]{1,0:T(8,128)S(1)}, f32[256,128]{1,0:T(8,128)S(1)}, u32[]{:S(2)}, u32[]{:S(2)}) collective-permute-start(f32[256,128]{1,0:T(8,128)S(1)} %get-tuple-element.54), channel_id=1, source_target_pairs={{0,8},{16,24},{32,40},{48,56},{64,72},{80,88},{96,104},{112,120},{... | collective-permute-start | bytes 393224 | tf_op jit(solution)/shard_map/ppermute | solution.py:542
  16.5 1.3 %collective-permute-start.7 = (f32[256,128]{1,0:T(8,128)S(1)}, f32[256,128]{1,0:T(8,128)S(1)}, u32[]{:S(2)}, u32[]{:S(2)}) collective-permute-start(f32[256,128]{1,0:T(8,128)S(1)} %get-tuple-element.55), channel_id=1, source_target_pairs={{8,16},{24,32},{40,48},{56,64},{72,80},{88,96},{104,112},{120,128}... | collective-permute-start | bytes 393224 | tf_op jit(solution)/shard_map/ppermute | solution.py:542
  18.0 1.5 %collective-permute-start.3 = (f32[328,128]{1,0:T(8,128)S(1)}, f32[328,128]{1,0:T(8,128)S(1)}, u32[]{:S(2)}, u32[]{:S(2)}) collective-permute-start(f32[328,128]{1,0:T(8,128)S(1)} %get-tuple-element.44), channel_id=1, source_target_pairs={{7,0},{0,1},{1,2},{2,3},{3,4},{4,5},{5,6},{6,7},{15,8},{8,9},{9,10... | collective-permute-start | bytes 503816 | tf_op jit(solution)/shard_map/ppermute | solution.py:534
  19.4 0.9 %shard_map.55.part = f32[24,2,24,128]{3,2,1,0:T(8,128)S(1)} custom-call(f32[117,2,24,128]{3,2,1,0:T(8,128)S(1)} %get-tuple-element.49.coef_in.coef, f32[81,2,24,128]{3,2,1,0:T(8,128)S(1)} %get-tuple-element.50.rolled_in.rolled, f32[24,2,24,128]{3,2,1,0:T(8,128)S(1)} %get-tuple-element.53.field), custom_call_target="tpu_custom_call" | custom-call | flops 990000000 | bytes 3240000 | tf_op jit(solution)/shard_map/pallas_call | solution.py:48
  20.4 0.6 collective-permute-done.7.other
  20.9 0.3 shard_map.56
  21.3 0.8 %collective-permute-start.8 = (f32[200,128]{1,0:T(8,128)S(1)}, f32[200,128]{1,0:T(8,128)S(1)}, u32[]{:S(2)}, u32[]{:S(2)}) collective-permute-start(f32[200,128]{1,0:T(8,128)S(1)} %get-tuple-element.56), channel_id=1, source_target_pairs={{1,0},{2,1},{3,2},{4,3},{5,4},{6,5},{7,6},{0,7},{9,8},{10,9},{11,1... | collective-permute-start | bytes 307208 | tf_op jit(solution)/shard_map/ppermute | solution.py:534
  22.1 0.7 %collective-permute-start.9 = (f32[200,128]{1,0:T(8,128)S(1)}, f32[200,128]{1,0:T(8,128)S(1)}, u32[]{:S(2)}, u32[]{:S(2)}) collective-permute-start(f32[200,128]{1,0:T(8,128)S(1)} %get-tuple-element.57), channel_id=1, source_target_pairs={{7,0},{0,1},{1,2},{2,3},{3,4},{4,5},{5,6},{6,7},{15,8},{8,9},{9,10... | collective-permute-start | bytes 307208 | tf_op jit(solution)/shard_map/ppermute | solution.py:534
  22.9 2.0 %collective-permute-start = (f32[664,128]{1,0:T(8,128)S(1)}, f32[664,128]{1,0:T(8,128)S(1)}, u32[]{:S(2)}, u32[]{:S(2)}) collective-permute-start(f32[664,128]{1,0:T(8,128)S(1)} %get-tuple-element.41), channel_id=1, source_target_pairs={{1,0},{2,1},{3,2},{4,3},{5,4},{6,5},{7,6},{0,7},{9,8},{10,9},{11,1... | collective-permute-start | bytes 1019912 | tf_op jit(solution)/shard_map/ppermute | solution.py:534
  25.2 2.6 %collective-permute-done.9.from_dn = f32[200,128]{1,0:T(8,128)S(1)} collective-permute-done((f32[200,128]{1,0:T(8,128)S(1)}, f32[200,128]{1,0:T(8,128)S(1)}, u32[]{:S(2)}, u32[]{:S(2)}) %collective-permute-start.9) | collective-permute-done | bytes 102432 | tf_op jit(solution)/shard_map/ppermute | solution.py:534
  27.8 0.5 shard_map.57
  28.3 6.0 %collective-permute-start.12 = (f32[400,128]{1,0:T(8,128)S(1)}, f32[400,128]{1,0:T(8,128)S(1)}, u32[]{:S(2)}, u32[]{:S(2)}) collective-permute-start(f32[400,128]{1,0:T(8,128)S(1)} %get-tuple-element.67), channel_id=1, source_target_pairs={{0,8},{16,24},{32,40},{48,56},{64,72},{80,88},{96,104},{112,120},{... | collective-permute-start | bytes 614408 | tf_op jit(solution)/shard_map/ppermute | solution.py:542
  34.3 0.3 shard_map.58
  34.6 1.7 %shard_map.61.part = f32[24,2,24,128]{3,2,1,0:T(8,128)S(1)} custom-call(f32[117,2,24,128]{3,2,1,0:T(8,128)S(1)} %get-tuple-element.60.coef, f32[81,2,24,128]{3,2,1,0:T(8,128)S(1)} %get-tuple-element.61.rolled, f32[24,2,24,128]{3,2,1,0:T(8,128)S(1)} %get-tuple-element.59._.field), custom_call_target="tpu_custom_call" | custom-call | flops 1870000000 | bytes 6120000 | tf_op jit(solution)/shard_map/pallas_call | solution.py:48
  36.3 3.2 %collective-permute-done.13.other = f32[400,128]{1,0:T(8,128)S(1)} collective-permute-done((f32[400,128]{1,0:T(8,128)S(1)}, f32[400,128]{1,0:T(8,128)S(1)}, u32[]{:S(2)}, u32[]{:S(2)}) %collective-permute-start.13) | collective-permute-done | bytes 204832 | tf_op jit(solution)/shard_map/ppermute | solution.py:542
  39.5 1.0 %shard_map.62 = (f32[24,2,24,128]{3,2,1,0:T(8,128)S(1)}, f32[352,128]{1,0:T(8,128)S(1)}, f32[352,128]{1,0:T(8,128)S(1)}) custom-call(f32[117,2,24,128]{3,2,1,0:T(8,128)S(1)} %get-tuple-element.60.coef, f32[81,2,24,128]{3,2,1,0:T(8,128)S(1)} %get-tuple-element.61.rolled, f32[6,2,24,128]{3,2,1,0:T(8,128)S(1)} %get-tuple-element.62.inverse, ...), custom_call_target="tpu_custom_call" | custom-call | flops 1430000000 | bytes 4680000 | tf_op jit(solution)/shard_map/pallas_call | solution.py:48
  40.5 3.7 %collective-permute-start.14 = (f32[352,128]{1,0:T(8,128)S(1)}, f32[352,128]{1,0:T(8,128)S(1)}, u32[]{:S(2)}, u32[]{:S(2)}) collective-permute-start(f32[352,128]{1,0:T(8,128)S(1)} %get-tuple-element.70), channel_id=1, source_target_pairs={{0,8},{16,24},{32,40},{48,56},{64,72},{80,88},{96,104},{112,120},{... | collective-permute-start | bytes 540680 | tf_op jit(solution)/shard_map/ppermute | solution.py:542
  44.3 1.7 %collective-permute-start.10 = (f32[1048,128]{1,0:T(8,128)S(1)}, f32[1048,128]{1,0:T(8,128)S(1)}, u32[]{:S(2)}, u32[]{:S(2)}) collective-permute-start(f32[1048,128]{1,0:T(8,128)S(1)} %get-tuple-element.63), channel_id=1, source_target_pairs={{0,8},{16,24},{32,40},{48,56},{64,72},{80,88},{96,104},{112,120},{... | collective-permute-start | bytes 1609736 | tf_op jit(solution)/shard_map/ppermute | solution.py:542
  46.2 1.7 %shard_map.63.part = f32[24,2,24,128]{3,2,1,0:T(8,128)S(1)} custom-call(f32[117,2,24,128]{3,2,1,0:T(8,128)S(1)} %get-tuple-element.60.coef, f32[81,2,24,128]{3,2,1,0:T(8,128)S(1)} %get-tuple-element.61.rolled, f32[24,2,24,128]{3,2,1,0:T(8,128)S(1)} %get-tuple-element.69.field), custom_call_target="tpu_custom_call" | custom-call | flops 1870000000 | bytes 6120000 | tf_op jit(solution)/shard_map/pallas_call | solution.py:48
  47.9 1.2 %collective-permute-done.15.other = f32[352,128]{1,0:T(8,128)S(1)} collective-permute-done((f32[352,128]{1,0:T(8,128)S(1)}, f32[352,128]{1,0:T(8,128)S(1)}, u32[]{:S(2)}, u32[]{:S(2)}) %collective-permute-start.15) | collective-permute-done | bytes 180256 | tf_op jit(solution)/shard_map/ppermute | solution.py:542
  49.1 0.6 shard_map.64.field
  49.7 1.7 %shard_map.65.part = f32[24,2,24,128]{3,2,1,0:T(8,128)S(1)} custom-call(f32[117,2,24,128]{3,2,1,0:T(8,128)S(1)} %get-tuple-element.60.coef, f32[81,2,24,128]{3,2,1,0:T(8,128)S(1)} %get-tuple-element.61.rolled, f32[24,2,24,128]{3,2,1,0:T(8,128)S(1)} %shard_map.64.field), custom_call_target="tpu_custom_call" | custom-call | flops 1870000000 | bytes 6120000 | tf_op jit(solution)/shard_map/pallas_call | solution.py:48
  51.5 3.5 %collective-permute-start.16 = (f32[544,128]{1,0:T(8,128)S(1)}, f32[544,128]{1,0:T(8,128)S(1)}, u32[]{:S(2)}, u32[]{:S(2)}) collective-permute-start(f32[544,128]{1,0:T(8,128)S(1)} %get-tuple-element.73), channel_id=1, source_target_pairs={{0,8},{16,24},{32,40},{48,56},{64,72},{80,88},{96,104},{112,120},{... | collective-permute-start | bytes 835592 | tf_op jit(solution)/shard_map/ppermute | solution.py:542
  55.4 0.8 %shard_map.66.far_part = f32[24,2,24,128]{3,2,1,0:T(8,128)S(1)} custom-call(f32[117,2,24,128]{3,2,1,0:T(8,128)S(1)} %get-tuple-element.60.coef, f32[81,24,128]{2,1,0:T(8,128)S(1)} %get-tuple-element.65.far_coef, f32[54,24,128]{2,1,0:T(8,128)S(1)} %get-tuple-element.72.far_rolled, f32[24,2,24,128]{3,2,1,0:T(8,128)S(1)} %shard_map.64.field), custom_call_target="tpu_custom_call" | custom-call | flops 880000000 | bytes 2880000 | tf_op jit(solution)/shard_map/pallas_call | solution.py:48
  56.2 5.0 %collective-permute-done.17.other = f32[544,128]{1,0:T(8,128)S(1)} collective-permute-done((f32[544,128]{1,0:T(8,128)S(1)}, f32[544,128]{1,0:T(8,128)S(1)}, u32[]{:S(2)}, u32[]{:S(2)}) %collective-permute-start.17) | collective-permute-done | bytes 278560 | tf_op jit(solution)/shard_map/ppermute | solution.py:542
  61.3 1.2 %shard_map.69 = (f32[24,2,24,128]{3,2,1,0:T(8,128)S(1)}, f32[24,2,24,128]{3,2,1,0:T(8,128)S(1)}, f32[1,8,128]{2,1,0:T(8,128)S(1)}) custom-call(f32[117,2,24,128]{3,2,1,0:T(8,128)S(1)} %get-tuple-element.60.coef, f32[81,2,24,128]{3,2,1,0:T(8,128)S(1)} %get-tuple-element.61.rolled, f32[81,24,128]{2,1,0:T(8,128)S(1)} %get-tuple-element.65.far_coef, ...), custom_call_target="tpu_custom_call" | custom-call | flops 330000000 | bytes 1080000 | tf_op jit(solution)/shard_map/pallas_call | solution.py:48
  62.4 2.0 %shard_map.70 = (f32[8,3,2,8,128]{4,3,2,1,0:T(8,128)}, f32[8,8,1,4,63]{4,3,2,1,0:T(4,128)}) custom-call(f32[24,2,24,128]{3,2,1,0:T(8,128)S(1)} %get-tuple-element.75.field, f32[24,2,24,128]{3,2,1,0:T(8,128)S(1)} %get-tuple-element.76.far, f32[1,8,128]{2,1,0:T(8,128)S(1)} %shard_map.67.segs.seg, f32[1,8,128]{2,1,0:T(8,128)S(1)} %get-tuple-element.77.far_seg), custom_call_target="tpu_custom_call" | custom-call | flops 3300000000 | bytes 10800000 | tf_op jit(solution)/shard_map/pallas_call | solution.py:48
  (31 shorter events, 2.0 us)
Async XLA Ops:
  0.6 1.2 %copy-start = (f32[14,3,3,2,8,128]{5,4,3,2,1,0:T(8,128)S(1)}, f32[14,3,3,2,8,128]{5,4,3,2,1,0:T(8,128)}, u32[]{:S(2)}) copy-start(f32[14,3,3,2,8,128]{5,4,3,2,1,0:T(8,128)} %stencil.5) | copy-start | bytes 3096580
  1.8 0.9 %copy-start.1 = (f32[8,3,2,8,128]{4,3,2,1,0:T(8,128)S(1)}, f32[8,3,2,8,128]{4,3,2,1,0:T(8,128)}, u32[]{:S(2)}) copy-start(f32[8,3,2,8,128]{4,3,2,1,0:T(8,128)} %cands.1) | copy-start | bytes 589828
  3.1 8.0 %collective-permute-start.4 = (f32[160,128]{1,0:T(8,128)S(1)}, f32[160,128]{1,0:T(8,128)S(1)}, u32[]{:S(2)}, u32[]{:S(2)}) collective-permute-start(f32[160,128]{1,0:T(8,128)S(1)} %get-tuple-element.45), channel_id=1, source_target_pairs={{1,0},{2,1},{3,2},{4,3},{5,4},{6,5},{7,6},{0,7},{9,8},{10,9},{11,1... | collective-permute-start | bytes 245768 | tf_op jit(solution)/shard_map/ppermute | solution.py:534
  9.6 4.5 %collective-permute-start.5 = (f32[160,128]{1,0:T(8,128)S(1)}, f32[160,128]{1,0:T(8,128)S(1)}, u32[]{:S(2)}, u32[]{:S(2)}) collective-permute-start(f32[160,128]{1,0:T(8,128)S(1)} %get-tuple-element.46), channel_id=1, source_target_pairs={{7,0},{0,1},{1,2},{2,3},{3,4},{4,5},{5,6},{6,7},{15,8},{8,9},{9,10... | collective-permute-start | bytes 245768 | tf_op jit(solution)/shard_map/ppermute | solution.py:534
  14.4 6.0 %collective-permute-start.6 = (f32[256,128]{1,0:T(8,128)S(1)}, f32[256,128]{1,0:T(8,128)S(1)}, u32[]{:S(2)}, u32[]{:S(2)}) collective-permute-start(f32[256,128]{1,0:T(8,128)S(1)} %get-tuple-element.54), channel_id=1, source_target_pairs={{0,8},{16,24},{32,40},{48,56},{64,72},{80,88},{96,104},{112,120},{... | collective-permute-start | bytes 393224 | tf_op jit(solution)/shard_map/ppermute | solution.py:542
  16.5 4.4 %collective-permute-start.7 = (f32[256,128]{1,0:T(8,128)S(1)}, f32[256,128]{1,0:T(8,128)S(1)}, u32[]{:S(2)}, u32[]{:S(2)}) collective-permute-start(f32[256,128]{1,0:T(8,128)S(1)} %get-tuple-element.55), channel_id=1, source_target_pairs={{8,16},{24,32},{40,48},{56,64},{72,80},{88,96},{104,112},{120,128}... | collective-permute-start | bytes 393224 | tf_op jit(solution)/shard_map/ppermute | solution.py:542
  17.9 7.1 %collective-permute-start.2 = (f32[328,128]{1,0:T(8,128)S(1)}, f32[328,128]{1,0:T(8,128)S(1)}, u32[]{:S(2)}, u32[]{:S(2)}) collective-permute-start(f32[328,128]{1,0:T(8,128)S(1)} %get-tuple-element.43), channel_id=1, source_target_pairs={{1,0},{2,1},{3,2},{4,3},{5,4},{6,5},{7,6},{0,7},{9,8},{10,9},{11,1... | collective-permute-start | bytes 503816 | tf_op jit(solution)/shard_map/ppermute | solution.py:534
  18.0 7.0 %collective-permute-start.3 = (f32[328,128]{1,0:T(8,128)S(1)}, f32[328,128]{1,0:T(8,128)S(1)}, u32[]{:S(2)}, u32[]{:S(2)}) collective-permute-start(f32[328,128]{1,0:T(8,128)S(1)} %get-tuple-element.44), channel_id=1, source_target_pairs={{7,0},{0,1},{1,2},{2,3},{3,4},{4,5},{5,6},{6,7},{15,8},{8,9},{9,10... | collective-permute-start | bytes 503816 | tf_op jit(solution)/shard_map/ppermute | solution.py:534
  19.4 1.5 %copy-start.2 = (s32[1,4,128]{2,1,0:T(4,128)S(1)}, s32[1,4,128]{2,1,0:T(4,128)}, u32[]{:S(2)}) copy-start(s32[1,4,128]{2,1,0:T(4,128)} %seg.3) | copy-start | bytes 6148
  21.3 3.9 %collective-permute-start.8 = (f32[200,128]{1,0:T(8,128)S(1)}, f32[200,128]{1,0:T(8,128)S(1)}, u32[]{:S(2)}, u32[]{:S(2)}) collective-permute-start(f32[200,128]{1,0:T(8,128)S(1)} %get-tuple-element.56), channel_id=1, source_target_pairs={{1,0},{2,1},{3,2},{4,3},{5,4},{6,5},{7,6},{0,7},{9,8},{10,9},{11,1... | collective-permute-start | bytes 307208 | tf_op jit(solution)/shard_map/ppermute | solution.py:534
  22.1 5.7 %collective-permute-start.9 = (f32[200,128]{1,0:T(8,128)S(1)}, f32[200,128]{1,0:T(8,128)S(1)}, u32[]{:S(2)}, u32[]{:S(2)}) collective-permute-start(f32[200,128]{1,0:T(8,128)S(1)} %get-tuple-element.57), channel_id=1, source_target_pairs={{7,0},{0,1},{1,2},{2,3},{3,4},{4,5},{5,6},{6,7},{15,8},{8,9},{9,10... | collective-permute-start | bytes 307208 | tf_op jit(solution)/shard_map/ppermute | solution.py:534
  22.9 11.4 %collective-permute-start = (f32[664,128]{1,0:T(8,128)S(1)}, f32[664,128]{1,0:T(8,128)S(1)}, u32[]{:S(2)}, u32[]{:S(2)}) collective-permute-start(f32[664,128]{1,0:T(8,128)S(1)} %get-tuple-element.41), channel_id=1, source_target_pairs={{1,0},{2,1},{3,2},{4,3},{5,4},{6,5},{7,6},{0,7},{9,8},{10,9},{11,1... | collective-permute-start | bytes 1019912 | tf_op jit(solution)/shard_map/ppermute | solution.py:534
  25.0 9.3 %collective-permute-start.1 = (f32[664,128]{1,0:T(8,128)S(1)}, f32[664,128]{1,0:T(8,128)S(1)}, u32[]{:S(2)}, u32[]{:S(2)}) collective-permute-start(f32[664,128]{1,0:T(8,128)S(1)} %get-tuple-element.42), channel_id=1, source_target_pairs={{7,0},{0,1},{1,2},{2,3},{3,4},{4,5},{5,6},{6,7},{15,8},{8,9},{9,10... | collective-permute-start | bytes 1019912 | tf_op jit(solution)/shard_map/ppermute | solution.py:534
  28.3 8.0 %collective-permute-start.12 = (f32[400,128]{1,0:T(8,128)S(1)}, f32[400,128]{1,0:T(8,128)S(1)}, u32[]{:S(2)}, u32[]{:S(2)}) collective-permute-start(f32[400,128]{1,0:T(8,128)S(1)} %get-tuple-element.67), channel_id=1, source_target_pairs={{0,8},{16,24},{32,40},{48,56},{64,72},{80,88},{96,104},{112,120},{... | collective-permute-start | bytes 614408 | tf_op jit(solution)/shard_map/ppermute | solution.py:542
  34.3 5.2 %collective-permute-start.13 = (f32[400,128]{1,0:T(8,128)S(1)}, f32[400,128]{1,0:T(8,128)S(1)}, u32[]{:S(2)}, u32[]{:S(2)}) collective-permute-start(f32[400,128]{1,0:T(8,128)S(1)} %get-tuple-element.68), channel_id=1, source_target_pairs={{8,16},{24,32},{40,48},{56,64},{72,80},{88,96},{104,112},{120,128}... | collective-permute-start | bytes 614408 | tf_op jit(solution)/shard_map/ppermute | solution.py:542
  40.5 7.4 %collective-permute-start.14 = (f32[352,128]{1,0:T(8,128)S(1)}, f32[352,128]{1,0:T(8,128)S(1)}, u32[]{:S(2)}, u32[]{:S(2)}) collective-permute-start(f32[352,128]{1,0:T(8,128)S(1)} %get-tuple-element.70), channel_id=1, source_target_pairs={{0,8},{16,24},{32,40},{48,56},{64,72},{80,88},{96,104},{112,120},{... | collective-permute-start | bytes 540680 | tf_op jit(solution)/shard_map/ppermute | solution.py:542
  44.2 4.9 %collective-permute-start.15 = (f32[352,128]{1,0:T(8,128)S(1)}, f32[352,128]{1,0:T(8,128)S(1)}, u32[]{:S(2)}, u32[]{:S(2)}) collective-permute-start(f32[352,128]{1,0:T(8,128)S(1)} %get-tuple-element.71), channel_id=1, source_target_pairs={{8,16},{24,32},{40,48},{56,64},{72,80},{88,96},{104,112},{120,128}... | collective-permute-start | bytes 540680 | tf_op jit(solution)/shard_map/ppermute | solution.py:542
  44.3 10.7 %collective-permute-start.10 = (f32[1048,128]{1,0:T(8,128)S(1)}, f32[1048,128]{1,0:T(8,128)S(1)}, u32[]{:S(2)}, u32[]{:S(2)}) collective-permute-start(f32[1048,128]{1,0:T(8,128)S(1)} %get-tuple-element.63), channel_id=1, source_target_pairs={{0,8},{16,24},{32,40},{48,56},{64,72},{80,88},{96,104},{112,120},{... | collective-permute-start | bytes 1609736 | tf_op jit(solution)/shard_map/ppermute | solution.py:542
  46.0 9.2 %collective-permute-start.11 = (f32[1048,128]{1,0:T(8,128)S(1)}, f32[1048,128]{1,0:T(8,128)S(1)}, u32[]{:S(2)}, u32[]{:S(2)}) collective-permute-start(f32[1048,128]{1,0:T(8,128)S(1)} %get-tuple-element.64), channel_id=1, source_target_pairs={{8,16},{24,32},{40,48},{56,64},{72,80},{88,96},{104,112},{120,128}... | collective-permute-start | bytes 1609736 | tf_op jit(solution)/shard_map/ppermute | solution.py:542
  51.5 4.7 %collective-permute-start.16 = (f32[544,128]{1,0:T(8,128)S(1)}, f32[544,128]{1,0:T(8,128)S(1)}, u32[]{:S(2)}, u32[]{:S(2)}) collective-permute-start(f32[544,128]{1,0:T(8,128)S(1)} %get-tuple-element.73), channel_id=1, source_target_pairs={{0,8},{16,24},{32,40},{48,56},{64,72},{80,88},{96,104},{112,120},{... | collective-permute-start | bytes 835592 | tf_op jit(solution)/shard_map/ppermute | solution.py:542
  55.0 6.3 %collective-permute-start.17 = (f32[544,128]{1,0:T(8,128)S(1)}, f32[544,128]{1,0:T(8,128)S(1)}, u32[]{:S(2)}, u32[]{:S(2)}) collective-permute-start(f32[544,128]{1,0:T(8,128)S(1)} %get-tuple-element.74), channel_id=1, source_target_pairs={{8,16},{24,32},{40,48},{56,64},{72,80},{88,96},{104,112},{120,128}... | collective-permute-start | bytes 835592 | tf_op jit(solution)/shard_map/ppermute | solution.py:542

commit v5 on v4

--- a/solution.py
+++ b/solution.py
@@ -77,7 +77,23 @@
     return [c / det for c in (c00, c01, c02, c11, c12, c22)]
 
 
-def pack_kernel(stencil, cands, rim_dn, rim_up, coef, rolled, inverse, field):
+def rim_kernel(stencil, cands, rim_dn, rim_up):
+    for c in range(K):
+        for d in range(3):
+            for p in range(2):
+                i = (c * 3 + d) * 2 + p
+                rim_dn[pl.ds(i, 1), :] = cands[c, d, p, 0:1]
+                rim_up[pl.ds(i, 1), :] = cands[c, d, p, 7:8]
+    for msg, ones, row in ((rim_dn, ONE_DN, 0), (rim_up, ONE_UP, 7)):
+        for n, j in enumerate(ones):
+            for e in range(3):
+                for d in range(3):
+                    for p in range(2):
+                        at = RIM_S + n * 18 + (e * 3 + d) * 2 + p
+                        msg[pl.ds(at, 1), :] = stencil[1 + j, e, d, p, row : row + 1]
+
+
+def own_kernel(stencil, cands, coef, rolled, inverse, field):
     own = pl.ds(8, 8)
     for c in range(K):
         for d in range(3):
@@ -95,19 +111,6 @@
                     rolled[ROLLED.index(j) * 9 + e * 3 + d, :, own, :] = roll_z(
                         block, neighbour_steps[j][2]
                     )
-    for c in range(K):
-        for d in range(3):
-            for p in range(2):
-                i = (c * 3 + d) * 2 + p
-                rim_dn[pl.ds(i, 1), :] = cands[c, d, p, 0:1]
-                rim_up[pl.ds(i, 1), :] = cands[c, d, p, 7:8]
-    for msg, ones, row in ((rim_dn, ONE_DN, 0), (rim_up, ONE_UP, 7)):
-        for n, j in enumerate(ones):
-            for e in range(3):
-                for d in range(3):
-                    for p in range(2):
-                        at = RIM_S + n * 18 + (e * 3 + d) * 2 + p
-                        msg[pl.ds(at, 1), :] = stencil[1 + j, e, d, p, row : row + 1]
 
 
 def roll_z(x, by):
@@ -547,9 +550,8 @@
 def body(stencil, cands, seg):
     frame = struct(24, 2, ROWS, 128)
     operator = [struct(117, 2, ROWS, 128), struct(9 * len(ROLLED), 2, ROWS, 128), struct(6, 2, ROWS, 128)]
-    rim_dn, rim_up, coef, rolled, inverse, field = call(
-        pack_kernel, [struct(RIM, 128)] * 2 + operator + [frame], stencil, cands
-    )
+    rim_dn, rim_up = call(rim_kernel, [struct(RIM, 128)] * 2, stencil, cands)
+    coef, rolled, inverse, field = call(own_kernel, operator + [frame], stencil, cands)
     rim_from_up = moved(rim_dn, "gy", 1)
     rim_from_dn = moved(rim_up, "gy", -1)
 

time: 64.5 us -> 64.3 us (level)
    pallas_call x21 -> x22, Pallas kernels: 14 us -> 14 us  [call(): pl.pallas_call(kernel, out_shape=out_shape, in_specs=[VMEM] * (len(args)...]
  transfers between devices with their start and end apart: 18 -> 18, of which waited for: 8 -> 8; matrix products, arithmetic and copies ran while one was open for 0% -> 0% of each run, Pallas kernels for 14% -> 15%
where the time goes in v5:
time: 64.3 us; the launch traced here: 64.2 us
  starting transfers between devices  30.2 us (47%)
  waiting for transfers between devices  17 us (26%)
  Pallas kernels  14 us (22%)
  local copies, waits for them, and re-layouts  2.14 us (3%)
  between operations  0.79 us (1%)
    ppermute x10, starting transfers between devices, swapped(): lax.ppermute(block, 'gx', two + [(j, i) for i, j in two])  18.6 us
    pallas_call x22, Pallas kernels, call(): pl.pallas_call(kernel, out_shape=out_shape, in_specs=[VMEM] * (len(args)...  14 us
    ppermute x8, starting transfers between devices, moved(): lax.ppermute(block, axis, [((i + by) % size, i) for i in range(size)])  11.6 us
    ppermute x10, waiting for transfers between devices, swapped(): lax.ppermute(block, 'gx', two + [(j, i) for i, j in two])  10.1 us
    ppermute x8, waiting for transfers between devices, moved(): lax.ppermute(block, axis, [((i + by) % size, i) for i in range(size)])  6.9 us
    unnamed x6, local copies, waits for them, and re-layouts  2.14 us
  transfers between devices with their start and end apart: 18, of which 8 were waited for; matrix products, arithmetic and copies ran while one was open for 0% of the time, Pallas kernels for 15%

profile of v5, /device:TPU:1, one launch (start us, length us, event | category | flops | bytes accessed | tf_op | source)
XLA Modules:
  0.0 64.2 jit_solution(14054225310816642497)
XLA Ops:
  0.6 1.2 %copy-done = f32[14,3,3,2,8,128]{5,4,3,2,1,0:T(8,128)S(1)} copy-done((f32[14,3,3,2,8,128]{5,4,3,2,1,0:T(8,128)S(1)}, f32[14,3,3,2,8,128]{5,4,3,2,1,0:T(8,128)}, u32[]{:S(2)}) %copy-start) | copy-done | bytes 1032216
  1.9 0.9 %copy-done.1 = f32[8,3,2,8,128]{4,3,2,1,0:T(8,128)S(1)} copy-done((f32[8,3,2,8,128]{4,3,2,1,0:T(8,128)S(1)}, f32[8,3,2,8,128]{4,3,2,1,0:T(8,128)}, u32[]{:S(2)}) %copy-start.1) | copy-done | bytes 196632
  2.9 6.5 %collective-permute-start.4 = (f32[160,128]{1,0:T(8,128)S(1)}, f32[160,128]{1,0:T(8,128)S(1)}, u32[]{:S(2)}, u32[]{:S(2)}) collective-permute-start(f32[160,128]{1,0:T(8,128)S(1)} %get-tuple-element.45), channel_id=1, source_target_pairs={{1,0},{2,1},{3,2},{4,3},{5,4},{6,5},{7,6},{0,7},{9,8},{10,9},{11,1... | collective-permute-start | bytes 245768 | tf_op jit(solution)/shard_map/ppermute | solution.py:537
  9.6 1.2 %collective-permute-done.4.from_up = f32[160,128]{1,0:T(8,128)S(1)} collective-permute-done((f32[160,128]{1,0:T(8,128)S(1)}, f32[160,128]{1,0:T(8,128)S(1)}, u32[]{:S(2)}, u32[]{:S(2)}) %collective-permute-start.4) | collective-permute-done | bytes 81952 | tf_op jit(solution)/shard_map/ppermute | solution.py:537
  10.8 3.0 %collective-permute-done.5.from_dn = f32[160,128]{1,0:T(8,128)S(1)} collective-permute-done((f32[160,128]{1,0:T(8,128)S(1)}, f32[160,128]{1,0:T(8,128)S(1)}, u32[]{:S(2)}, u32[]{:S(2)}) %collective-permute-start.5) | collective-permute-done | bytes 81952 | tf_op jit(solution)/shard_map/ppermute | solution.py:537
  14.1 2.2 %collective-permute-start.6 = (f32[256,128]{1,0:T(8,128)S(1)}, f32[256,128]{1,0:T(8,128)S(1)}, u32[]{:S(2)}, u32[]{:S(2)}) collective-permute-start(f32[256,128]{1,0:T(8,128)S(1)} %get-tuple-element.54), channel_id=1, source_target_pairs={{0,8},{16,24},{32,40},{48,56},{64,72},{80,88},{96,104},{112,120},{... | collective-permute-start | bytes 393224 | tf_op jit(solution)/shard_map/ppermute | solution.py:545
  16.3 1.3 %collective-permute-start.7 = (f32[256,128]{1,0:T(8,128)S(1)}, f32[256,128]{1,0:T(8,128)S(1)}, u32[]{:S(2)}, u32[]{:S(2)}) collective-permute-start(f32[256,128]{1,0:T(8,128)S(1)} %get-tuple-element.55), channel_id=1, source_target_pairs={{8,16},{24,32},{40,48},{56,64},{72,80},{88,96},{104,112},{120,128}... | collective-permute-start | bytes 393224 | tf_op jit(solution)/shard_map/ppermute | solution.py:545
  17.8 1.5 %collective-permute-start.3 = (f32[328,128]{1,0:T(8,128)S(1)}, f32[328,128]{1,0:T(8,128)S(1)}, u32[]{:S(2)}, u32[]{:S(2)}) collective-permute-start(f32[328,128]{1,0:T(8,128)S(1)} %get-tuple-element.44), channel_id=1, source_target_pairs={{7,0},{0,1},{1,2},{2,3},{3,4},{4,5},{5,6},{6,7},{15,8},{8,9},{9,10... | collective-permute-start | bytes 503816 | tf_op jit(solution)/shard_map/ppermute | solution.py:537
  19.2 0.9 %shard_map.56.part = f32[24,2,24,128]{3,2,1,0:T(8,128)S(1)} custom-call(f32[117,2,24,128]{3,2,1,0:T(8,128)S(1)} %get-tuple-element.49.coef_in.coef, f32[81,2,24,128]{3,2,1,0:T(8,128)S(1)} %get-tuple-element.50.rolled_in.rolled, f32[24,2,24,128]{3,2,1,0:T(8,128)S(1)} %get-tuple-element.53.field), custom_call_target="tpu_custom_call" | custom-call | flops 990000000 | bytes 3240000 | tf_op jit(solution)/shard_map/pallas_call | solution.py:48
  20.2 0.6 collective-permute-done.7.other
  20.7 0.3 shard_map.57
  21.1 0.8 %collective-permute-start.8 = (f32[200,128]{1,0:T(8,128)S(1)}, f32[200,128]{1,0:T(8,128)S(1)}, u32[]{:S(2)}, u32[]{:S(2)}) collective-permute-start(f32[200,128]{1,0:T(8,128)S(1)} %get-tuple-element.56), channel_id=1, source_target_pairs={{1,0},{2,1},{3,2},{4,3},{5,4},{6,5},{7,6},{0,7},{9,8},{10,9},{11,1... | collective-permute-start | bytes 307208 | tf_op jit(solution)/shard_map/ppermute | solution.py:537
  21.9 0.7 %collective-permute-start.9 = (f32[200,128]{1,0:T(8,128)S(1)}, f32[200,128]{1,0:T(8,128)S(1)}, u32[]{:S(2)}, u32[]{:S(2)}) collective-permute-start(f32[200,128]{1,0:T(8,128)S(1)} %get-tuple-element.57), channel_id=1, source_target_pairs={{7,0},{0,1},{1,2},{2,3},{3,4},{4,5},{5,6},{6,7},{15,8},{8,9},{9,10... | collective-permute-start | bytes 307208 | tf_op jit(solution)/shard_map/ppermute | solution.py:537
  22.7 2.0 %collective-permute-start = (f32[664,128]{1,0:T(8,128)S(1)}, f32[664,128]{1,0:T(8,128)S(1)}, u32[]{:S(2)}, u32[]{:S(2)}) collective-permute-start(f32[664,128]{1,0:T(8,128)S(1)} %get-tuple-element.41), channel_id=1, source_target_pairs={{1,0},{2,1},{3,2},{4,3},{5,4},{6,5},{7,6},{0,7},{9,8},{10,9},{11,1... | collective-permute-start | bytes 1019912 | tf_op jit(solution)/shard_map/ppermute | solution.py:537
  25.0 2.6 %collective-permute-done.9.from_dn = f32[200,128]{1,0:T(8,128)S(1)} collective-permute-done((f32[200,128]{1,0:T(8,128)S(1)}, f32[200,128]{1,0:T(8,128)S(1)}, u32[]{:S(2)}, u32[]{:S(2)}) %collective-permute-start.9) | collective-permute-done | bytes 102432 | tf_op jit(solution)/shard_map/ppermute | solution.py:537
  27.6 0.5 shard_map.58
  28.1 6.0 %collective-permute-start.12 = (f32[400,128]{1,0:T(8,128)S(1)}, f32[400,128]{1,0:T(8,128)S(1)}, u32[]{:S(2)}, u32[]{:S(2)}) collective-permute-start(f32[400,128]{1,0:T(8,128)S(1)} %get-tuple-element.67), channel_id=1, source_target_pairs={{0,8},{16,24},{32,40},{48,56},{64,72},{80,88},{96,104},{112,120},{... | collective-permute-start | bytes 614408 | tf_op jit(solution)/shard_map/ppermute | solution.py:545
  34.1 0.3 shard_map.59
  34.4 1.7 %shard_map.62.part = f32[24,2,24,128]{3,2,1,0:T(8,128)S(1)} custom-call(f32[117,2,24,128]{3,2,1,0:T(8,128)S(1)} %get-tuple-element.60.coef, f32[81,2,24,128]{3,2,1,0:T(8,128)S(1)} %get-tuple-element.61.rolled, f32[24,2,24,128]{3,2,1,0:T(8,128)S(1)} %get-tuple-element.59._.field), custom_call_target="tpu_custom_call" | custom-call | flops 1870000000 | bytes 6120000 | tf_op jit(solution)/shard_map/pallas_call | solution.py:48
  36.1 3.2 %collective-permute-done.13.other = f32[400,128]{1,0:T(8,128)S(1)} collective-permute-done((f32[400,128]{1,0:T(8,128)S(1)}, f32[400,128]{1,0:T(8,128)S(1)}, u32[]{:S(2)}, u32[]{:S(2)}) %collective-permute-start.13) | collective-permute-done | bytes 204832 | tf_op jit(solution)/shard_map/ppermute | solution.py:545
  39.3 1.0 %shard_map.63 = (f32[24,2,24,128]{3,2,1,0:T(8,128)S(1)}, f32[352,128]{1,0:T(8,128)S(1)}, f32[352,128]{1,0:T(8,128)S(1)}) custom-call(f32[117,2,24,128]{3,2,1,0:T(8,128)S(1)} %get-tuple-element.60.coef, f32[81,2,24,128]{3,2,1,0:T(8,128)S(1)} %get-tuple-element.61.rolled, f32[6,2,24,128]{3,2,1,0:T(8,128)S(1)} %get-tuple-element.62.inverse, ...), custom_call_target="tpu_custom_call" | custom-call | flops 1430000000 | bytes 4680000 | tf_op jit(solution)/shard_map/pallas_call | solution.py:48
  40.3 3.7 %collective-permute-start.14 = (f32[352,128]{1,0:T(8,128)S(1)}, f32[352,128]{1,0:T(8,128)S(1)}, u32[]{:S(2)}, u32[]{:S(2)}) collective-permute-start(f32[352,128]{1,0:T(8,128)S(1)} %get-tuple-element.70), channel_id=1, source_target_pairs={{0,8},{16,24},{32,40},{48,56},{64,72},{80,88},{96,104},{112,120},{... | collective-permute-start | bytes 540680 | tf_op jit(solution)/shard_map/ppermute | solution.py:545
  44.1 1.7 %collective-permute-start.10 = (f32[1048,128]{1,0:T(8,128)S(1)}, f32[1048,128]{1,0:T(8,128)S(1)}, u32[]{:S(2)}, u32[]{:S(2)}) collective-permute-start(f32[1048,128]{1,0:T(8,128)S(1)} %get-tuple-element.63), channel_id=1, source_target_pairs={{0,8},{16,24},{32,40},{48,56},{64,72},{80,88},{96,104},{112,120},{... | collective-permute-start | bytes 1609736 | tf_op jit(solution)/shard_map/ppermute | solution.py:545
  46.0 1.7 %shard_map.64.part = f32[24,2,24,128]{3,2,1,0:T(8,128)S(1)} custom-call(f32[117,2,24,128]{3,2,1,0:T(8,128)S(1)} %get-tuple-element.60.coef, f32[81,2,24,128]{3,2,1,0:T(8,128)S(1)} %get-tuple-element.61.rolled, f32[24,2,24,128]{3,2,1,0:T(8,128)S(1)} %get-tuple-element.69.field), custom_call_target="tpu_custom_call" | custom-call | flops 1870000000 | bytes 6120000 | tf_op jit(solution)/shard_map/pallas_call | solution.py:48
  47.7 1.2 %collective-permute-done.15.other = f32[352,128]{1,0:T(8,128)S(1)} collective-permute-done((f32[352,128]{1,0:T(8,128)S(1)}, f32[352,128]{1,0:T(8,128)S(1)}, u32[]{:S(2)}, u32[]{:S(2)}) %collective-permute-start.15) | collective-permute-done | bytes 180256 | tf_op jit(solution)/shard_map/ppermute | solution.py:545
  48.9 0.6 shard_map.65.field
  49.5 1.7 %shard_map.66.part = f32[24,2,24,128]{3,2,1,0:T(8,128)S(1)} custom-call(f32[117,2,24,128]{3,2,1,0:T(8,128)S(1)} %get-tuple-element.60.coef, f32[81,2,24,128]{3,2,1,0:T(8,128)S(1)} %get-tuple-element.61.rolled, f32[24,2,24,128]{3,2,1,0:T(8,128)S(1)} %shard_map.65.field), custom_call_target="tpu_custom_call" | custom-call | flops 1870000000 | bytes 6120000 | tf_op jit(solution)/shard_map/pallas_call | solution.py:48
  51.3 3.5 %collective-permute-start.16 = (f32[544,128]{1,0:T(8,128)S(1)}, f32[544,128]{1,0:T(8,128)S(1)}, u32[]{:S(2)}, u32[]{:S(2)}) collective-permute-start(f32[544,128]{1,0:T(8,128)S(1)} %get-tuple-element.73), channel_id=1, source_target_pairs={{0,8},{16,24},{32,40},{48,56},{64,72},{80,88},{96,104},{112,120},{... | collective-permute-start | bytes 835592 | tf_op jit(solution)/shard_map/ppermute | solution.py:545
  55.2 0.8 %shard_map.67.far_part = f32[24,2,24,128]{3,2,1,0:T(8,128)S(1)} custom-call(f32[117,2,24,128]{3,2,1,0:T(8,128)S(1)} %get-tuple-element.60.coef, f32[81,24,128]{2,1,0:T(8,128)S(1)} %get-tuple-element.65.far_coef, f32[54,24,128]{2,1,0:T(8,128)S(1)} %get-tuple-element.72.far_rolled, f32[24,2,24,128]{3,2,1,0:T(8,128)S(1)} %shard_map.65.field), custom_call_target="tpu_custom_call" | custom-call | flops 880000000 | bytes 2880000 | tf_op jit(solution)/shard_map/pallas_call | solution.py:48
  56.0 5.0 %collective-permute-done.17.other = f32[544,128]{1,0:T(8,128)S(1)} collective-permute-done((f32[544,128]{1,0:T(8,128)S(1)}, f32[544,128]{1,0:T(8,128)S(1)}, u32[]{:S(2)}, u32[]{:S(2)}) %collective-permute-start.17) | collective-permute-done | bytes 278560 | tf_op jit(solution)/shard_map/ppermute | solution.py:545
  61.1 1.2 %shard_map.70 = (f32[24,2,24,128]{3,2,1,0:T(8,128)S(1)}, f32[24,2,24,128]{3,2,1,0:T(8,128)S(1)}, f32[1,8,128]{2,1,0:T(8,128)S(1)}) custom-call(f32[117,2,24,128]{3,2,1,0:T(8,128)S(1)} %get-tuple-element.60.coef, f32[81,2,24,128]{3,2,1,0:T(8,128)S(1)} %get-tuple-element.61.rolled, f32[81,24,128]{2,1,0:T(8,128)S(1)} %get-tuple-element.65.far_coef, ...), custom_call_target="tpu_custom_call" | custom-call | flops 330000000 | bytes 1080000 | tf_op jit(solution)/shard_map/pallas_call | solution.py:48
  62.2 2.0 %shard_map.71 = (f32[8,3,2,8,128]{4,3,2,1,0:T(8,128)}, f32[8,8,1,4,63]{4,3,2,1,0:T(4,128)}) custom-call(f32[24,2,24,128]{3,2,1,0:T(8,128)S(1)} %get-tuple-element.75.field, f32[24,2,24,128]{3,2,1,0:T(8,128)S(1)} %get-tuple-element.76.far, f32[1,8,128]{2,1,0:T(8,128)S(1)} %shard_map.68.segs.seg, f32[1,8,128]{2,1,0:T(8,128)S(1)} %get-tuple-element.77.far_seg), custom_call_target="tpu_custom_call" | custom-call | flops 3300000000 | bytes 10800000 | tf_op jit(solution)/shard_map/pallas_call | solution.py:48
  (32 shorter events, 2.0 us)
Async XLA Ops:
  0.6 1.2 %copy-start = (f32[14,3,3,2,8,128]{5,4,3,2,1,0:T(8,128)S(1)}, f32[14,3,3,2,8,128]{5,4,3,2,1,0:T(8,128)}, u32[]{:S(2)}) copy-start(f32[14,3,3,2,8,128]{5,4,3,2,1,0:T(8,128)} %stencil.7) | copy-start | bytes 3096580
  1.8 0.9 %copy-start.1 = (f32[8,3,2,8,128]{4,3,2,1,0:T(8,128)S(1)}, f32[8,3,2,8,128]{4,3,2,1,0:T(8,128)}, u32[]{:S(2)}) copy-start(f32[8,3,2,8,128]{4,3,2,1,0:T(8,128)} %cands.3) | copy-start | bytes 589828
  2.9 8.0 %collective-permute-start.4 = (f32[160,128]{1,0:T(8,128)S(1)}, f32[160,128]{1,0:T(8,128)S(1)}, u32[]{:S(2)}, u32[]{:S(2)}) collective-permute-start(f32[160,128]{1,0:T(8,128)S(1)} %get-tuple-element.45), channel_id=1, source_target_pairs={{1,0},{2,1},{3,2},{4,3},{5,4},{6,5},{7,6},{0,7},{9,8},{10,9},{11,1... | collective-permute-start | bytes 245768 | tf_op jit(solution)/shard_map/ppermute | solution.py:537
  9.4 4.5 %collective-permute-start.5 = (f32[160,128]{1,0:T(8,128)S(1)}, f32[160,128]{1,0:T(8,128)S(1)}, u32[]{:S(2)}, u32[]{:S(2)}) collective-permute-start(f32[160,128]{1,0:T(8,128)S(1)} %get-tuple-element.46), channel_id=1, source_target_pairs={{7,0},{0,1},{1,2},{2,3},{3,4},{4,5},{5,6},{6,7},{15,8},{8,9},{9,10... | collective-permute-start | bytes 245768 | tf_op jit(solution)/shard_map/ppermute | solution.py:537
  14.1 6.0 %collective-permute-start.6 = (f32[256,128]{1,0:T(8,128)S(1)}, f32[256,128]{1,0:T(8,128)S(1)}, u32[]{:S(2)}, u32[]{:S(2)}) collective-permute-start(f32[256,128]{1,0:T(8,128)S(1)} %get-tuple-element.54), channel_id=1, source_target_pairs={{0,8},{16,24},{32,40},{48,56},{64,72},{80,88},{96,104},{112,120},{... | collective-permute-start | bytes 393224 | tf_op jit(solution)/shard_map/ppermute | solution.py:545
  16.3 4.4 %collective-permute-start.7 = (f32[256,128]{1,0:T(8,128)S(1)}, f32[256,128]{1,0:T(8,128)S(1)}, u32[]{:S(2)}, u32[]{:S(2)}) collective-permute-start(f32[256,128]{1,0:T(8,128)S(1)} %get-tuple-element.55), channel_id=1, source_target_pairs={{8,16},{24,32},{40,48},{56,64},{72,80},{88,96},{104,112},{120,128}... | collective-permute-start | bytes 393224 | tf_op jit(solution)/shard_map/ppermute | solution.py:545
  17.7 7.1 %collective-permute-start.2 = (f32[328,128]{1,0:T(8,128)S(1)}, f32[328,128]{1,0:T(8,128)S(1)}, u32[]{:S(2)}, u32[]{:S(2)}) collective-permute-start(f32[328,128]{1,0:T(8,128)S(1)} %get-tuple-element.43), channel_id=1, source_target_pairs={{1,0},{2,1},{3,2},{4,3},{5,4},{6,5},{7,6},{0,7},{9,8},{10,9},{11,1... | collective-permute-start | bytes 503816 | tf_op jit(solution)/shard_map/ppermute | solution.py:537
  17.8 7.0 %collective-permute-start.3 = (f32[328,128]{1,0:T(8,128)S(1)}, f32[328,128]{1,0:T(8,128)S(1)}, u32[]{:S(2)}, u32[]{:S(2)}) collective-permute-start(f32[328,128]{1,0:T(8,128)S(1)} %get-tuple-element.44), channel_id=1, source_target_pairs={{7,0},{0,1},{1,2},{2,3},{3,4},{4,5},{5,6},{6,7},{15,8},{8,9},{9,10... | collective-permute-start | bytes 503816 | tf_op jit(solution)/shard_map/ppermute | solution.py:537
  19.2 1.5 %copy-start.2 = (s32[1,4,128]{2,1,0:T(4,128)S(1)}, s32[1,4,128]{2,1,0:T(4,128)}, u32[]{:S(2)}) copy-start(s32[1,4,128]{2,1,0:T(4,128)} %seg.3) | copy-start | bytes 6148
  21.1 3.9 %collective-permute-start.8 = (f32[200,128]{1,0:T(8,128)S(1)}, f32[200,128]{1,0:T(8,128)S(1)}, u32[]{:S(2)}, u32[]{:S(2)}) collective-permute-start(f32[200,128]{1,0:T(8,128)S(1)} %get-tuple-element.56), channel_id=1, source_target_pairs={{1,0},{2,1},{3,2},{4,3},{5,4},{6,5},{7,6},{0,7},{9,8},{10,9},{11,1... | collective-permute-start | bytes 307208 | tf_op jit(solution)/shard_map/ppermute | solution.py:537
  21.9 5.7 %collective-permute-start.9 = (f32[200,128]{1,0:T(8,128)S(1)}, f32[200,128]{1,0:T(8,128)S(1)}, u32[]{:S(2)}, u32[]{:S(2)}) collective-permute-start(f32[200,128]{1,0:T(8,128)S(1)} %get-tuple-element.57), channel_id=1, source_target_pairs={{7,0},{0,1},{1,2},{2,3},{3,4},{4,5},{5,6},{6,7},{15,8},{8,9},{9,10... | collective-permute-start | bytes 307208 | tf_op jit(solution)/shard_map/ppermute | solution.py:537
  22.7 11.4 %collective-permute-start = (f32[664,128]{1,0:T(8,128)S(1)}, f32[664,128]{1,0:T(8,128)S(1)}, u32[]{:S(2)}, u32[]{:S(2)}) collective-permute-start(f32[664,128]{1,0:T(8,128)S(1)} %get-tuple-element.41), channel_id=1, source_target_pairs={{1,0},{2,1},{3,2},{4,3},{5,4},{6,5},{7,6},{0,7},{9,8},{10,9},{11,1... | collective-permute-start | bytes 1019912 | tf_op jit(solution)/shard_map/ppermute | solution.py:537
  24.8 9.3 %collective-permute-start.1 = (f32[664,128]{1,0:T(8,128)S(1)}, f32[664,128]{1,0:T(8,128)S(1)}, u32[]{:S(2)}, u32[]{:S(2)}) collective-permute-start(f32[664,128]{1,0:T(8,128)S(1)} %get-tuple-element.42), channel_id=1, source_target_pairs={{7,0},{0,1},{1,2},{2,3},{3,4},{4,5},{5,6},{6,7},{15,8},{8,9},{9,10... | collective-permute-start | bytes 1019912 | tf_op jit(solution)/shard_map/ppermute | solution.py:537
  28.1 8.0 %collective-permute-start.12 = (f32[400,128]{1,0:T(8,128)S(1)}, f32[400,128]{1,0:T(8,128)S(1)}, u32[]{:S(2)}, u32[]{:S(2)}) collective-permute-start(f32[400,128]{1,0:T(8,128)S(1)} %get-tuple-element.67), channel_id=1, source_target_pairs={{0,8},{16,24},{32,40},{48,56},{64,72},{80,88},{96,104},{112,120},{... | collective-permute-start | bytes 614408 | tf_op jit(solution)/shard_map/ppermute | solution.py:545
  34.1 5.2 %collective-permute-start.13 = (f32[400,128]{1,0:T(8,128)S(1)}, f32[400,128]{1,0:T(8,128)S(1)}, u32[]{:S(2)}, u32[]{:S(2)}) collective-permute-start(f32[400,128]{1,0:T(8,128)S(1)} %get-tuple-element.68), channel_id=1, source_target_pairs={{8,16},{24,32},{40,48},{56,64},{72,80},{88,96},{104,112},{120,128}... | collective-permute-start | bytes 614408 | tf_op jit(solution)/shard_map/ppermute | solution.py:545
  40.3 7.4 %collective-permute-start.14 = (f32[352,128]{1,0:T(8,128)S(1)}, f32[352,128]{1,0:T(8,128)S(1)}, u32[]{:S(2)}, u32[]{:S(2)}) collective-permute-start(f32[352,128]{1,0:T(8,128)S(1)} %get-tuple-element.70), channel_id=1, source_target_pairs={{0,8},{16,24},{32,40},{48,56},{64,72},{80,88},{96,104},{112,120},{... | collective-permute-start | bytes 540680 | tf_op jit(solution)/shard_map/ppermute | solution.py:545
  44.0 4.9 %collective-permute-start.15 = (f32[352,128]{1,0:T(8,128)S(1)}, f32[352,128]{1,0:T(8,128)S(1)}, u32[]{:S(2)}, u32[]{:S(2)}) collective-permute-start(f32[352,128]{1,0:T(8,128)S(1)} %get-tuple-element.71), channel_id=1, source_target_pairs={{8,16},{24,32},{40,48},{56,64},{72,80},{88,96},{104,112},{120,128}... | collective-permute-start | bytes 540680 | tf_op jit(solution)/shard_map/ppermute | solution.py:545
  44.1 10.7 %collective-permute-start.10 = (f32[1048,128]{1,0:T(8,128)S(1)}, f32[1048,128]{1,0:T(8,128)S(1)}, u32[]{:S(2)}, u32[]{:S(2)}) collective-permute-start(f32[1048,128]{1,0:T(8,128)S(1)} %get-tuple-element.63), channel_id=1, source_target_pairs={{0,8},{16,24},{32,40},{48,56},{64,72},{80,88},{96,104},{112,120},{... | collective-permute-start | bytes 1609736 | tf_op jit(solution)/shard_map/ppermute | solution.py:545
  45.8 9.2 %collective-permute-start.11 = (f32[1048,128]{1,0:T(8,128)S(1)}, f32[1048,128]{1,0:T(8,128)S(1)}, u32[]{:S(2)}, u32[]{:S(2)}) collective-permute-start(f32[1048,128]{1,0:T(8,128)S(1)} %get-tuple-element.64), channel_id=1, source_target_pairs={{8,16},{24,32},{40,48},{56,64},{72,80},{88,96},{104,112},{120,128}... | collective-permute-start | bytes 1609736 | tf_op jit(solution)/shard_map/ppermute | solution.py:545
  51.3 4.7 %collective-permute-start.16 = (f32[544,128]{1,0:T(8,128)S(1)}, f32[544,128]{1,0:T(8,128)S(1)}, u32[]{:S(2)}, u32[]{:S(2)}) collective-permute-start(f32[544,128]{1,0:T(8,128)S(1)} %get-tuple-element.73), channel_id=1, source_target_pairs={{0,8},{16,24},{32,40},{48,56},{64,72},{80,88},{96,104},{112,120},{... | collective-permute-start | bytes 835592 | tf_op jit(solution)/shard_map/ppermute | solution.py:545
  54.8 6.3 %collective-permute-start.17 = (f32[544,128]{1,0:T(8,128)S(1)}, f32[544,128]{1,0:T(8,128)S(1)}, u32[]{:S(2)}, u32[]{:S(2)}) collective-permute-start(f32[544,128]{1,0:T(8,128)S(1)} %get-tuple-element.74), channel_id=1, source_target_pairs={{8,16},{24,32},{40,48},{56,64},{72,80},{88,96},{104,112},{120,128}... | collective-permute-start | bytes 835592 | tf_op jit(solution)/shard_map/ppermute | solution.py:545
